TPU v7x, 256 devices: a whole 4x4x8 slice. The times are simulated.
256 devices in a mesh: ctx: 8 (over z), ch: 32 (over x, y, core).
Axes of the slice: x: 4, y: 4, z: 8, core: 2. Of those that a mesh axis runs over, the one named last changes fastest.
Arguments:
- u_rows: bfloat16 [16384, 8192], P(('ctx', 'ch')), may hold values from -6 to 6
- gain: float32 [8192], replicated, may hold values from 0.1 to 1.9
- skip: float32 [8192], P('ch'), may hold values from -4 to 4
- residues: float32 [8192, 16], P('ch'), may hold values from -1.5 to 1.5
- rates: float32 [8192, 16], P('ch'), may hold values from 1.8310547e-05 to 0.04
- grad_out: bfloat16 [16384, 8192], P('ctx', 'ch'), may hold values from -6 to 6
- doc_lengths: int32 [4], replicated, may hold values from 1 to 8192, 16384 in all
- doc_streams: int32 [4], replicated, may hold values from 0 to 1
Outputs:
- input_grad: bfloat16 [16384, 8192], P(('ctx', 'ch'))
- residue_grad: float32 [2, 8192, 16], P(None, 'ch')
Inputs may be any that keep to these rules, and one draw needn't show every extreme that they name: `doc_lengths`: the lengths sum to 16384 and the largest is exactly 8192.
All inputs are finite; a program needn't handle non-finite values.
Results may differ from a plain program's by a relative error of at most 0.015.
Values may be sent and summed in bfloat16 or wider, within the bound.
No kernel may reach another device: no remote copies, remote signals or barrier semaphores. Data moves between devices by JAX's collectives and lax.ppermute only.
A program may use at most 64 MiB of HBM per device.

v0:
```python
import math

import jax
import jax.numpy as jnp
from jax import lax
from jax.sharding import PartitionSpec as P

highest = lax.Precision.HIGHEST


def prefix(value, axis, combine, identity):
    count, here = (lax.axis_size(axis), lax.axis_index(axis))
    everything = jax.tree.map(
        lambda part, kind: lax.all_gather(part.astype(kind), axis),
        value,
        (jnp.bfloat16, jnp.bfloat16),
    )
    start = jax.tree.map(
        lambda part, zero: jnp.broadcast_to(jnp.asarray(zero, part.dtype), part.shape),
        value,
        identity,
    )

    def step(k, before):
        reached = k < here
        new = combine(
            before, jax.tree.map(lambda part, own: part[k].astype(own.dtype), everything, value)
        )
        return jax.tree.map(lambda a, b: jnp.where(reached, a, b), new, before)

    return lax.fori_loop(0, count, step, start)


def prefix_2(value, axis, combine, identity):
    count, here = (lax.axis_size(axis), lax.axis_index(axis))
    everything = jax.tree.map(lambda part: lax.all_gather(part, axis), value)
    start = jax.tree.map(
        lambda part, zero: jnp.broadcast_to(jnp.asarray(zero, part.dtype), part.shape),
        value,
        identity,
    )

    def step(k, before):
        at = count - 1 - k
        reached = at > here
        new = combine(before, jax.tree.map(lambda part: part[at], everything))
        return jax.tree.map(lambda a, b: jnp.where(reached, a, b), new, before)

    return lax.fori_loop(0, count, step, start)


def token_tables(doc_lengths, doc_streams, positions):
    starts = jnp.cumsum(doc_lengths) - doc_lengths
    start_flag = jnp.any(positions[:, None] == starts[None, :], axis=1).astype(jnp.float32)
    document = jnp.sum((positions[:, None] >= starts[None, :]).astype(jnp.int32), axis=1) - 1
    doc_total = doc_lengths.shape[0]
    member = (document[:, None] == jnp.arange(doc_total, dtype=jnp.int32)[None, :]).astype(
        jnp.int32
    )
    stream = jnp.sum(member * doc_streams[None, :], axis=1)
    onehot = (stream[:, None] == jnp.arange(2, dtype=jnp.int32)[None, :]).astype(jnp.float32)
    return (start_flag, onehot)


def chain_combine(earlier, later):
    return (earlier[0] * later[0], later[0] * earlier[1] + later[1])


def conv_backward(x_cols, grad_out, skip, residues, rates, doc_lengths, doc_streams):
    rows, chans = x_cols.shape
    modes = rates.shape[1]
    decay = jnp.exp(-rates)
    mode_scale = jnp.sqrt(1.0 - decay * decay)
    mode_weight = residues * mode_scale
    positions = lax.axis_index("ctx") * rows + jnp.arange(rows, dtype=jnp.int32)
    start_flag, onehot = token_tables(doc_lengths, doc_streams, positions)
    block = min(128, rows)
    blocks = rows // block
    offsets = jnp.arange(block, dtype=jnp.float32)
    powers = jnp.exp(-rates[None] * offsets[:, None, None])
    reversed_powers = powers[::-1]
    x_blocks = x_cols.reshape(blocks, block, chans)
    dy_blocks = grad_out.reshape(blocks, block, chans)
    start_blocks = start_flag.reshape(blocks, block)
    pick_blocks = onehot.reshape(blocks, block, 2)
    later = lax.broadcasted_iota(jnp.int32, (block, block), 0) >= lax.broadcasted_iota(
        jnp.int32, (block, block), 1
    )

    def masks(start_block):
        count_in = jnp.cumsum(start_block)
        same = later & (count_in[:, None] == count_in[None, :])
        return (jnp.where(same, 1.0, 0.0).astype(jnp.float32), count_in)

    def forward(carry, operands):
        state, multiplier, local_sum, carry_sum = carry
        x_block, dy_block, start_block, pick = operands
        forward_mask, count_in = masks(start_block)
        head = jnp.where(count_in == 0.0, 1.0, 0.0)
        ratio = (x_block.astype(jnp.float32)[:, :, None] / powers).reshape(block, chans * modes)
        inner = jnp.dot(forward_mask, ratio, precision=highest).reshape(block, chans, modes)
        lead = decay[None] * powers * head[:, None, None]
        states = powers * inner + lead * state[None]
        reach = lead * multiplier[None]
        dy_float = dy_block.astype(jnp.float32)[:, :, None]
        local_sum = local_sum + jnp.dot(
            pick.T, (dy_float * states).reshape(block, chans * modes), precision=highest
        ).reshape(2, chans, modes)
        carry_sum = carry_sum + jnp.dot(
            pick.T, (dy_float * reach).reshape(block, chans * modes), precision=highest
        ).reshape(2, chans, modes)
        return ((states[-1], reach[-1], local_sum, carry_sum), None)

    zero_state = jnp.zeros((chans, modes), jnp.float32)
    zero_sum = jnp.zeros((2, chans, modes), jnp.float32)
    start_carry = (zero_state, jnp.ones((chans, modes), jnp.float32), zero_sum, zero_sum)
    (end_state, through, local_sum, carry_sum), _ = lax.scan(
        forward, start_carry, (x_blocks, dy_blocks, start_blocks, pick_blocks)
    )

    def backward(carry, operands):
        dy_block, start_block = operands
        forward_mask, count_in = masks(start_block)
        tail = jnp.where(count_in == count_in[-1], 1.0, 0.0)
        weighted = (dy_block.astype(jnp.float32)[:, :, None] * powers).reshape(block, chans * modes)
        inner = jnp.dot(forward_mask.T, weighted, precision=highest).reshape(block, chans, modes)
        states = inner / powers + reversed_powers * tail[:, None, None] * carry[None]
        outgoing = decay * (1.0 - start_block[0]) * states[0]
        return (outgoing, jnp.sum(mode_weight[None] * states, axis=2))

    leaving, conv_blocks = lax.scan(backward, zero_state, (dy_blocks, start_blocks), reverse=True)
    identity_pair = (jnp.ones_like(through), zero_state)
    entering = prefix((through, end_state), "ctx", chain_combine, identity_pair)[1]
    arriving = prefix_2((through, leaving), "ctx", chain_combine, identity_pair)[1]
    window = rows * lax.axis_size("ctx")
    residue_part = (local_sum + carry_sum * entering[None]) * mode_scale[None] / math.sqrt(window)
    residue_grad = lax.psum(residue_part.astype(jnp.bfloat16), "ctx").astype(jnp.float32)
    total_count = jnp.cumsum(start_flag)
    tail_all = jnp.where(total_count == total_count[-1], 1.0, 0.0).reshape(blocks, block)
    source = mode_weight * arriving

    def correct(operands):
        index, conv_block, tail_block = operands
        distance = ((blocks - 1 - index) * block).astype(jnp.float32)
        factor = source * jnp.exp(-rates * distance)
        return conv_block + jnp.sum(reversed_powers * factor[None], axis=2) * tail_block[:, None]

    conv_grad = lax.map(
        correct, (jnp.arange(blocks, dtype=jnp.int32), conv_blocks, tail_all)
    ).reshape(rows, chans)
    normed_grad = (skip[None, :] * grad_out.astype(jnp.float32) + conv_grad).astype(jnp.bfloat16)
    return (normed_grad, residue_grad)


def local(u_rows, gain, skip, residues, rates, grad_out, doc_lengths, doc_streams):
    width = gain.shape[0]
    u_cols = lax.all_to_all(u_rows, "ch", split_axis=1, concat_axis=0, tiled=True)
    col_float = u_cols.astype(jnp.float32)
    group_width = u_cols.shape[1]
    gain_cols = lax.dynamic_slice_in_dim(gain, lax.axis_index("ch") * group_width, group_width)
    square_total = lax.psum(jnp.sum(col_float * col_float, axis=1), "ch")
    inv_cols = lax.rsqrt(square_total / width + 1e-05)
    normal_cols = col_float * inv_cols[:, None]
    x_cols = (normal_cols * gain_cols[None, :]).astype(jnp.bfloat16)
    normed_grad, residue_grad = conv_backward(
        x_cols, grad_out, skip, residues, rates, doc_lengths, doc_streams
    )
    scaled = gain_cols[None, :] * normed_grad.astype(jnp.float32)
    project = lax.psum(jnp.sum(normal_cols * scaled, axis=1), "ch") / width
    grad_cols = (inv_cols[:, None] * (scaled - normal_cols * project[:, None])).astype(jnp.bfloat16)
    input_grad = lax.all_to_all(grad_cols, "ch", split_axis=0, concat_axis=1, tiled=True)
    return (input_grad, residue_grad)


def solution(mesh):
    return jax.shard_map(
        local,
        mesh=mesh,
        in_specs=(
            P(("ctx", "ch"), None),
            P(),
            P("ch"),
            P("ch", None),
            P("ch", None),
            P("ctx", "ch"),
            P(),
            P(),
        ),
        out_specs=(P(("ctx", "ch"), None), P(None, "ch", None)),
        check_vma=False,
    )
```

profile of v0, /device:TPU:1, one launch (start us, length us, event | category | flops | bytes accessed | tf_op | source)
XLA Modules:
  0.0 852.5 jit_solution(12601578811131579376)
XLA Ops:
  3.0 8.6 %all-to-all-start = ((bf16[64,32,256]{2,0,1:T(8,128)(2,1)}), bf16[64,32,256]{2,0,1:T(8,128)(2,1)S(1)}, u32[]{:S(2)}, u32[]{:S(2)}) async-start(bf16[64,32,256]{2,0,1:T(8,128)(2,1)} %bitcast.155), calls=%async_computation | async-start | bytes 2097152 | tf_op jit(solution)/shard_map/all_to_all | solution.py:157
  16.7 13.6 %rev.3 = f32[128,256,16]{1,0,2:T(8,128)S(1)} reverse(f32[128,256,16]{1,0,2:T(8,128)} %multiply_exponential_fusion.2), dimensions={0} | reverse | bytes 4194304 | tf_op jit(solution)/shard_map/rev | solution.py:81
  31.9 129.5 %while.78 = (s32[]{:T(128)}, f32[256,16]{0,1:T(8,128)S(1)}, f32[16,128,256]{2,1,0:T(8,128)}, f32[16,128]{1,0:T(8,128)}, f32[256,16]{0,1:T(8,128)S(1)}, /*index=5...) while((s32[]{:T(128)}, f32[256,16]{0,1:T(8,128)S(1)}, ...), condition=%wide.region_7.8_spmd.clone, body=%wide.region_4.0_spmd.clone.sunk | while | flops 810119296 | bytes 5086431 | solution.py:131
  35.7 3.5 multiply_reduce_fusion.7
  43.8 3.5 multiply_reduce_fusion.7
  51.9 3.5 multiply_reduce_fusion.7
  60.0 3.5 multiply_reduce_fusion.7
  68.1 3.5 multiply_reduce_fusion.7
  76.2 3.5 multiply_reduce_fusion.7
  84.3 3.5 multiply_reduce_fusion.7
  92.3 3.5 multiply_reduce_fusion.7
  100.4 3.5 multiply_reduce_fusion.7
  108.5 3.5 multiply_reduce_fusion.7
  116.6 3.5 multiply_reduce_fusion.7
  124.7 3.5 multiply_reduce_fusion.7
  132.8 3.5 multiply_reduce_fusion.7
  140.9 3.5 multiply_reduce_fusion.7
  149.0 3.5 multiply_reduce_fusion.7
  157.1 3.5 multiply_reduce_fusion.7
  161.5 2.6 copy.152
  165.4 22.0 %all-gather.1 = f32[2048,16]{0,1:T(8,128)S(1)} all-gather(f32[256,16]{0,1:T(8,128)S(1)} %get-tuple-element.588), channel_id=3, replica_groups=mesh['ctx'=8,'ch'=32] {'ctx'}, dimensions={0}, use_global_device_ids=true | all-gather | bytes 147456 | tf_op jit(solution)/shard_map/all_gather | solution.py:36
  191.5 69.8 %psum.21 = f32[2048]{0:T(1024)S(1)} all-reduce(f32[2048]{0:T(1024)S(1)} %reduce_sum.70), channel_id=1, replica_groups=mesh['ctx'=8,'ch'=32] {'ch'}, use_global_device_ids=true, to_apply=%region_1.0 | all-reduce | flops 2048 | bytes 16384 | tf_op jit(solution)/shard_map/psum | solution.py:161
  263.1 332.1 %while.81 = (s32[]{:T(128)}, f32[256,16]{0,1:T(8,128)}, f32[256,16]{0,1:T(8,128)S(1)}, f32[2,256,16]{1,0,2:T(2,128)}, f32[2,256,16]{1,0,2:T(2,128)}, /*index=5*/...) while((s32[]{:T(128)}, f32[256,16]{0,1:T(8,128)}, ...), condition=%wide.wide.region_14.15_spmd.clone, body=%wide.wide.region_12.14_spmd.clone.sunk | while | flops 838520960 | bytes 34260636 | solution.py:117
  274.6 3.6 multiply_add_fusion.3
  280.2 2.8 fusion.112
  295.3 3.6 multiply_add_fusion.3
  301.0 2.9 fusion.112
  316.1 3.6 multiply_add_fusion.3
  321.7 2.9 fusion.112
  336.8 3.6 multiply_add_fusion.3
  342.5 2.9 fusion.112
  357.6 3.6 multiply_add_fusion.3
  363.3 2.9 fusion.112
  378.4 3.6 multiply_add_fusion.3
  384.0 2.8 fusion.112
  399.1 3.6 multiply_add_fusion.3
  404.7 2.9 fusion.112
  419.9 3.6 multiply_add_fusion.3
  425.5 2.9 fusion.112
  440.6 3.6 multiply_add_fusion.3
  446.2 2.9 fusion.112
  461.3 3.6 multiply_add_fusion.3
  467.0 2.9 fusion.112
  482.1 3.6 multiply_add_fusion.3
  487.7 2.9 fusion.112
  502.9 3.6 multiply_add_fusion.3
  508.5 2.9 fusion.112
  523.7 3.6 multiply_add_fusion.3
  529.3 2.9 fusion.112
  544.4 3.6 multiply_add_fusion.3
  550.1 2.9 fusion.112
  565.2 3.6 multiply_add_fusion.3
  570.9 2.9 fusion.112
  586.0 3.6 multiply_add_fusion.3
  591.7 2.9 fusion.112
  595.2 18.7 %all-gather = f32[2048,16]{0,1:T(8,128)S(1)} all-gather(f32[256,16]{0,1:T(8,128)S(1)} %get-tuple-element.587), channel_id=2, replica_groups=mesh['ctx'=8,'ch'=32] {'ctx'}, dimensions={0}, use_global_device_ids=true | all-gather | bytes 147456 | tf_op jit(solution)/shard_map/all_gather | solution.py:36
  614.6 18.2 %all-gather.2 = bf16[2048,16]{0,1:T(8,128)(2,1)S(1)} all-gather(bf16[256,16]{0,1:T(8,128)(2,1)S(1)} %convert_element_type.143), channel_id=4, replica_groups=mesh['ctx'=8,'ch'=32] {'ctx'}, dimensions={0}, use_global_device_ids=true | all-gather | bytes 73728 | tf_op jit(solution)/shard_map/all_gather | solution.py:14
  632.8 18.4 %all-gather.3 = bf16[2048,16]{0,1:T(8,128)(2,1)S(1)} all-gather(bf16[256,16]{0,1:T(8,128)(2,1)S(1)} %convert_element_type.144), channel_id=5, replica_groups=mesh['ctx'=8,'ch'=32] {'ctx'}, dimensions={0}, use_global_device_ids=true | all-gather | bytes 73728 | tf_op jit(solution)/shard_map/all_gather | solution.py:14
  651.2 17.5 %while.79 = (s32[]{:T(128)}, f32[256,16]{0,1:T(8,128)}, s32[]{:T(128)}, f32[8,256,16]{1,0,2:T(8,128)S(1)}, f32[8,256,16]{1,0,2:T(8,128)}, /*index=5*/s32[]{:T(128)}, s32[]{:T(128)}, s32[]{:T(128)}, s32[]{:T(128)}) while((s32[]{:T(128)}, f32[256,16]{0,1:T(8,128)}, s32[]{:T(128)}, f32[8,256,16]{1,0,2:T(8,128)S(1)}, ...), condition=%wide.region_16.17_spmd.clone, body=%wide.region_15.16_spmd.clone.sunk | while | flops 16392 | bytes 131243 | solution.py:49
  671.0 65.5 %while.77 = (s32[]{:T(128)}, f32[16,128,256]{2,1,0:T(8,128)}, f32[16,128,256]{2,1,0:T(8,128)}, s32[16]{0:T(128)S(1)}, f32[1,256,16]{1,2,0:T(8,128)S(1)}, /*index...) while((s32[]{:T(128)}, f32[16,128,256]{2,1,0:T(8,128)}, ...), condition=%wide.region_19.20_spmd, body=%wide.region_17.19_spmd.sunk | while | flops 1089541 | bytes 2688685 | solution.py:148
  736.5 2.8 multiply_reduce_fusion.2
  739.2 82.0 %psum.22 = f32[2048]{0:T(1024)S(1)} all-reduce(f32[2048]{0:T(1024)S(1)} %get-tuple-element.965), channel_id=1, replica_groups=mesh['ctx'=8,'ch'=32] {'ch'}, use_global_device_ids=true, to_apply=%region_21.22 | all-reduce | flops 2048 | bytes 16384 | tf_op jit(solution)/shard_map/psum | solution.py:169
  822.8 4.3 all-to-all-start.1
  827.5 23.4 %psum.23 = bf16[2,256,16]{1,2,0:T(8,128)(2,1)S(1)} all-reduce(bf16[2,256,16]{1,2,0:T(8,128)(2,1)S(1)} %fusion.71), channel_id=1, replica_groups=mesh['ctx'=8,'ch'=32] {'ctx'}, use_global_device_ids=true, to_apply=%region_24.25 | all-reduce | flops 8192 | bytes 32768 | tf_op jit(solution)/shard_map/psum | solution.py:137
  (1242 shorter events, 390.4 us)
Async XLA Ops:
  0.6 11.0 %copy-start.31 = (s32[4]{0:T(128)S(1)}, s32[4]{0:T(128)}, u32[]{:S(2)}) copy-start(s32[4]{0:T(128)} %param.24) | copy-start | bytes 52
  0.6 13.1 %copy-start.25 = (f32[256,16]{0,1:T(8,128)S(1)}, f32[256,16]{0,1:T(8,128)}, u32[]{:S(2)}) copy-start(f32[256,16]{0,1:T(8,128)} %param.22) | copy-start | bytes 49156
  0.7 13.1 %copy-start.26 = (f32[256,16]{0,1:T(8,128)S(1)}, f32[256,16]{0,1:T(8,128)}, u32[]{:S(2)}) copy-start(f32[256,16]{0,1:T(8,128)} %param.21) | copy-start | bytes 49156
  3.0 188.0 %all-to-all-start = ((bf16[64,32,256]{2,0,1:T(8,128)(2,1)}), bf16[64,32,256]{2,0,1:T(8,128)(2,1)S(1)}, u32[]{:S(2)}, u32[]{:S(2)}) async-start(bf16[64,32,256]{2,0,1:T(8,128)(2,1)} %bitcast.155), calls=%async_computation | async-start | bytes 2097152 | tf_op jit(solution)/shard_map/all_to_all | solution.py:157
  161.5 27.5 %copy-start.30 = (s32[4]{0:T(128)S(1)}, s32[4]{0:T(128)}, u32[]{:S(2)}) copy-start(s32[4]{0:T(128)} %param.25) | copy-start | bytes 52
  188.9 73.2 %copy-start.23 = (f32[256]{0:T(256)}, f32[256]{0:T(256)S(1)}, u32[]{:S(2)}) copy-start(f32[256]{0:T(256)S(1)} %dynamic_slice.90) | copy-start | bytes 3076
  263.1 6.1 copy-start.1
  278.3 5.4 copy-start.2
  278.3 5.4 copy-start.4
  283.7 6.1 copy-start.1
  299.0 5.5 copy-start.2
  299.0 5.5 copy-start.4
  304.5 6.1 copy-start.1
  319.7 5.5 copy-start.2
  319.8 5.5 copy-start.4
  325.2 6.1 copy-start.1
  340.5 5.5 copy-start.2
  340.5 5.5 copy-start.4
  346.0 6.1 copy-start.1
  361.3 5.5 copy-start.2
  361.3 5.5 copy-start.4
  366.8 6.1 copy-start.1
  382.0 5.4 copy-start.2
  382.0 5.4 copy-start.4
  387.5 6.1 copy-start.1
  402.7 5.6 copy-start.2
  402.7 5.5 copy-start.4
  408.3 6.1 copy-start.1
  423.5 5.5 copy-start.2
  423.5 5.5 copy-start.4
  429.0 6.1 copy-start.1
  444.2 5.5 copy-start.2
  444.2 5.5 copy-start.4
  449.8 6.1 copy-start.1
  465.0 5.5 copy-start.2
  465.0 5.5 copy-start.4
  470.5 6.1 copy-start.1
  485.7 5.5 copy-start.2
  485.7 5.5 copy-start.4
  491.3 6.1 copy-start.1
  506.5 5.6 copy-start.2
  506.5 5.6 copy-start.4
  512.1 6.1 copy-start.1
  527.3 5.5 copy-start.2
  527.3 5.5 copy-start.4
  532.9 6.1 copy-start.1
  548.1 5.5 copy-start.2
  548.1 5.5 copy-start.4
  553.6 6.1 copy-start.1
  568.9 5.6 copy-start.2
  568.9 5.6 copy-start.4
  574.5 6.1 copy-start.1
  589.7 5.5 copy-start.2
  589.7 5.5 copy-start.4
  595.2 75.7 %copy-start = (f32[128,256,16]{1,2,0:T(8,128)S(1)}, f32[128,256,16]{1,2,0:T(8,128)}, u32[]{:S(2)}) copy-start(f32[128,256,16]{1,2,0:T(8,128)} %copy.152) | copy-start | bytes 6291460
  595.2 75.7 %copy-start.15 = (f32[1,256,16]{1,2,0:T(8,128)S(1)}, f32[1,256,16]{1,2,0:T(8,128)}, u32[]{:S(2)}) copy-start(f32[1,256,16]{1,2,0:T(8,128)} %get-tuple-element.1417) | copy-start | bytes 49156
  670.9 65.5 %copy-start.17 = (f32[2048]{0:T(1024)S(1)}, f32[2048]{0:T(1024)}, u32[]{:S(2)}) copy-start(f32[2048]{0:T(1024)} %get-tuple-element.983) | copy-start | bytes 24580
  670.9 65.5 %copy-start.24 = (f32[256]{0:T(256)S(1)}, f32[256]{0:T(256)}, u32[]{:S(2)}) copy-start(f32[256]{0:T(256)} %copy-done.23) | copy-start | bytes 3076
  671.0 65.5 %copy-start.29 = (f32[256]{0:T(256)S(1)}, f32[256]{0:T(256)}, u32[]{:S(2)}) copy-start(f32[256]{0:T(256)} %param.20) | copy-start | bytes 3076
  821.3 5.8 copy-start.16
  821.3 6.2 copy-start.11
  821.3 6.2 copy-start.14
  821.3 6.2 copy-start.18
  822.8 28.7 %all-to-all-start.1 = ((bf16[32,64,256]{2,1,0:T(8,128)(2,1)}), bf16[32,64,256]{2,1,0:T(8,128)(2,1)S(1)}, u32[]{:S(2)}, u32[]{:S(2)}) async-start(bf16[32,64,256]{2,1,0:T(8,128)(2,1)} %bitcast.18), calls=%async_computation.1 | async-start | bytes 2097152 | tf_op jit(solution)/shard_map/all_to_all | solution.py:171
  (225 other events, 627.1 us)
where the time goes:
time: 869 us; the launch traced here: 853 us
  blocking collectives  252 us (29%)
  other arithmetic  195 us (22%)
  matrix products  191 us (22%)
  local copies, waits for them, and re-layouts  183 us (21%)
  loops' own time  17 us (2%)
  starting transfers between devices  12.9 us (1%)
    psum x1, blocking collectives, local(): project = lax.psum(jnp.sum(normal_cols * scaled, axis=1), 'ch') / width  82 us
    psum x1, blocking collectives, local(): square_total = lax.psum(jnp.sum(col_float * col_float, axis=1), 'ch')  69.8 us
    dot_general x16, matrix products, forward(): jnp.dot(forward_mask, ratio, precision=highest).reshape(block, chans, modes)  57.6 us
    dot_general x16, matrix products, backward(): jnp.dot(forward_mask.T, weighted, precision=highest)  56.6 us
    dot_general x16, matrix products, forward(): jnp.dot(pick.T, (dy_float * reach).reshape(block, chans * modes), precisi...  46.1 us
    all_gather x2, blocking collectives, prefix_2(): everything = jax.tree.map(lambda part: lax.all_gather(part, axis), value)  40.7 us
    mul x16, other arithmetic, forward(): dy_float * reach  39.5 us
    mul x16, other arithmetic, forward(): lead = decay[None] * powers * head[:, None, None]  38.8 us
  transfers between devices with their start and end apart: 2, of which 0 were waited for; matrix products, arithmetic and copies ran while one was open for 18% of the time, Pallas kernels for 0%

commit v1 on v0

v1 whole, which is shorter than its diff:
```python
import math

import jax
import jax.numpy as jnp
from jax import lax
from jax.experimental import pallas as pl
from jax.experimental.pallas import tpu as pltpu
from jax.sharding import PartitionSpec as P

F32 = jnp.float32
BF16 = jnp.bfloat16
SEGS = 8
LANES = 128
UNROLL = 8
ROW_BLOCK = 16


def params(limit=32 * 1024 * 1024):
    return pltpu.CompilerParams(vmem_limit_bytes=limit)


def vmem():
    return pl.BlockSpec(memory_space=pltpu.VMEM)


def smem():
    return pl.BlockSpec(memory_space=pltpu.SMEM)


def cost(flops, size):
    return pl.CostEstimate(flops=flops, bytes_accessed=size, transcendentals=0)


def inverse_rms(u_ref, eps=1e-05):
    rows, width = u_ref.shape
    total = jnp.zeros((rows, LANES), F32)
    for c in range(width // LANES):
        part = u_ref[:, c * LANES : (c + 1) * LANES].astype(F32)
        total = total + part * part
    return lax.rsqrt(jnp.sum(total, axis=1, keepdims=True) / width + eps)


def norm_kernel(u_ref, gain_ref, out_ref):
    groups, _, chans = out_ref.shape
    inv = inverse_rms(u_ref)
    for c in range(groups):
        cols = slice(c * chans, (c + 1) * chans)
        normal = u_ref[:, cols].astype(F32) * inv
        out_ref[c] = (normal * gain_ref[:, cols]).astype(BF16)


def norm_rows(u_rows, gain, groups):
    rows, width = u_rows.shape
    chans = width // groups
    return pl.pallas_call(
        norm_kernel,
        grid=(rows // ROW_BLOCK,),
        in_specs=[
            pl.BlockSpec((ROW_BLOCK, width), lambda i: (i, 0)),
            pl.BlockSpec((1, width), lambda i: (0, 0)),
        ],
        out_specs=pl.BlockSpec((groups, ROW_BLOCK, chans), lambda i: (0, i, 0)),
        out_shape=jax.ShapeDtypeStruct((groups, rows, chans), BF16),
        compiler_params=params(),
        cost_estimate=cost(8 * rows * width, 4 * rows * width),
        name="norm_rows",
    )(u_rows, gain)


def final_kernel(u_ref, gain_ref, grad_ref, out_ref):
    groups, rows, chans = grad_ref.shape
    width = groups * chans
    inv = inverse_rms(u_ref)
    total = jnp.zeros((rows, chans), F32)
    for c in range(groups):
        cols = slice(c * chans, (c + 1) * chans)
        normal = u_ref[:, cols].astype(F32) * inv
        total = total + normal * (gain_ref[:, cols] * grad_ref[c].astype(F32))
    project = jnp.sum(total, axis=1, keepdims=True) / width
    for c in range(groups):
        cols = slice(c * chans, (c + 1) * chans)
        normal = u_ref[:, cols].astype(F32) * inv
        scaled = gain_ref[:, cols] * grad_ref[c].astype(F32)
        out_ref[:, cols] = (inv * (scaled - normal * project)).astype(BF16)


def final_rows(u_rows, gain, grad_rows):
    rows, width = u_rows.shape
    groups, _, chans = grad_rows.shape
    return pl.pallas_call(
        final_kernel,
        grid=(rows // ROW_BLOCK,),
        in_specs=[
            pl.BlockSpec((ROW_BLOCK, width), lambda i: (i, 0)),
            pl.BlockSpec((1, width), lambda i: (0, 0)),
            pl.BlockSpec((groups, ROW_BLOCK, chans), lambda i: (0, i, 0)),
        ],
        out_specs=pl.BlockSpec((ROW_BLOCK, width), lambda i: (i, 0)),
        out_shape=jax.ShapeDtypeStruct((rows, width), BF16),
        compiler_params=params(),
        cost_estimate=cost(16 * rows * width, 6 * rows * width),
        name="final_rows",
    )(u_rows, gain, grad_rows)


def doc_starts(lens_ref):
    starts, at = [], jnp.int32(0)
    for k in range(lens_ref.shape[0] - 1):
        at = at + lens_ref[k]
        starts.append(at)
    return starts


def sort_down(codes):
    codes = list(codes)
    for end in range(len(codes) - 1, 0, -1):
        for k in range(end):
            high = jnp.maximum(codes[k], codes[k + 1])
            low = jnp.minimum(codes[k], codes[k + 1])
            codes[k], codes[k + 1] = high, low
    return codes


def cut_codes(starts, streams, base, seg_len):
    codes = []
    for start, stream in zip(starts, streams):
        place = start - base
        inside = (place >= 0) & (place < SEGS * seg_len)
        code = (place % seg_len) * 16 + place // seg_len
        codes.append(jnp.where(inside, code, 15) * 2 + stream)
    return sort_down(codes)


def any_start(starts, first, count):
    found = jnp.bool_(False)
    for start in starts:
        found = found | ((start >= first) & (start < first + count))
    return found


def time_loop(cuts_ref, seg_len, step, cut, carry):
    def piece(p, state):
        top, inner = state
        code = cuts_ref[p]
        low = code // 32
        count = top - low
        full = count // UNROLL

        def many(k, value):
            first = top - (k + 1) * UNROLL
            for j in range(UNROLL - 1, -1, -1):
                value = step(first + j, value)
            return value

        def one(k, value):
            return step(top - full * UNROLL - 1 - k, value)

        inner = lax.fori_loop(0, full, many, inner)
        inner = lax.fori_loop(0, count - full * UNROLL, one, inner)
        inner = cut((code // 2) % 16, code % 2, inner)
        return (low, inner)

    return lax.fori_loop(0, cuts_ref.shape[0], piece, (jnp.int32(seg_len), carry))[1]


def widen(source_ref, target_ref, chunk=64):
    def body(k, _):
        rows = pl.ds(k * chunk, chunk)
        for h in range(target_ref.shape[0]):
            target_ref[h, rows, :] = source_ref[rows, h * LANES : (h + 1) * LANES].astype(F32)
        return 0

    lax.fori_loop(0, source_ref.shape[0] // chunk, body, 0)


def spread(ref, r, cols):
    return jnp.broadcast_to(ref[r : r + 1, cols], (SEGS, LANES))


def segment(ref, s, modes):
    rows = slice(s * modes, (s + 1) * modes)
    return jnp.concatenate([ref[h, rows, :] for h in range(ref.shape[0])], axis=1)


def put_segment(ref, s, modes, value):
    for h in range(ref.shape[0]):
        ref[h, s * modes : (s + 1) * modes, :] = value[:, h * LANES : (h + 1) * LANES]


def store_cuts(cuts_ref, codes):
    for k, code in enumerate(codes):
        cuts_ref[k] = code
    cuts_ref[len(codes)] = jnp.int32(30)


def leave_kernel(lens_ref, rates_ref, grad_ref, seg_ref, dev_ref, wide_ref, decay_ref, cuts_ref):
    tokens, chans = grad_ref.shape
    modes = rates_ref.shape[0]
    seg_len = tokens // SEGS
    base = lax.axis_index("ctx") * tokens
    starts = doc_starts(lens_ref)
    store_cuts(cuts_ref, cut_codes(starts, [0] * len(starts), base, seg_len))
    decay_ref[...] = jnp.exp(-rates_ref[...])
    widen(grad_ref, wide_ref)
    row = lax.broadcasted_iota(jnp.int32, (SEGS, LANES), 0)
    for h in range(chans // LANES):
        cols = slice(h * LANES, (h + 1) * LANES)
        decay = [spread(decay_ref, r, cols) for r in range(modes)]

        def step(i, state):
            grad = wide_ref[h, pl.ds(i, SEGS, stride=seg_len), :]
            return tuple(grad + decay[r] * state[r] for r in range(modes))

        def cut(segment, stream, state):
            hold = row != segment
            return tuple(jnp.where(hold, part, 0.0) for part in state)

        zero = jnp.zeros((SEGS, LANES), F32)
        state = time_loop(cuts_ref, seg_len, step, cut, (zero,) * modes)
        for r in range(modes):
            seg_ref[h, pl.ds(r, SEGS, stride=modes), :] = decay[r] * state[r]
    through = jnp.exp(-rates_ref[...] * float(seg_len))
    leaving = segment(seg_ref, SEGS - 1, modes)
    for s in range(SEGS - 2, -1, -1):
        kept = jnp.where(any_start(starts, base + s * seg_len, seg_len), 0.0, 1.0)
        leaving = segment(seg_ref, s, modes) + (through * kept) * leaving
    for k in range(dev_ref.shape[0]):
        dev_ref[k] = leaving


def leave(doc_lengths, rates, grad_out, copies):
    modes, chans = rates.shape
    tokens = grad_out.shape[0]
    return pl.pallas_call(
        leave_kernel,
        in_specs=[smem(), vmem(), vmem()],
        out_specs=[vmem(), vmem()],
        out_shape=[
            jax.ShapeDtypeStruct((chans // LANES, SEGS * modes, LANES), F32),
            jax.ShapeDtypeStruct((copies, modes, chans), F32),
        ],
        scratch_shapes=[
            pltpu.VMEM((chans // LANES, tokens, LANES), F32),
            pltpu.VMEM((modes, chans), F32),
            pltpu.SMEM((doc_lengths.shape[0],), jnp.int32),
        ],
        compiler_params=params(),
        cost_estimate=cost(2 * tokens * chans * modes, 2 * tokens * chans),
        name="leave",
    )(doc_lengths, rates, grad_out)


def back_kernel(
    lens_ref, rates_ref, residues_ref, skip_ref, grad_ref, seg_ref, dev_ref,
    out_ref, arrive_ref, wide_ref, conv_ref, decay_ref, weight_ref, cuts_ref,
):
    tokens, chans = grad_ref.shape
    modes = rates_ref.shape[0]
    seg_len = tokens // SEGS
    here = lax.axis_index("ctx")
    base = here * tokens
    starts = doc_starts(lens_ref)
    store_cuts(cuts_ref, cut_codes(starts, [0] * len(starts), base, seg_len))
    rates = rates_ref[...]
    decay_all = jnp.exp(-rates)
    decay_ref[...] = decay_all
    weight_ref[...] = residues_ref[...] * jnp.sqrt(1.0 - decay_all * decay_all)
    through = jnp.exp(-rates * float(tokens))
    arriving = jnp.zeros((modes, chans), F32)
    for k in range(dev_ref.shape[0] - 1, 0, -1):
        kept = jnp.where(any_start(starts, k * tokens, tokens), 0.0, 1.0)
        arriving = jnp.where(k > here, dev_ref[k] + (through * kept) * arriving, arriving)
    through = jnp.exp(-rates * float(seg_len))
    put_segment(arrive_ref, SEGS - 1, modes, arriving)
    for s in range(SEGS - 1, 0, -1):
        kept = jnp.where(any_start(starts, base + s * seg_len, seg_len), 0.0, 1.0)
        arriving = segment(seg_ref, s, modes) + (through * kept) * arriving
        put_segment(arrive_ref, s - 1, modes, arriving)
    widen(grad_ref, wide_ref)
    row = lax.broadcasted_iota(jnp.int32, (SEGS, LANES), 0)
    for h in range(chans // LANES):
        cols = slice(h * LANES, (h + 1) * LANES)
        decay = [spread(decay_ref, r, cols) for r in range(modes)]
        weight = [spread(weight_ref, r, cols) for r in range(modes)]
        skip = jnp.broadcast_to(skip_ref[:, cols], (SEGS, LANES))

        def step(i, state):
            rows = pl.ds(i, SEGS, stride=seg_len)
            grad = wide_ref[h, rows, :]
            back = tuple(grad + part for part in state)
            terms = [weight[r] * back[r] for r in range(modes)] + [skip * grad]
            while len(terms) > 1:
                terms = [a + b for a, b in zip(terms[::2], terms[1::2])] + terms[len(terms) // 2 * 2 :]
            conv_ref[h, rows, :] = terms[0]
            return tuple(decay[r] * back[r] for r in range(modes))

        def cut(segment, stream, state):
            hold = row != segment
            return tuple(jnp.where(hold, part, 0.0) for part in state)

        entry = tuple(arrive_ref[h, pl.ds(r, SEGS, stride=modes), :] for r in range(modes))
        time_loop(cuts_ref, seg_len, step, cut, entry)

    def narrow(k, _):
        rows = pl.ds(k * 64, 64)
        for h in range(conv_ref.shape[0]):
            out_ref[rows, h * LANES : (h + 1) * LANES] = conv_ref[h, rows, :].astype(BF16)
        return 0

    lax.fori_loop(0, tokens // 64, narrow, 0)


def back_pass(doc_lengths, rates, residues, skip, grad_out, seg_leaving, dev_leaving):
    modes, chans = rates.shape
    tokens = grad_out.shape[0]
    return pl.pallas_call(
        back_kernel,
        in_specs=[smem()] + [vmem()] * 6,
        out_specs=[vmem(), vmem()],
        out_shape=[
            jax.ShapeDtypeStruct((tokens, chans), BF16),
            jax.ShapeDtypeStruct((chans // LANES, SEGS * modes, LANES), F32),
        ],
        scratch_shapes=[
            pltpu.VMEM((chans // LANES, tokens, LANES), F32),
            pltpu.VMEM((chans // LANES, tokens, LANES), F32),
            pltpu.VMEM((modes, chans), F32),
            pltpu.VMEM((modes, chans), F32),
            pltpu.SMEM((doc_lengths.shape[0],), jnp.int32),
        ],
        compiler_params=params(),
        cost_estimate=cost(4 * tokens * chans * modes, 4 * tokens * chans),
        name="back_pass",
    )(doc_lengths, rates, residues, skip, grad_out, seg_leaving, dev_leaving)


def residue_kernel(
    window, lens_ref, streams_ref, rates_ref, grad_ref, x_ref, arrive_ref,
    out_ref, wide_ref, x_wide_ref, decay_ref, total_ref, cuts_ref,
):
    tokens, chans = grad_ref.shape
    modes = rates_ref.shape[0]
    seg_len = tokens // SEGS
    base = lax.axis_index("ctx") * tokens
    starts = doc_starts(lens_ref)
    streams = [streams_ref[k] for k in range(len(starts) + 1)]
    store_cuts(cuts_ref, cut_codes(starts, streams[1:], base, seg_len))
    decay_all = jnp.exp(-rates_ref[...])
    decay_ref[...] = decay_all
    widen(grad_ref, wide_ref)
    widen(x_ref, x_wide_ref)
    total_ref[...] = jnp.zeros_like(total_ref)
    row = lax.broadcasted_iota(jnp.int32, (SEGS, LANES), 0)
    first = base + row * seg_len
    stream_at = jnp.full((SEGS, LANES), streams[0], jnp.int32)
    for start, stream in zip(starts, streams[1:]):
        stream_at = jnp.where(first >= start, stream, stream_at)
    for h in range(chans // LANES):
        cols = slice(h * LANES, (h + 1) * LANES)
        decay = [spread(decay_ref, r, cols) for r in range(modes)]

        def step(i, carry):
            state, total = carry
            rows = pl.ds(i, SEGS, stride=seg_len)
            grad = wide_ref[h, rows, :]
            x = x_wide_ref[h, rows, :]
            back = tuple(grad + part for part in state)
            total = tuple(total[r] + x * back[r] for r in range(modes))
            return (tuple(decay[r] * back[r] for r in range(modes)), total)

        def cut(segment, stream, carry):
            state, total = carry
            hold = row != segment
            for r in range(modes):
                total_ref[stream, r, :, cols] += jnp.where(hold, 0.0, total[r])
            return (
                tuple(jnp.where(hold, part, 0.0) for part in state),
                tuple(jnp.where(hold, part, 0.0) for part in total),
            )

        zero = jnp.zeros((SEGS, LANES), F32)
        entry = tuple(arrive_ref[h, pl.ds(r, SEGS, stride=modes), :] for r in range(modes))
        _, total = time_loop(cuts_ref, seg_len, step, cut, (entry, (zero,) * modes))
        for s in range(2):
            for r in range(modes):
                total_ref[s, r, :, cols] += jnp.where(stream_at == s, total[r], 0.0)
    scale = jnp.sqrt(1.0 - decay_all * decay_all) / math.sqrt(window)
    for s in range(2):
        part = (jnp.sum(total_ref[s], axis=1) * scale).astype(BF16)
        for k in range(out_ref.shape[0]):
            out_ref[k, s] = part


def residue_pass(doc_lengths, doc_streams, rates, grad_out, x_cols, arriving, copies, window):
    modes, chans = rates.shape
    tokens = grad_out.shape[0]

    def kernel(*refs):
        residue_kernel(window, *refs)

    return pl.pallas_call(
        kernel,
        in_specs=[smem(), smem()] + [vmem()] * 4,
        out_specs=vmem(),
        out_shape=jax.ShapeDtypeStruct((copies, 2, modes, chans), BF16),
        scratch_shapes=[
            pltpu.VMEM((chans // LANES, tokens, LANES), F32),
            pltpu.VMEM((chans // LANES, tokens, LANES), F32),
            pltpu.VMEM((modes, chans), F32),
            pltpu.VMEM((2, modes, SEGS, chans), F32),
            pltpu.SMEM((doc_lengths.shape[0],), jnp.int32),
        ],
        compiler_params=params(),
        cost_estimate=cost(4 * tokens * chans * modes, 4 * tokens * chans),
        name="residue_pass",
    )(doc_lengths, doc_streams, rates, grad_out, x_cols, arriving)


def local(u_rows, gain, skip, residues, rates, grad_out, doc_lengths, doc_streams):
    ctx, groups = lax.axis_size("ctx"), lax.axis_size("ch")
    tokens, chans = grad_out.shape
    gain = gain[None, :]
    rates, residues = rates.T, residues.T
    x_send = norm_rows(u_rows, gain, groups)
    x_cols = lax.all_to_all(x_send, "ch", split_axis=0, concat_axis=0, tiled=True)
    x_cols = x_cols.reshape(tokens, chans)
    seg_leaving, dev_leaving = leave(doc_lengths, rates, grad_out, ctx)
    dev_leaving = lax.all_to_all(dev_leaving, "ctx", split_axis=0, concat_axis=0, tiled=True)
    normed_grad, arriving = back_pass(
        doc_lengths, rates, residues, skip[None, :], grad_out, seg_leaving, dev_leaving
    )
    grad_rows = lax.all_to_all(
        normed_grad.reshape(groups, tokens // groups, chans), "ch", split_axis=0, concat_axis=0, tiled=True
    )
    parts = residue_pass(
        doc_lengths, doc_streams, rates, grad_out, x_cols, arriving, ctx, tokens * ctx
    )
    parts = lax.all_to_all(parts, "ctx", split_axis=0, concat_axis=0, tiled=True)
    residue_grad = jnp.sum(parts.astype(F32), axis=0).transpose(0, 2, 1)
    input_grad = final_rows(u_rows, gain, grad_rows)
    return (input_grad, residue_grad)


def solution(mesh):
    return jax.shard_map(
        local,
        mesh=mesh,
        in_specs=(
            P(("ctx", "ch"), None),
            P(),
            P("ch"),
            P("ch", None),
            P("ch", None),
            P("ctx", "ch"),
            P(),
            P(),
        ),
        out_specs=(P(("ctx", "ch"), None), P(None, "ch", None)),
        check_vma=False,
    )
```

time: 869 us -> 87.3 us (0.10); the launches traced: 853 us -> 86.6 us
  blocking collectives: 252 us -> 0 us
  other arithmetic: 195 us -> 0.63 us
  matrix products: 191 us -> 0 us
  local copies, waits for them, and re-layouts: 183 us -> 9.63 us
  Pallas kernels: 0 us -> 25 us
  waiting for transfers between devices: 0.01 us -> 24.8 us
  loops' own time: 17 us -> 0 us
  starting transfers between devices: 12.9 us -> 25.8 us
    dot_general x64 -> x0, matrix products: 191 us -> none  [the longest x16 57.6 us: forward(): jnp.dot(forward_mask, ratio, precision=highest).reshape(block, chans, modes)]
    psum x3 -> x0, blocking collectives: 175 us -> none  [the longest x1 82 us: local(): project = lax.psum(jnp.sum(normal_cols * scaled, axis=1), 'ch') / width]
    mul x82 -> x0, other arithmetic: 90.1 us -> none  [the longest x16 39.5 us: forward(): dy_float * reach]
    all_gather x4 -> x0, blocking collectives: 77.3 us -> none  [the longest x2 40.7 us: prefix_2(): everything = jax.tree.map(lambda part: lax.all_gather(part, axis), value)]
    dynamic_slice x89 -> x0, local copies, waits for them, and re-layouts: 41.3 us -> none  [the longest x32 20.4 us: conv_backward(): lax.map(correct, (jnp.arange(blocks, dtype=jnp.int32), conv_blocks, tail_...]
    exp x16 -> x0, local copies, waits for them, and re-layouts: 36.1 us -> none  [conv_backward(): powers = jnp.exp(-rates[None] * offsets[:, None, None])]
    convert_element_type x57 -> x0, other arithmetic: 32.3 us -> none  [the longest x16 13.7 us: forward(): dy_float = dy_block.astype(jnp.float32)[:, :, None]]
    another operation x68 -> x0, local copies, waits for them, and re-layouts: 28.9 us -> none
  transfers between devices with their start and end apart: 2 -> 4, of which waited for: 0 -> 4; matrix products, arithmetic and copies ran while one was open for 18% -> 0% of each run, Pallas kernels for 0% -> 23%
where the time goes in v1:
time: 87.3 us; the launch traced here: 86.6 us
  starting transfers between devices  25.8 us (30%)
  Pallas kernels  25 us (29%)
  waiting for transfers between devices  24.8 us (28%)
  local copies, waits for them, and re-layouts  9.63 us (11%)
    unnamed x32, local copies, waits for them, and re-layouts  9.63 us
    all_to_all x1, starting transfers between devices, local(): lax.all_to_all(x_send, 'ch', split_axis=0, concat_axis=0, tiled=True)  9.5 us
    all_to_all x1, starting transfers between devices, local(): lax.all_to_all(dev_leaving, 'ctx', split_axis=0, concat_axis=0, tiled=True)  9.01 us
    pallas_call x1, Pallas kernels, residue_pass(): pl.pallas_call(kernel, in_specs=[smem(), smem()] + [vmem()] * 4, out_spec...  8.85 us
    pallas_call x1, Pallas kernels, back_pass(): pl.pallas_call(back_kernel, in_specs=[smem()] + [vmem()] * 6, out_specs=[...  7.53 us
    all_to_all x1, waiting for transfers between devices, local(): lax.all_to_all(x_send, 'ch', split_axis=0, concat_axis=0, tiled=True)  6.82 us
    all_to_all x1, waiting for transfers between devices, local(): lax.all_to_all(normed_grad.reshape(groups, tokens // groups, chans), 'ch'...  6.18 us
    all_to_all x1, waiting for transfers between devices, local(): lax.all_to_all(parts, 'ctx', split_axis=0, concat_axis=0, tiled=True)  6.01 us
  transfers between devices with their start and end apart: 4, of which 4 were waited for; matrix products, arithmetic and copies ran while one was open for 0% of the time, Pallas kernels for 23%

profile of v1, /device:TPU:1, one launch (start us, length us, event | category | flops | bytes accessed | tf_op | source)
XLA Modules:
  0.0 86.6 jit_solution(13703365696582488143)
XLA Ops:
  0.6 0.0 copy-start.13
  0.6 0.6 copy-done.13
  1.3 0.0 copy-start
  1.3 1.2 %copy-done = bf16[2048,256]{1,0:T(8,128)(2,1)S(1)} copy-done((bf16[2048,256]{1,0:T(8,128)(2,1)S(1)}, bf16[2048,256]{1,0:T(8,128)(2,1)}, u32[]{:S(2)}) %copy-start) | copy-done | bytes 1048600
  2.5 0.0 copy-start.7
  2.5 0.7 copy-done.7
  3.2 0.0 copy-start.2
  3.2 5.1 %leave.1 = (f32[2,128,128]{2,1,0:T(8,128)S(1)}, f32[8,16,256]{2,1,0:T(8,128)}) custom-call(s32[4]{0:T(128)S(1)} %copy-done.13, f32[16,256]{1,0:T(8,128)S(1)} %bitcast.9, bf16[2048,256]{1,0:T(8,128)(2,1)S(1)} %copy-done), custom_call_target="tpu_custom_call" | custom-call | flops 16777216 | bytes 1048576 | tf_op jit(solution)/shard_map/leave/pallas_call | solution.py:234
  8.3 0.0 copy-start.10
  8.3 0.0 copy-start.9
  8.3 0.6 copy-done.10
  9.0 9.0 %all-to-all-start = ((f32[8,16,256]{2,1,0:T(8,128)}), f32[8,16,256]{2,1,0:T(8,128)S(1)}, u32[]{:S(2)}, u32[]{:S(2)}) async-start(f32[8,16,256]{2,1,0:T(8,128)} %get-tuple-element.7), calls=%async_computation | async-start | bytes 262144 | tf_op jit(solution)/shard_map/all_to_all | solution.py:428
  18.0 0.0 copy-done.2
  18.0 0.0 copy-done.9
  18.0 1.0 %norm_rows.1 = bf16[32,64,256]{2,1,0:T(8,128)(2,1)S(1)} custom-call(bf16[64,8192]{1,0:T(8,128)(2,1)S(1)} %copy-done.2, f32[1,8192]{1,0:T(1,128)S(1)} %bitcast.12), custom_call_target="tpu_custom_call" | custom-call | flops 4194304 | bytes 2097152 | tf_op jit(solution)/shard_map/norm_rows/pallas_call | solution.py:55
  19.0 0.0 copy-start.5
  19.0 1.0 %copy-done.5 = bf16[32,64,256]{2,1,0:T(8,128)(2,1)} copy-done((bf16[32,64,256]{2,1,0:T(8,128)(2,1)}, bf16[32,64,256]{2,1,0:T(8,128)(2,1)S(1)}, u32[]{:S(2)}) %copy-start.5) | copy-done | bytes 1048600
  20.0 0.0 copy-start.1
  20.0 5.8 %all-to-all-done.dev_ref = f32[8,16,256]{2,1,0:T(8,128)S(1)} async-done(((f32[8,16,256]{2,1,0:T(8,128)}), f32[8,16,256]{2,1,0:T(8,128)S(1)}, u32[]{:S(2)}, u32[]{:S(2)}) %all-to-all-start) | async-done | bytes 131104 | tf_op jit(solution)/shard_map/all_to_all | solution.py:428
  25.8 0.0 copy-start.8
  25.8 0.0 copy-start.12
  25.8 9.5 %all-to-all-start.2 = ((bf16[32,64,256]{2,1,0:T(8,128)(2,1)}), bf16[32,64,256]{2,1,0:T(8,128)(2,1)S(1)}, u32[]{:S(2)}, u32[]{:S(2)}) async-start(bf16[32,64,256]{2,1,0:T(8,128)(2,1)} %copy-done.5), calls=%async_computation.2 | async-start | bytes 2097152 | tf_op jit(solution)/shard_map/all_to_all | solution.py:425
  35.3 0.0 copy-start.14
  35.3 0.0 copy-done.1
  35.3 0.0 copy-done.8
  35.3 0.0 copy-done.12
  35.3 0.6 copy-done.14
  36.0 0.0 copy-start.11
  36.0 0.9 %copy-done.11 = f32[2,128,128]{2,1,0:T(8,128)S(1)} copy-done((f32[2,128,128]{2,1,0:T(8,128)S(1)}, f32[2,128,128]{2,1,0:T(8,128)}, u32[]{:S(2)}) %copy-start.11) | copy-done | bytes 131096
  36.9 7.5 %back_pass.1 = (bf16[2048,256]{1,0:T(8,128)(2,1)S(1)}, f32[2,128,128]{2,1,0:T(8,128)S(1)}) custom-call(s32[4]{0:T(128)S(1)} %copy-done.13, f32[16,256]{1,0:T(8,128)S(1)} %bitcast.10, f32[16,256]{1,0:T(8,128)S(1)} %bitcast.14, f32[1,256]{1,0:T(1,128)S(1)} %bitcast.15, bf16[2048,256]{1,0:T(8,128)(2,1)S(1)} %copy-done.1, f32[2,128,128]{2,1,0:T(8,128)S(1)} %copy-done.11, ...), custom_call_target="tpu_custom_call" | custom-call | flops 33554432 | bytes 2097152 | tf_op jit(solution)/shard_map/back_pass/pallas_call | solution.py:316
  44.4 0.0 copy-start.6
  44.4 1.0 %copy-done.6 = bf16[2048,256]{1,0:T(8,128)(2,1)} copy-done((bf16[2048,256]{1,0:T(8,128)(2,1)}, bf16[2048,256]{1,0:T(8,128)(2,1)S(1)}, u32[]{:S(2)}) %copy-start.6) | copy-done | bytes 1048600
  45.4 6.8 %all-to-all-done.2 = bf16[32,64,256]{2,1,0:T(8,128)(2,1)S(1)} async-done(((bf16[32,64,256]{2,1,0:T(8,128)(2,1)}), bf16[32,64,256]{2,1,0:T(8,128)(2,1)S(1)}, u32[]{:S(2)}, u32[]{:S(2)}) %all-to-all-start.2) | async-done | bytes 1048608 | tf_op jit(solution)/shard_map/all_to_all | solution.py:425
  52.2 0.0 copy-start.3
  52.2 1.0 %copy-done.3 = bf16[32,64,256]{2,1,0:T(8,128)(2,1)} copy-done((bf16[32,64,256]{2,1,0:T(8,128)(2,1)}, bf16[32,64,256]{2,1,0:T(8,128)(2,1)S(1)}, u32[]{:S(2)}) %copy-start.3) | copy-done | bytes 1048600
  53.2 4.0 %all-to-all-start.1 = ((bf16[32,64,256]{2,1,0:T(8,128)(2,1)}), bf16[32,64,256]{2,1,0:T(8,128)(2,1)S(1)}, u32[]{:S(2)}, u32[]{:S(2)}) async-start(bf16[32,64,256]{2,1,0:T(8,128)(2,1)} %bitcast.8), calls=%async_computation.1 | async-start | bytes 2097152 | tf_op jit(solution)/shard_map/all_to_all | solution.py:432
  57.1 0.0 copy-start.15
  57.2 0.6 copy-done.15
  57.8 0.0 copy-start.4
  57.8 1.2 %copy-done.4 = bf16[32,64,256]{2,1,0:T(8,128)(2,1)S(1)} copy-done((bf16[32,64,256]{2,1,0:T(8,128)(2,1)S(1)}, bf16[32,64,256]{2,1,0:T(8,128)(2,1)}, u32[]{:S(2)}) %copy-start.4) | copy-done | bytes 1048600
  59.0 8.8 %residue_pass.1 = bf16[8,2,16,256]{3,2,1,0:T(8,128)(2,1)} custom-call(s32[4]{0:T(128)S(1)} %copy-done.13, s32[4]{0:T(128)S(1)} %copy-done.15, f32[16,256]{1,0:T(8,128)S(1)} %bitcast.11, bf16[2048,256]{1,0:T(8,128)(2,1)S(1)} %copy-done.1, bf16[2048,256]{1,0:T(8,128)(2,1)S(1)} %bitcast.7, f32[2,128,128]{2,1,0:T(8,128)S(1)} %get-tuple-element.9.refs_5_), custom_call_target="tpu_custom_call" | custom-call | flops 33554432 | bytes 2097152 | tf_op jit(solution)/shard_map/residue_pass/pallas_call | solution.py:401
  67.9 6.2 %all-to-all-done.1.grad_ref = bf16[32,64,256]{2,1,0:T(8,128)(2,1)S(1)} async-done(((bf16[32,64,256]{2,1,0:T(8,128)(2,1)}), bf16[32,64,256]{2,1,0:T(8,128)(2,1)S(1)}, u32[]{:S(2)}, u32[]{:S(2)}) %all-to-all-start.1) | async-done | bytes 1048608 | tf_op jit(solution)/shard_map/all_to_all | solution.py:432
  74.1 3.4 %all-to-all-start.3 = ((bf16[8,2,16,256]{3,2,1,0:T(8,128)(2,1)}), bf16[8,2,16,256]{3,2,1,0:T(8,128)(2,1)S(1)}, u32[]{:S(2)}, u32[]{:S(2)}) async-start(bf16[8,2,16,256]{3,2,1,0:T(8,128)(2,1)} %residue_pass.1), calls=%async_computation.3 | async-start | bytes 262144 | tf_op jit(solution)/shard_map/all_to_all | solution.py:438
  77.4 2.5 %final_rows.1 = bf16[64,8192]{1,0:T(8,128)(2,1)} custom-call(bf16[64,8192]{1,0:T(8,128)(2,1)S(1)} %copy-done.2, f32[1,8192]{1,0:T(1,128)S(1)} %bitcast.13, bf16[32,64,256]{2,1,0:T(8,128)(2,1)S(1)} %all-to-all-done.1.grad_ref), custom_call_target="tpu_custom_call" | custom-call | flops 8388608 | bytes 3145728 | tf_op jit(solution)/shard_map/final_rows/pallas_call | solution.py:90
  80.0 6.0 %all-to-all-done.3 = bf16[8,2,16,256]{3,2,1,0:T(8,128)(2,1)S(1)} async-done(((bf16[8,2,16,256]{3,2,1,0:T(8,128)(2,1)}), bf16[8,2,16,256]{3,2,1,0:T(8,128)(2,1)S(1)}, u32[]{:S(2)}, u32[]{:S(2)}) %all-to-all-start.3) | async-done | bytes 131104 | tf_op jit(solution)/shard_map/all_to_all | solution.py:438
  86.0 0.6 convert_reduce_fusion
Async XLA Ops:
  0.6 0.7 copy-start.13
  1.3 1.2 %copy-start = (bf16[2048,256]{1,0:T(8,128)(2,1)S(1)}, bf16[2048,256]{1,0:T(8,128)(2,1)}, u32[]{:S(2)}) copy-start(bf16[2048,256]{1,0:T(8,128)(2,1)} %refs_3_.1) | copy-start | bytes 3145732
  2.5 0.7 copy-start.7
  3.2 14.8 %copy-start.2 = (bf16[64,8192]{1,0:T(8,128)(2,1)S(1)}, bf16[64,8192]{1,0:T(8,128)(2,1)}, u32[]{:S(2)}) copy-start(bf16[64,8192]{1,0:T(8,128)(2,1)} %u_ref.3) | copy-start | bytes 3145732
  8.3 0.7 copy-start.10
  8.3 9.7 %copy-start.9 = (f32[8192]{0:T(1024)S(1)}, f32[8192]{0:T(1024)}, u32[]{:S(2)}) copy-start(f32[8192]{0:T(1024)} %param.9) | copy-start | bytes 98308
  9.0 16.8 %all-to-all-start = ((f32[8,16,256]{2,1,0:T(8,128)}), f32[8,16,256]{2,1,0:T(8,128)S(1)}, u32[]{:S(2)}, u32[]{:S(2)}) async-start(f32[8,16,256]{2,1,0:T(8,128)} %get-tuple-element.7), calls=%async_computation | async-start | bytes 262144 | tf_op jit(solution)/shard_map/all_to_all | solution.py:428
  19.0 1.0 %copy-start.5 = (bf16[32,64,256]{2,1,0:T(8,128)(2,1)}, bf16[32,64,256]{2,1,0:T(8,128)(2,1)S(1)}, u32[]{:S(2)}) copy-start(bf16[32,64,256]{2,1,0:T(8,128)(2,1)S(1)} %norm_rows.1) | copy-start | bytes 3145732
  20.0 15.3 %copy-start.1 = (bf16[2048,256]{1,0:T(8,128)(2,1)S(1)}, bf16[2048,256]{1,0:T(8,128)(2,1)}, u32[]{:S(2)}) copy-start(bf16[2048,256]{1,0:T(8,128)(2,1)} %refs_3_.1) | copy-start | bytes 3145732
  25.8 9.5 %copy-start.8 = (f32[256,16]{0,1:T(8,128)S(1)}, f32[256,16]{0,1:T(8,128)}, u32[]{:S(2)}) copy-start(f32[256,16]{0,1:T(8,128)} %param.12) | copy-start | bytes 49156
  25.8 9.5 %copy-start.12 = (f32[256,16]{0,1:T(8,128)S(1)}, f32[256,16]{0,1:T(8,128)}, u32[]{:S(2)}) copy-start(f32[256,16]{0,1:T(8,128)} %param.11) | copy-start | bytes 49156
  25.8 26.4 %all-to-all-start.2 = ((bf16[32,64,256]{2,1,0:T(8,128)(2,1)}), bf16[32,64,256]{2,1,0:T(8,128)(2,1)S(1)}, u32[]{:S(2)}, u32[]{:S(2)}) async-start(bf16[32,64,256]{2,1,0:T(8,128)(2,1)} %copy-done.5), calls=%async_computation.2 | async-start | bytes 2097152 | tf_op jit(solution)/shard_map/all_to_all | solution.py:425
  35.3 0.7 copy-start.14
  36.0 0.9 %copy-start.11 = (f32[2,128,128]{2,1,0:T(8,128)S(1)}, f32[2,128,128]{2,1,0:T(8,128)}, u32[]{:S(2)}) copy-start(f32[2,128,128]{2,1,0:T(8,128)} %copy-done.10) | copy-start | bytes 393220
  44.4 1.0 %copy-start.6 = (bf16[2048,256]{1,0:T(8,128)(2,1)}, bf16[2048,256]{1,0:T(8,128)(2,1)S(1)}, u32[]{:S(2)}) copy-start(bf16[2048,256]{1,0:T(8,128)(2,1)S(1)} %get-tuple-element.8) | copy-start | bytes 3145732
  52.2 1.0 %copy-start.3 = (bf16[32,64,256]{2,1,0:T(8,128)(2,1)}, bf16[32,64,256]{2,1,0:T(8,128)(2,1)S(1)}, u32[]{:S(2)}) copy-start(bf16[32,64,256]{2,1,0:T(8,128)(2,1)S(1)} %all-to-all-done.2) | copy-start | bytes 3145732
  53.2 20.9 %all-to-all-start.1 = ((bf16[32,64,256]{2,1,0:T(8,128)(2,1)}), bf16[32,64,256]{2,1,0:T(8,128)(2,1)S(1)}, u32[]{:S(2)}, u32[]{:S(2)}) async-start(bf16[32,64,256]{2,1,0:T(8,128)(2,1)} %bitcast.8), calls=%async_computation.1 | async-start | bytes 2097152 | tf_op jit(solution)/shard_map/all_to_all | solution.py:432
  57.1 0.7 copy-start.15
  57.8 1.2 %copy-start.4 = (bf16[32,64,256]{2,1,0:T(8,128)(2,1)S(1)}, bf16[32,64,256]{2,1,0:T(8,128)(2,1)}, u32[]{:S(2)}) copy-start(bf16[32,64,256]{2,1,0:T(8,128)(2,1)} %copy-done.3) | copy-start | bytes 3145732
  74.1 11.9 %all-to-all-start.3 = ((bf16[8,2,16,256]{3,2,1,0:T(8,128)(2,1)}), bf16[8,2,16,256]{3,2,1,0:T(8,128)(2,1)S(1)}, u32[]{:S(2)}, u32[]{:S(2)}) async-start(bf16[8,2,16,256]{3,2,1,0:T(8,128)(2,1)} %residue_pass.1), calls=%async_computation.3 | async-start | bytes 262144 | tf_op jit(solution)/shard_map/all_to_all | solution.py:438

commit v2 on v1

v2 whole, which is shorter than its diff:
```python
import math

import jax
import jax.numpy as jnp
from jax import lax
from jax.experimental import pallas as pl
from jax.experimental.pallas import tpu as pltpu
from jax.sharding import PartitionSpec as P

F32 = jnp.float32
BF16 = jnp.bfloat16
SEGS = 8
LANES = 128
UNROLL = 8
PIECES = 4
ROW_BLOCK = 16


def cost(flops, size):
    return pl.CostEstimate(flops=flops, bytes_accessed=size, transcendentals=0)


def load(pairs, sems):
    copies = [pltpu.make_async_copy(a, b, sems.at[k]) for k, (a, b) in enumerate(pairs)]
    for copy in copies:
        copy.start()
    return copies


def call(kernel, outs, scratch, sems, name, estimate, *operands):
    return pl.pallas_call(
        kernel,
        in_specs=[pl.BlockSpec(memory_space=pl.ANY)] * len(operands),
        out_specs=[pl.BlockSpec(memory_space=pl.ANY)] * len(outs),
        out_shape=outs,
        scratch_shapes=scratch + [pltpu.SemaphoreType.DMA((sems,))],
        compiler_params=pltpu.CompilerParams(vmem_limit_bytes=60 * 1024 * 1024),
        cost_estimate=estimate,
        name=name,
    )(*operands)


def inverse_rms(u_ref, eps=1e-05):
    rows, width = u_ref.shape
    total = jnp.zeros((rows, LANES), F32)
    for c in range(width // LANES):
        part = u_ref[:, c * LANES : (c + 1) * LANES].astype(F32)
        total = total + part * part
    return lax.rsqrt(jnp.sum(total, axis=1, keepdims=True) / width + eps)


def norm_kernel(u_hbm, gain_hbm, out_hbm, u_ref, gain_ref, out_ref, sems):
    blocks, groups, rows, chans = out_ref.shape
    span = [pl.ds(b * rows, rows) for b in range(blocks)]
    gain_copy, *u_copies = load(
        [(gain_hbm, gain_ref)] + [(u_hbm.at[span[b]], u_ref.at[b]) for b in range(blocks)], sems
    )
    gain_copy.wait()
    out_copies = []
    for b in range(blocks):
        u_copies[b].wait()
        inv = inverse_rms(u_ref.at[b])
        for c in range(groups):
            cols = slice(c * chans, (c + 1) * chans)
            normal = u_ref[b, :, cols].astype(F32) * inv
            out_ref[b, c] = (normal * gain_ref[:, cols]).astype(BF16)
        copy = pltpu.make_async_copy(out_ref.at[b], out_hbm.at[:, span[b]], sems.at[1 + blocks + b])
        copy.start()
        out_copies.append(copy)
    for copy in out_copies:
        copy.wait()


def norm_rows(u_rows, gain, groups):
    rows, width = u_rows.shape
    chans, blocks = width // groups, rows // ROW_BLOCK
    return call(
        norm_kernel,
        [jax.ShapeDtypeStruct((groups, rows, chans), BF16)],
        [
            pltpu.VMEM((blocks, ROW_BLOCK, width), BF16),
            pltpu.VMEM((1, width), F32),
            pltpu.VMEM((blocks, groups, ROW_BLOCK, chans), BF16),
        ],
        1 + 2 * blocks,
        "norm_rows",
        cost(8 * rows * width, 4 * rows * width),
        u_rows,
        gain,
    )[0]


def final_kernel(u_hbm, gain_hbm, grad_hbm, out_hbm, u_ref, gain_ref, grad_ref, out_ref, sems):
    blocks, groups, rows, chans = grad_ref.shape
    width = groups * chans
    span = [pl.ds(b * rows, rows) for b in range(blocks)]
    gain_copy, *copies = load(
        [(gain_hbm, gain_ref)]
        + [(u_hbm.at[span[b]], u_ref.at[b]) for b in range(blocks)]
        + [(grad_hbm.at[:, span[b]], grad_ref.at[b]) for b in range(blocks)],
        sems,
    )
    gain_copy.wait()
    out_copies = []
    for b in range(blocks):
        copies[b].wait()
        inv = inverse_rms(u_ref.at[b])
        copies[blocks + b].wait()
        total = jnp.zeros((rows, chans), F32)
        for c in range(groups):
            cols = slice(c * chans, (c + 1) * chans)
            normal = u_ref[b, :, cols].astype(F32) * inv
            total = total + normal * (gain_ref[:, cols] * grad_ref[b, c].astype(F32))
        project = jnp.sum(total, axis=1, keepdims=True) / width
        for c in range(groups):
            cols = slice(c * chans, (c + 1) * chans)
            normal = u_ref[b, :, cols].astype(F32) * inv
            scaled = gain_ref[:, cols] * grad_ref[b, c].astype(F32)
            out_ref[b, :, cols] = (inv * (scaled - normal * project)).astype(BF16)
        copy = pltpu.make_async_copy(out_ref.at[b], out_hbm.at[span[b]], sems.at[1 + 2 * blocks + b])
        copy.start()
        out_copies.append(copy)
    for copy in out_copies:
        copy.wait()


def final_rows(u_rows, gain, grad_rows):
    rows, width = u_rows.shape
    groups, _, chans = grad_rows.shape
    blocks = rows // ROW_BLOCK
    return call(
        final_kernel,
        [jax.ShapeDtypeStruct((rows, width), BF16)],
        [
            pltpu.VMEM((blocks, ROW_BLOCK, width), BF16),
            pltpu.VMEM((1, width), F32),
            pltpu.VMEM((blocks, groups, ROW_BLOCK, chans), BF16),
            pltpu.VMEM((blocks, ROW_BLOCK, width), BF16),
        ],
        1 + 3 * blocks,
        "final_rows",
        cost(16 * rows * width, 6 * rows * width),
        u_rows,
        gain,
        grad_rows,
    )[0]


def doc_starts(lens_ref):
    starts, at = [], jnp.int32(0)
    for k in range(lens_ref.shape[0] - 1):
        at = at + lens_ref[k]
        starts.append(at)
    return starts


def sort_down(codes):
    codes = list(codes)
    for end in range(len(codes) - 1, 0, -1):
        for k in range(end):
            high = jnp.maximum(codes[k], codes[k + 1])
            low = jnp.minimum(codes[k], codes[k + 1])
            codes[k], codes[k + 1] = high, low
    return codes


def cut_codes(starts, streams, base, seg_len):
    codes = []
    for start, stream in zip(starts, streams):
        place = start - base
        inside = (place >= 0) & (place < SEGS * seg_len)
        code = (place % seg_len) * 16 + place // seg_len
        codes.append(jnp.where(inside, code, 15) * 2 + stream)
    return sort_down(codes)


def any_start(starts, first, count):
    found = jnp.bool_(False)
    for start in starts:
        found = found | ((start >= first) & (start < first + count))
    return found


def time_loop(cuts_ref, seg_len, step, cut, carry):
    def piece(p, state):
        top, inner = state
        code = cuts_ref[p]
        low = code // 32
        count = top - low
        full = count // UNROLL

        def many(k, value):
            first = top - (k + 1) * UNROLL
            for j in range(UNROLL - 1, -1, -1):
                value = step(first + j, value)
            return value

        def one(k, value):
            return step(top - full * UNROLL - 1 - k, value)

        inner = lax.fori_loop(0, full, many, inner)
        inner = lax.fori_loop(0, count - full * UNROLL, one, inner)
        inner = cut((code // 2) % 16, code % 2, inner)
        return (low, inner)

    return lax.fori_loop(0, cuts_ref.shape[0], piece, (jnp.int32(seg_len), carry))[1]


def pieces(source_ref, target_ref):
    chunk = source_ref.shape[0] // PIECES
    spans = [pl.ds(k * chunk, chunk) for k in range(PIECES)]
    return [(source_ref.at[rows], target_ref.at[rows]) for rows in spans]


def widen(source_ref, target_ref, copies, chunk=32):
    halves, tokens, _ = target_ref.shape
    size = tokens // len(copies)
    for k, copy in enumerate(copies):
        copy.wait()

        def body(j, _):
            rows = pl.ds(k * size + j * chunk, chunk)
            for h in range(halves):
                target_ref[h, rows, :] = source_ref[rows, h * LANES : (h + 1) * LANES].astype(F32)
            return 0

        lax.fori_loop(0, size // chunk, body, 0)


def spread(ref, r, cols):
    return jnp.broadcast_to(ref[r : r + 1, cols], (SEGS, LANES))


def segment(ref, s, modes):
    rows = slice(s * modes, (s + 1) * modes)
    return jnp.concatenate([ref[h, rows, :] for h in range(ref.shape[0])], axis=1)


def put_segment(ref, s, modes, value):
    for h in range(ref.shape[0]):
        ref[h, s * modes : (s + 1) * modes, :] = value[:, h * LANES : (h + 1) * LANES]


def store_cuts(cuts_ref, codes):
    for k, code in enumerate(codes):
        cuts_ref[k] = code
    cuts_ref[len(codes)] = jnp.int32(30)


def leave_kernel(
    lens_hbm, rates_hbm, grad_hbm, seg_hbm, dev_hbm,
    lens_ref, rates_ref, grad_ref, seg_ref, dev_ref, wide_ref, decay_ref, cuts_ref, sems,
):
    tokens, chans = grad_ref.shape
    modes = rates_ref.shape[0]
    seg_len = tokens // SEGS
    lens_copy, rates_copy, *grad_copies = load(
        [(lens_hbm, lens_ref), (rates_hbm, rates_ref)] + pieces(grad_hbm, grad_ref), sems
    )
    base = lax.axis_index("ctx") * tokens
    lens_copy.wait()
    starts = doc_starts(lens_ref)
    store_cuts(cuts_ref, cut_codes(starts, [0] * len(starts), base, seg_len))
    rates_copy.wait()
    decay_ref[...] = jnp.exp(-rates_ref[...])
    widen(grad_ref, wide_ref, grad_copies)
    row = lax.broadcasted_iota(jnp.int32, (SEGS, LANES), 0)
    for h in range(chans // LANES):
        cols = slice(h * LANES, (h + 1) * LANES)
        decay = [spread(decay_ref, r, cols) for r in range(modes)]

        def step(i, state):
            grad = wide_ref[h, pl.ds(i, SEGS, stride=seg_len), :]
            return tuple(grad + decay[r] * state[r] for r in range(modes))

        def cut(place, stream, state):
            hold = row != place
            return tuple(jnp.where(hold, part, 0.0) for part in state)

        zero = jnp.zeros((SEGS, LANES), F32)
        state = time_loop(cuts_ref, seg_len, step, cut, (zero,) * modes)
        for r in range(modes):
            seg_ref[h, pl.ds(r, SEGS, stride=modes), :] = decay[r] * state[r]
    through = jnp.exp(-rates_ref[...] * float(seg_len))
    leaving = segment(seg_ref, SEGS - 1, modes)
    for s in range(SEGS - 2, -1, -1):
        kept = jnp.where(any_start(starts, base + s * seg_len, seg_len), 0.0, 1.0)
        leaving = segment(seg_ref, s, modes) + (through * kept) * leaving
    dev_ref[...] = leaving
    for copy in load([(dev_ref, dev_hbm), (seg_ref, seg_hbm)], sems):
        copy.wait()


def state_scratch(docs, modes, tokens, chans):
    halves = chans // LANES
    return {
        "lens": pltpu.SMEM((docs,), jnp.int32),
        "cuts": pltpu.SMEM((docs,), jnp.int32),
        "mode": pltpu.VMEM((modes, chans), F32),
        "narrow": pltpu.VMEM((tokens, chans), BF16),
        "wide": pltpu.VMEM((halves, tokens, LANES), F32),
        "segs": pltpu.VMEM((halves, SEGS * modes, LANES), F32),
    }


def leave(doc_lengths, rates, grad_out):
    modes, chans = rates.shape
    tokens = grad_out.shape[0]
    kinds = state_scratch(doc_lengths.shape[0], modes, tokens, chans)
    return call(
        leave_kernel,
        [
            jax.ShapeDtypeStruct((chans // LANES, SEGS * modes, LANES), F32),
            jax.ShapeDtypeStruct((modes, chans), F32),
        ],
        [kinds[k] for k in ("lens", "mode", "narrow", "segs", "mode", "wide", "mode", "cuts")],
        2 + PIECES,
        "leave",
        cost(2 * tokens * chans * modes, 2 * tokens * chans),
        doc_lengths,
        rates,
        grad_out,
    )


def back_kernel(
    lens_hbm, rates_hbm, residues_hbm, skip_hbm, grad_hbm, seg_hbm, *refs,
):
    later = refs[: -14]
    (out_hbm, arrive_hbm, lens_ref, rates_ref, weight_ref, skip_ref, grad_ref, seg_ref, later_ref,
     arrive_ref, wide_ref, decay_ref, cuts_ref, sems) = refs[-14:]
    tokens, chans = grad_ref.shape
    modes = rates_ref.shape[0]
    seg_len = tokens // SEGS
    lens_copy, *copies = load(
        [
            (lens_hbm, lens_ref), (rates_hbm, rates_ref), (residues_hbm, weight_ref),
            (skip_hbm, skip_ref), (seg_hbm, seg_ref),
        ]
        + [(ref, later_ref.at[k]) for k, ref in enumerate(later)]
        + pieces(grad_hbm, grad_ref),
        sems,
    )
    copies, grad_copies = copies[: 4 + len(later)], copies[4 + len(later) :]
    here = lax.axis_index("ctx")
    base = here * tokens
    lens_copy.wait()
    starts = doc_starts(lens_ref)
    store_cuts(cuts_ref, cut_codes(starts, [0] * len(starts), base, seg_len))
    for copy in copies:
        copy.wait()
    rates = rates_ref[...]
    decay_all = jnp.exp(-rates)
    decay_ref[...] = decay_all
    weight_ref[...] = weight_ref[...] * jnp.sqrt(1.0 - decay_all * decay_all)
    through = jnp.exp(-rates * float(tokens))
    arriving = jnp.zeros((modes, chans), F32)
    for k in range(len(later), 0, -1):
        kept = jnp.where(any_start(starts, (here + k) * tokens, tokens), 0.0, 1.0)
        arriving = later_ref[k - 1] + (through * kept) * arriving
    through = jnp.exp(-rates * float(seg_len))
    put_segment(arrive_ref, SEGS - 1, modes, arriving)
    for s in range(SEGS - 1, 0, -1):
        kept = jnp.where(any_start(starts, base + s * seg_len, seg_len), 0.0, 1.0)
        arriving = segment(seg_ref, s, modes) + (through * kept) * arriving
        put_segment(arrive_ref, s - 1, modes, arriving)
    arrive_copy = pltpu.make_async_copy(arrive_ref, arrive_hbm, sems.at[0])
    arrive_copy.start()
    widen(grad_ref, wide_ref, grad_copies)
    row = lax.broadcasted_iota(jnp.int32, (SEGS, LANES), 0)
    for h in range(chans // LANES):
        cols = slice(h * LANES, (h + 1) * LANES)
        decay = [spread(decay_ref, r, cols) for r in range(modes)]
        weight = [spread(weight_ref, r, cols) for r in range(modes)]
        skip = jnp.broadcast_to(skip_ref[:, cols], (SEGS, LANES))

        def step(i, state):
            rows = pl.ds(i, SEGS, stride=seg_len)
            grad = wide_ref[h, rows, :]
            back = tuple(grad + part for part in state)
            terms = [weight[r] * back[r] for r in range(modes)] + [skip * grad]
            while len(terms) > 1:
                terms = [a + b for a, b in zip(terms[::2], terms[1::2])] + terms[len(terms) // 2 * 2 :]
            wide_ref[h, rows, :] = terms[0]
            return tuple(decay[r] * back[r] for r in range(modes))

        def cut(place, stream, state):
            hold = row != place
            return tuple(jnp.where(hold, part, 0.0) for part in state)

        entry = tuple(arrive_ref[h, pl.ds(r, SEGS, stride=modes), :] for r in range(modes))
        time_loop(cuts_ref, seg_len, step, cut, entry)

    out_copies = []
    for k, (source, target) in enumerate(pieces(grad_ref, out_hbm)):
        size = target.shape[0]

        def narrow(j, _):
            rows = pl.ds(k * size + j * 32, 32)
            for h in range(wide_ref.shape[0]):
                grad_ref[rows, h * LANES : (h + 1) * LANES] = wide_ref[h, rows, :].astype(BF16)
            return 0

        lax.fori_loop(0, size // 32, narrow, 0)
        copy = pltpu.make_async_copy(source, target, sems.at[1 + k])
        copy.start()
        out_copies.append(copy)
    for copy in out_copies:
        copy.wait()
    arrive_copy.wait()


def back_pass(doc_lengths, rates, residues, skip, grad_out, seg_leaving, later):
    modes, chans = rates.shape
    tokens = grad_out.shape[0]
    kinds = state_scratch(doc_lengths.shape[0], modes, tokens, chans)
    kinds["skip"] = pltpu.VMEM((1, chans), F32)
    kinds["later"] = pltpu.VMEM((len(later), modes, chans), F32)
    names = ("lens", "mode", "mode", "skip", "narrow", "segs", "later", "segs", "wide", "mode", "cuts")
    return call(
        back_kernel,
        [
            jax.ShapeDtypeStruct((tokens, chans), BF16),
            jax.ShapeDtypeStruct((chans // LANES, SEGS * modes, LANES), F32),
        ],
        [kinds[k] for k in names],
        5 + len(later) + PIECES,
        "back_pass",
        cost(4 * tokens * chans * modes, 4 * tokens * chans),
        doc_lengths,
        rates,
        residues,
        skip,
        grad_out,
        seg_leaving,
        *later,
    )


def residue_kernel(
    window, lens_hbm, streams_hbm, rates_hbm, grad_hbm, x_hbm, arrive_hbm, out_hbm,
    lens_ref, streams_ref, rates_ref, grad_ref, x_ref, arrive_ref, out_ref,
    wide_ref, x_wide_ref, decay_ref, total_ref, cuts_ref, sems,
):
    tokens, chans = grad_ref.shape
    modes = rates_ref.shape[0]
    seg_len = tokens // SEGS
    copies = load(
        [
            (lens_hbm, lens_ref), (streams_hbm, streams_ref), (rates_hbm, rates_ref),
            (arrive_hbm, arrive_ref),
        ]
        + pieces(grad_hbm, grad_ref)
        + pieces(x_hbm, x_ref),
        sems,
    )
    base = lax.axis_index("ctx") * tokens
    for copy in copies[:4]:
        copy.wait()
    copies = copies[4:]
    starts = doc_starts(lens_ref)
    streams = [streams_ref[k] for k in range(len(starts) + 1)]
    store_cuts(cuts_ref, cut_codes(starts, streams[1:], base, seg_len))
    decay_all = jnp.exp(-rates_ref[...])
    decay_ref[...] = decay_all
    widen(grad_ref, wide_ref, copies[: len(copies) // 2])
    widen(x_ref, x_wide_ref, copies[len(copies) // 2 :])
    total_ref[...] = jnp.zeros_like(total_ref)
    row = lax.broadcasted_iota(jnp.int32, (SEGS, LANES), 0)
    first = base + row * seg_len
    stream_at = jnp.full((SEGS, LANES), streams[0], jnp.int32)
    for start, stream in zip(starts, streams[1:]):
        stream_at = jnp.where(first >= start, stream, stream_at)
    for h in range(chans // LANES):
        cols = slice(h * LANES, (h + 1) * LANES)
        decay = [spread(decay_ref, r, cols) for r in range(modes)]

        def step(i, carry):
            state, total = carry
            rows = pl.ds(i, SEGS, stride=seg_len)
            grad = wide_ref[h, rows, :]
            x = x_wide_ref[h, rows, :]
            back = tuple(grad + part for part in state)
            total = tuple(total[r] + x * back[r] for r in range(modes))
            return (tuple(decay[r] * back[r] for r in range(modes)), total)

        def cut(place, stream, carry):
            state, total = carry
            hold = row != place
            for r in range(modes):
                total_ref[stream, r, :, cols] += jnp.where(hold, 0.0, total[r])
            return (
                tuple(jnp.where(hold, part, 0.0) for part in state),
                tuple(jnp.where(hold, part, 0.0) for part in total),
            )

        zero = jnp.zeros((SEGS, LANES), F32)
        entry = tuple(arrive_ref[h, pl.ds(r, SEGS, stride=modes), :] for r in range(modes))
        _, total = time_loop(cuts_ref, seg_len, step, cut, (entry, (zero,) * modes))
        for s in range(2):
            for r in range(modes):
                total_ref[s, r, :, cols] += jnp.where(stream_at == s, total[r], 0.0)
    scale = jnp.sqrt(1.0 - decay_all * decay_all) / math.sqrt(window)
    for s in range(2):
        out_ref[s] = (jnp.sum(total_ref[s], axis=1) * scale).astype(BF16)
    for copy in load([(out_ref, out_hbm)], sems):
        copy.wait()


def residue_pass(doc_lengths, doc_streams, rates, grad_out, x_cols, arriving, window):
    modes, chans = rates.shape
    tokens = grad_out.shape[0]
    kinds = state_scratch(doc_lengths.shape[0], modes, tokens, chans)
    kinds["out"] = pltpu.VMEM((2, modes, chans), BF16)
    kinds["total"] = pltpu.VMEM((2, modes, SEGS, chans), F32)
    names = ("lens", "lens", "mode", "narrow", "narrow", "segs", "out", "wide", "wide", "mode", "total", "cuts")

    def kernel(*refs):
        residue_kernel(window, *refs)

    return call(
        kernel,
        [jax.ShapeDtypeStruct((2, modes, chans), BF16)],
        [kinds[k] for k in names],
        4 + 2 * (PIECES),
        "residue_pass",
        cost(4 * tokens * chans * modes, 4 * tokens * chans),
        doc_lengths,
        doc_streams,
        rates,
        grad_out,
        x_cols,
        arriving,
    )[0]


def from_later(value, axis):
    count = lax.axis_size(axis)
    return [
        lax.ppermute(value, axis, [(i + k, i) for i in range(count - k)]) for k in range(1, count)
    ]


def sum_over(value, axis):
    count = lax.axis_size(axis)
    parts = [value] + [
        lax.ppermute(value, axis, [(i, (i + k) % count) for i in range(count)]) for k in range(1, count)
    ]
    parts = [part.astype(F32) for part in parts]
    while len(parts) > 1:
        half = len(parts) // 2
        parts = [a + b for a, b in zip(parts[:half], parts[half:])]
    return parts[0]


def local(u_rows, gain, skip, residues, rates, grad_out, doc_lengths, doc_streams):
    ctx, groups = lax.axis_size("ctx"), lax.axis_size("ch")
    tokens, chans = grad_out.shape
    gain = gain[None, :]
    rates, residues = rates.T, residues.T
    x_send = norm_rows(u_rows, gain, groups)
    x_send, rates = lax.optimization_barrier((x_send, rates))
    x_cols = lax.all_to_all(x_send, "ch", split_axis=0, concat_axis=0, tiled=True)
    x_cols = x_cols.reshape(tokens, chans)
    seg_leaving, dev_leaving = leave(doc_lengths, rates, grad_out)
    later = from_later(dev_leaving, "ctx")
    normed_grad, arriving = back_pass(
        doc_lengths, rates, residues, skip[None, :], grad_out, seg_leaving, later
    )
    grad_rows = lax.all_to_all(
        normed_grad.reshape(groups, tokens // groups, chans), "ch", split_axis=0, concat_axis=0, tiled=True
    )
    parts = residue_pass(doc_lengths, doc_streams, rates, grad_out, x_cols, arriving, tokens * ctx)
    residue_grad = sum_over(parts, "ctx").transpose(0, 2, 1)
    input_grad = final_rows(u_rows, gain, grad_rows)
    return (input_grad, residue_grad)


def solution(mesh):
    return jax.shard_map(
        local,
        mesh=mesh,
        in_specs=(
            P(("ctx", "ch"), None),
            P(),
            P("ch"),
            P("ch", None),
            P("ch", None),
            P("ctx", "ch"),
            P(),
            P(),
        ),
        out_specs=(P(("ctx", "ch"), None), P(None, "ch", None)),
        check_vma=False,
    )
```

time: 87.3 us -> 81.3 us (0.931)
  the two profiles are of different devices: /device:TPU:1 before, /device:TPU:2 now
where the time goes in v2:
time: 81.3 us; the launch traced here: 80.6 us
  starting transfers between devices  39.4 us (48%)
  Pallas kernels  30 us (37%)
  waiting for transfers between devices  7.16 us (9%)
  local copies, waits for them, and re-layouts  2.57 us (3%)
  between operations  0.86 us (1%)
    pallas_call x5, Pallas kernels, call(): pl.pallas_call(kernel, in_specs=[pl.BlockSpec(memory_space=pl.ANY)] * len...  30 us
    ppermute x7, starting transfers between devices, sum_over(): lax.ppermute(value, axis, [(i, (i + k) % count) for i in range(count)])  15.3 us
    ppermute x7, starting transfers between devices, from_later(): lax.ppermute(value, axis, [(i + k, i) for i in range(count - k)])  9.03 us
    all_to_all x1, starting transfers between devices, local(): lax.all_to_all(x_send, 'ch', split_axis=0, concat_axis=0, tiled=True)  7.63 us
    all_to_all x1, starting transfers between devices, local(): lax.all_to_all(normed_grad.reshape(groups, tokens // groups, chans), 'ch'...  7.38 us
    ppermute x7, waiting for transfers between devices, from_later(): lax.ppermute(value, axis, [(i + k, i) for i in range(count - k)])  7.08 us
    unnamed x20, local copies, waits for them, and re-layouts  2.57 us
  transfers between devices with their start and end apart: 16, of which 5 were waited for; matrix products, arithmetic and copies ran while one was open for 0% of the time, Pallas kernels for 34%

profile of v2, /device:TPU:2, one launch (start us, length us, event | category | flops | bytes accessed | tf_op | source)
XLA Modules:
  0.0 80.6 jit_solution(14161044466224660843)
XLA Ops:
  0.6 2.5 %norm_rows.1 = bf16[32,64,256]{2,1,0:T(8,128)(2,1)} custom-call(bf16[64,8192]{1,0:T(8,128)(2,1)} %u_hbm.3, f32[1,8192]{1,0:T(1,128)} %bitcast.13), custom_call_target="tpu_custom_call" | custom-call | flops 4194304 | bytes 2097152 | tf_op jit(solution)/shard_map/norm_rows/pallas_call | solution.py:31
  3.2 7.6 %all-to-all-start.1 = ((bf16[32,64,256]{2,1,0:T(8,128)(2,1)}), bf16[32,64,256]{2,1,0:T(8,128)(2,1)S(1)}, u32[]{:S(2)}, u32[]{:S(2)}) async-start(bf16[32,64,256]{2,1,0:T(8,128)(2,1)} %norm_rows.1), calls=%async_computation.1 | async-start | bytes 2097152 | tf_op jit(solution)/shard_map/all_to_all | solution.py:563
  10.8 5.6 %leave.1 = (f32[2,128,128]{2,1,0:T(8,128)}, f32[16,256]{1,0:T(8,128)}) custom-call(s32[4]{0:T(128)} %refs_0_.1, f32[16,256]{1,0:T(8,128)} %bitcast.10, bf16[2048,256]{1,0:T(8,128)(2,1)} %refs_3_.1), custom_call_target="tpu_custom_call" | custom-call | flops 16777216 | bytes 1048576 | tf_op jit(solution)/shard_map/leave/pallas_call | solution.py:31
  16.4 1.3 %collective-permute-start.6 = (f32[16,256]{1,0:T(8,128)}, f32[16,256]{1,0:T(8,128)S(1)}, u32[]{:S(2)}, u32[]{:S(2)}) collective-permute-start(f32[16,256]{1,0:T(8,128)} %get-tuple-element.10), channel_id=1, source_target_pairs={{224,0},{225,1},{226,2},{227,3},{228,4},{229,5},{230,6},{231,7},{2... | collective-permute-start | bytes 49160 | tf_op jit(solution)/shard_map/ppermute | solution.py:540
  17.7 1.3 %collective-permute-start.5 = (f32[16,256]{1,0:T(8,128)}, f32[16,256]{1,0:T(8,128)S(1)}, u32[]{:S(2)}, u32[]{:S(2)}) collective-permute-start(f32[16,256]{1,0:T(8,128)} %get-tuple-element.10), channel_id=1, source_target_pairs={{192,0},{224,32},{193,1},{225,33},{194,2},{226,34},{195,3},{227,35... | collective-permute-start | bytes 49160 | tf_op jit(solution)/shard_map/ppermute | solution.py:540
  19.0 1.3 %collective-permute-start.4 = (f32[16,256]{1,0:T(8,128)}, f32[16,256]{1,0:T(8,128)S(1)}, u32[]{:S(2)}, u32[]{:S(2)}) collective-permute-start(f32[16,256]{1,0:T(8,128)} %get-tuple-element.10), channel_id=1, source_target_pairs={{160,0},{192,32},{224,64},{161,1},{193,33},{225,65},{162,2},{194,3... | collective-permute-start | bytes 49160 | tf_op jit(solution)/shard_map/ppermute | solution.py:540
  20.3 1.3 %collective-permute-start.3 = (f32[16,256]{1,0:T(8,128)}, f32[16,256]{1,0:T(8,128)S(1)}, u32[]{:S(2)}, u32[]{:S(2)}) collective-permute-start(f32[16,256]{1,0:T(8,128)} %get-tuple-element.10), channel_id=1, source_target_pairs={{128,0},{160,32},{192,64},{224,96},{129,1},{161,33},{193,65},{225,... | collective-permute-start | bytes 49160 | tf_op jit(solution)/shard_map/ppermute | solution.py:540
  21.6 1.3 %collective-permute-start.2 = (f32[16,256]{1,0:T(8,128)}, f32[16,256]{1,0:T(8,128)S(1)}, u32[]{:S(2)}, u32[]{:S(2)}) collective-permute-start(f32[16,256]{1,0:T(8,128)} %get-tuple-element.10), channel_id=1, source_target_pairs={{96,0},{128,32},{160,64},{192,96},{224,128},{97,1},{129,33},{161,6... | collective-permute-start | bytes 49160 | tf_op jit(solution)/shard_map/ppermute | solution.py:540
  22.9 2.6 %collective-permute-done.6.refs_6_ = f32[16,256]{1,0:T(8,128)S(1)} collective-permute-done((f32[16,256]{1,0:T(8,128)}, f32[16,256]{1,0:T(8,128)S(1)}, u32[]{:S(2)}, u32[]{:S(2)}) %collective-permute-start.6) | collective-permute-done | bytes 16416 | tf_op jit(solution)/shard_map/ppermute | solution.py:540
  25.5 0.0 copy-start.3
  25.5 1.3 %collective-permute-start.1 = (f32[16,256]{1,0:T(8,128)}, f32[16,256]{1,0:T(8,128)S(1)}, u32[]{:S(2)}, u32[]{:S(2)}) collective-permute-start(f32[16,256]{1,0:T(8,128)} %get-tuple-element.10), channel_id=1, source_target_pairs={{64,0},{96,32},{128,64},{160,96},{192,128},{224,160},{65,1},{97,33... | collective-permute-start | bytes 49160 | tf_op jit(solution)/shard_map/ppermute | solution.py:540
  26.7 0.0 collective-permute-done.5.refs_5_
  26.8 0.0 copy-start.4
  26.8 1.3 %collective-permute-start = (f32[16,256]{1,0:T(8,128)}, f32[16,256]{1,0:T(8,128)S(1)}, u32[]{:S(2)}, u32[]{:S(2)}) collective-permute-start(f32[16,256]{1,0:T(8,128)} %get-tuple-element.10), channel_id=1, source_target_pairs={{32,0},{64,32},{96,64},{128,96},{160,128},{192,160},{224,192},{33,... | collective-permute-start | bytes 49160 | tf_op jit(solution)/shard_map/ppermute | solution.py:540
  28.1 0.0 collective-permute-done.4.refs_4_
  28.1 0.0 copy-start.5
  28.1 2.0 %collective-permute-done.3.refs_3_ = f32[16,256]{1,0:T(8,128)S(1)} collective-permute-done((f32[16,256]{1,0:T(8,128)}, f32[16,256]{1,0:T(8,128)S(1)}, u32[]{:S(2)}, u32[]{:S(2)}) %collective-permute-start.3) | collective-permute-done | bytes 16416 | tf_op jit(solution)/shard_map/ppermute | solution.py:540
  30.0 0.0 copy-start.6
  30.1 0.0 collective-permute-done.2.refs_2_
  30.1 0.0 copy-start.7
  30.1 2.1 %collective-permute-done.1.refs_1_ = f32[16,256]{1,0:T(8,128)S(1)} collective-permute-done((f32[16,256]{1,0:T(8,128)}, f32[16,256]{1,0:T(8,128)S(1)}, u32[]{:S(2)}, u32[]{:S(2)}) %collective-permute-start.1) | collective-permute-done | bytes 16416 | tf_op jit(solution)/shard_map/ppermute | solution.py:540
  32.2 0.0 copy-start.8
  32.2 0.4 collective-permute-done.refs_0_
  32.6 0.0 copy-start.9
  32.6 0.0 copy-done.3
  32.6 0.0 copy-done.4
  32.6 0.0 copy-done.5
  32.6 0.0 copy-done.6
  32.6 0.0 copy-done.7
  32.6 0.1 copy-done.8
  32.8 0.4 copy-done.9
  33.2 9.0 %back_pass.1 = (bf16[2048,256]{1,0:T(8,128)(2,1)}, f32[2,128,128]{2,1,0:T(8,128)}) custom-call(s32[4]{0:T(128)} %refs_0_.1, f32[16,256]{1,0:T(8,128)} %bitcast.11, f32[16,256]{1,0:T(8,128)} %bitcast.15, f32[1,256]{1,0:T(1,128)} %bitcast.16, bf16[2048,256]{1,0:T(8,128)(2,1)} %refs_3_.1, f32[2,128,128]{2,1,0:T(8,128)} %get-tuple-element.9.seg_hbm, ...), custom_call_target="tpu_custom_call" | custom-call | flops 33554432 | bytes 2097152 | tf_op jit(solution)/shard_map/back_pass/pallas_call | solution.py:31
  42.3 0.0 all-to-all-done.1
  42.3 0.0 copy-start.1
  42.3 1.0 %copy-done.1 = bf16[32,64,256]{2,1,0:T(8,128)(2,1)} copy-done((bf16[32,64,256]{2,1,0:T(8,128)(2,1)}, bf16[32,64,256]{2,1,0:T(8,128)(2,1)S(1)}, u32[]{:S(2)}) %copy-start.1) | copy-done | bytes 1048600
  43.3 7.4 %all-to-all-start = ((bf16[32,64,256]{2,1,0:T(8,128)(2,1)}), bf16[32,64,256]{2,1,0:T(8,128)(2,1)S(1)}, u32[]{:S(2)}, u32[]{:S(2)}) async-start(bf16[32,64,256]{2,1,0:T(8,128)(2,1)} %bitcast.9), calls=%async_computation | async-start | bytes 2097152 | tf_op jit(solution)/shard_map/all_to_all | solution.py:570
  50.6 9.3 %residue_pass.1 = bf16[2,16,256]{2,1,0:T(8,128)(2,1)} custom-call(s32[4]{0:T(128)} %refs_0_.1, s32[4]{0:T(128)} %refs_1_.1, f32[16,256]{1,0:T(8,128)} %bitcast.12, bf16[2048,256]{1,0:T(8,128)(2,1)} %refs_3_.1, bf16[2048,256]{1,0:T(8,128)(2,1)} %bitcast.8, f32[2,128,128]{2,1,0:T(8,128)} %get-tuple-element.13.refs_5_), custom_call_target="tpu_custom_call" | custom-call | flops 33554432 | bytes 2097152 | tf_op jit(solution)/shard_map/residue_pass/pallas_call | solution.py:31
  60.0 0.0 copy-start.2
  60.0 4.2 %collective-permute-start.13 = (bf16[2,16,256]{2,1,0:T(8,128)(2,1)}, bf16[2,16,256]{2,1,0:T(8,128)(2,1)S(1)}, u32[]{:S(2)}, u32[]{:S(2)}) collective-permute-start(bf16[2,16,256]{2,1,0:T(8,128)(2,1)} %residue_pass.1), channel_id=1, source_target_pairs={{0,224},{32,0},{64,32},{96,64},{128,96},{160,128},{192,160},{224,1... | collective-permute-start | bytes 49160 | tf_op jit(solution)/shard_map/ppermute | solution.py:547
  64.2 1.4 %collective-permute-start.12 = (bf16[2,16,256]{2,1,0:T(8,128)(2,1)}, bf16[2,16,256]{2,1,0:T(8,128)(2,1)S(1)}, u32[]{:S(2)}, u32[]{:S(2)}) collective-permute-start(bf16[2,16,256]{2,1,0:T(8,128)(2,1)} %residue_pass.1), channel_id=1, source_target_pairs={{0,96},{32,128},{64,160},{96,192},{128,224},{160,0},{192,32},{224,... | collective-permute-start | bytes 49160 | tf_op jit(solution)/shard_map/ppermute | solution.py:547
  65.6 3.6 %collective-permute-start.11 = (bf16[2,16,256]{2,1,0:T(8,128)(2,1)}, bf16[2,16,256]{2,1,0:T(8,128)(2,1)S(1)}, u32[]{:S(2)}, u32[]{:S(2)}) collective-permute-start(bf16[2,16,256]{2,1,0:T(8,128)(2,1)} %residue_pass.1), channel_id=1, source_target_pairs={{0,160},{32,192},{64,224},{96,0},{128,32},{160,64},{192,96},{224,1... | collective-permute-start | bytes 49160 | tf_op jit(solution)/shard_map/ppermute | solution.py:547
  69.2 0.0 collective-permute-start.10
  69.2 2.5 %collective-permute-start.9 = (bf16[2,16,256]{2,1,0:T(8,128)(2,1)}, bf16[2,16,256]{2,1,0:T(8,128)(2,1)S(1)}, u32[]{:S(2)}, u32[]{:S(2)}) collective-permute-start(bf16[2,16,256]{2,1,0:T(8,128)(2,1)} %residue_pass.1), channel_id=1, source_target_pairs={{0,192},{32,224},{64,0},{96,32},{128,64},{160,96},{192,128},{224,1... | collective-permute-start | bytes 49160 | tf_op jit(solution)/shard_map/ppermute | solution.py:547
  71.8 0.0 collective-permute-done.13
  71.8 0.4 collective-permute-start.8
  72.1 0.0 collective-permute-done.12
  72.2 3.2 %collective-permute-start.7 = (bf16[2,16,256]{2,1,0:T(8,128)(2,1)}, bf16[2,16,256]{2,1,0:T(8,128)(2,1)S(1)}, u32[]{:S(2)}, u32[]{:S(2)}) collective-permute-start(bf16[2,16,256]{2,1,0:T(8,128)(2,1)} %residue_pass.1), channel_id=1, source_target_pairs={{0,128},{32,160},{64,192},{96,224},{128,0},{160,32},{192,64},{224,... | collective-permute-start | bytes 49160 | tf_op jit(solution)/shard_map/ppermute | solution.py:547
  75.4 0.0 all-to-all-done.grad_hbm
  75.4 0.0 copy-start
  75.4 1.0 %copy-done = bf16[32,64,256]{2,1,0:T(8,128)(2,1)} copy-done((bf16[32,64,256]{2,1,0:T(8,128)(2,1)}, bf16[32,64,256]{2,1,0:T(8,128)(2,1)S(1)}, u32[]{:S(2)}) %copy-start) | copy-done | bytes 1048600
  76.4 3.5 %final_rows.1 = bf16[64,8192]{1,0:T(8,128)(2,1)} custom-call(bf16[64,8192]{1,0:T(8,128)(2,1)} %u_hbm.3, f32[1,8192]{1,0:T(1,128)} %bitcast.14, bf16[32,64,256]{2,1,0:T(8,128)(2,1)} %copy-done), custom_call_target="tpu_custom_call" | custom-call | flops 8388608 | bytes 3145728 | tf_op jit(solution)/shard_map/final_rows/pallas_call | solution.py:31
  79.9 0.0 collective-permute-done.11
  79.9 0.0 collective-permute-done.10
  79.9 0.0 collective-permute-done.9
  79.9 0.0 collective-permute-done.8
  80.0 0.1 collective-permute-done.7
  80.0 0.0 copy-done.2
  80.0 0.6 add_bitcast_fusion
Async XLA Ops:
  3.2 39.1 %all-to-all-start.1 = ((bf16[32,64,256]{2,1,0:T(8,128)(2,1)}), bf16[32,64,256]{2,1,0:T(8,128)(2,1)S(1)}, u32[]{:S(2)}, u32[]{:S(2)}) async-start(bf16[32,64,256]{2,1,0:T(8,128)(2,1)} %norm_rows.1), calls=%async_computation.1 | async-start | bytes 2097152 | tf_op jit(solution)/shard_map/all_to_all | solution.py:563
  16.4 9.1 %collective-permute-start.6 = (f32[16,256]{1,0:T(8,128)}, f32[16,256]{1,0:T(8,128)S(1)}, u32[]{:S(2)}, u32[]{:S(2)}) collective-permute-start(f32[16,256]{1,0:T(8,128)} %get-tuple-element.10), channel_id=1, source_target_pairs={{224,0},{225,1},{226,2},{227,3},{228,4},{229,5},{230,6},{231,7},{2... | collective-permute-start | bytes 49160 | tf_op jit(solution)/shard_map/ppermute | solution.py:540
  17.7 9.1 %collective-permute-start.5 = (f32[16,256]{1,0:T(8,128)}, f32[16,256]{1,0:T(8,128)S(1)}, u32[]{:S(2)}, u32[]{:S(2)}) collective-permute-start(f32[16,256]{1,0:T(8,128)} %get-tuple-element.10), channel_id=1, source_target_pairs={{192,0},{224,32},{193,1},{225,33},{194,2},{226,34},{195,3},{227,35... | collective-permute-start | bytes 49160 | tf_op jit(solution)/shard_map/ppermute | solution.py:540
  19.0 9.1 %collective-permute-start.4 = (f32[16,256]{1,0:T(8,128)}, f32[16,256]{1,0:T(8,128)S(1)}, u32[]{:S(2)}, u32[]{:S(2)}) collective-permute-start(f32[16,256]{1,0:T(8,128)} %get-tuple-element.10), channel_id=1, source_target_pairs={{160,0},{192,32},{224,64},{161,1},{193,33},{225,65},{162,2},{194,3... | collective-permute-start | bytes 49160 | tf_op jit(solution)/shard_map/ppermute | solution.py:540
  20.3 9.8 %collective-permute-start.3 = (f32[16,256]{1,0:T(8,128)}, f32[16,256]{1,0:T(8,128)S(1)}, u32[]{:S(2)}, u32[]{:S(2)}) collective-permute-start(f32[16,256]{1,0:T(8,128)} %get-tuple-element.10), channel_id=1, source_target_pairs={{128,0},{160,32},{192,64},{224,96},{129,1},{161,33},{193,65},{225,... | collective-permute-start | bytes 49160 | tf_op jit(solution)/shard_map/ppermute | solution.py:540
  21.6 8.5 %collective-permute-start.2 = (f32[16,256]{1,0:T(8,128)}, f32[16,256]{1,0:T(8,128)S(1)}, u32[]{:S(2)}, u32[]{:S(2)}) collective-permute-start(f32[16,256]{1,0:T(8,128)} %get-tuple-element.10), channel_id=1, source_target_pairs={{96,0},{128,32},{160,64},{192,96},{224,128},{97,1},{129,33},{161,6... | collective-permute-start | bytes 49160 | tf_op jit(solution)/shard_map/ppermute | solution.py:540
  25.5 7.2 %copy-start.3 = (f32[16,256]{1,0:T(8,128)}, f32[16,256]{1,0:T(8,128)S(1)}, u32[]{:S(2)}) copy-start(f32[16,256]{1,0:T(8,128)S(1)} %collective-permute-done.6.refs_6_) | copy-start | bytes 49156
  25.5 6.7 %collective-permute-start.1 = (f32[16,256]{1,0:T(8,128)}, f32[16,256]{1,0:T(8,128)S(1)}, u32[]{:S(2)}, u32[]{:S(2)}) collective-permute-start(f32[16,256]{1,0:T(8,128)} %get-tuple-element.10), channel_id=1, source_target_pairs={{64,0},{96,32},{128,64},{160,96},{192,128},{224,160},{65,1},{97,33... | collective-permute-start | bytes 49160 | tf_op jit(solution)/shard_map/ppermute | solution.py:540
  26.8 5.9 %copy-start.4 = (f32[16,256]{1,0:T(8,128)}, f32[16,256]{1,0:T(8,128)S(1)}, u32[]{:S(2)}) copy-start(f32[16,256]{1,0:T(8,128)S(1)} %collective-permute-done.5.refs_5_) | copy-start | bytes 49156
  26.8 5.8 %collective-permute-start = (f32[16,256]{1,0:T(8,128)}, f32[16,256]{1,0:T(8,128)S(1)}, u32[]{:S(2)}, u32[]{:S(2)}) collective-permute-start(f32[16,256]{1,0:T(8,128)} %get-tuple-element.10), channel_id=1, source_target_pairs={{32,0},{64,32},{96,64},{128,96},{160,128},{192,160},{224,192},{33,... | collective-permute-start | bytes 49160 | tf_op jit(solution)/shard_map/ppermute | solution.py:540
  28.1 4.5 %copy-start.5 = (f32[16,256]{1,0:T(8,128)}, f32[16,256]{1,0:T(8,128)S(1)}, u32[]{:S(2)}) copy-start(f32[16,256]{1,0:T(8,128)S(1)} %collective-permute-done.4.refs_4_) | copy-start | bytes 49156
  30.0 2.6 %copy-start.6 = (f32[16,256]{1,0:T(8,128)}, f32[16,256]{1,0:T(8,128)S(1)}, u32[]{:S(2)}) copy-start(f32[16,256]{1,0:T(8,128)S(1)} %collective-permute-done.3.refs_3_) | copy-start | bytes 49156
  30.1 2.6 %copy-start.7 = (f32[16,256]{1,0:T(8,128)}, f32[16,256]{1,0:T(8,128)S(1)}, u32[]{:S(2)}) copy-start(f32[16,256]{1,0:T(8,128)S(1)} %collective-permute-done.2.refs_2_) | copy-start | bytes 49156
  32.2 0.6 copy-start.8
  32.6 0.6 copy-start.9
  42.3 1.0 %copy-start.1 = (bf16[32,64,256]{2,1,0:T(8,128)(2,1)}, bf16[32,64,256]{2,1,0:T(8,128)(2,1)S(1)}, u32[]{:S(2)}) copy-start(bf16[32,64,256]{2,1,0:T(8,128)(2,1)S(1)} %all-to-all-done.1) | copy-start | bytes 3145732
  43.3 32.1 %all-to-all-start = ((bf16[32,64,256]{2,1,0:T(8,128)(2,1)}), bf16[32,64,256]{2,1,0:T(8,128)(2,1)S(1)}, u32[]{:S(2)}, u32[]{:S(2)}) async-start(bf16[32,64,256]{2,1,0:T(8,128)(2,1)} %bitcast.9), calls=%async_computation | async-start | bytes 2097152 | tf_op jit(solution)/shard_map/all_to_all | solution.py:570
  60.0 20.0 %copy-start.2 = (bf16[2,16,256]{2,1,0:T(8,128)(2,1)S(1)}, bf16[2,16,256]{2,1,0:T(8,128)(2,1)}, u32[]{:S(2)}) copy-start(bf16[2,16,256]{2,1,0:T(8,128)(2,1)} %residue_pass.1) | copy-start | bytes 49156
  60.0 11.8 %collective-permute-start.13 = (bf16[2,16,256]{2,1,0:T(8,128)(2,1)}, bf16[2,16,256]{2,1,0:T(8,128)(2,1)S(1)}, u32[]{:S(2)}, u32[]{:S(2)}) collective-permute-start(bf16[2,16,256]{2,1,0:T(8,128)(2,1)} %residue_pass.1), channel_id=1, source_target_pairs={{0,224},{32,0},{64,32},{96,64},{128,96},{160,128},{192,160},{224,1... | collective-permute-start | bytes 49160 | tf_op jit(solution)/shard_map/ppermute | solution.py:547
  64.2 8.0 %collective-permute-start.12 = (bf16[2,16,256]{2,1,0:T(8,128)(2,1)}, bf16[2,16,256]{2,1,0:T(8,128)(2,1)S(1)}, u32[]{:S(2)}, u32[]{:S(2)}) collective-permute-start(bf16[2,16,256]{2,1,0:T(8,128)(2,1)} %residue_pass.1), channel_id=1, source_target_pairs={{0,96},{32,128},{64,160},{96,192},{128,224},{160,0},{192,32},{224,... | collective-permute-start | bytes 49160 | tf_op jit(solution)/shard_map/ppermute | solution.py:547
  65.6 14.3 %collective-permute-start.11 = (bf16[2,16,256]{2,1,0:T(8,128)(2,1)}, bf16[2,16,256]{2,1,0:T(8,128)(2,1)S(1)}, u32[]{:S(2)}, u32[]{:S(2)}) collective-permute-start(bf16[2,16,256]{2,1,0:T(8,128)(2,1)} %residue_pass.1), channel_id=1, source_target_pairs={{0,160},{32,192},{64,224},{96,0},{128,32},{160,64},{192,96},{224,1... | collective-permute-start | bytes 49160 | tf_op jit(solution)/shard_map/ppermute | solution.py:547
  69.2 10.7 %collective-permute-start.10 = (bf16[2,16,256]{2,1,0:T(8,128)(2,1)}, bf16[2,16,256]{2,1,0:T(8,128)(2,1)S(1)}, u32[]{:S(2)}, u32[]{:S(2)}) collective-permute-start(bf16[2,16,256]{2,1,0:T(8,128)(2,1)} %residue_pass.1), channel_id=1, source_target_pairs={{0,32},{32,64},{64,96},{96,128},{128,160},{160,192},{192,224},{224... | collective-permute-start | bytes 49160 | tf_op jit(solution)/shard_map/ppermute | solution.py:547
  69.2 10.7 %collective-permute-start.9 = (bf16[2,16,256]{2,1,0:T(8,128)(2,1)}, bf16[2,16,256]{2,1,0:T(8,128)(2,1)S(1)}, u32[]{:S(2)}, u32[]{:S(2)}) collective-permute-start(bf16[2,16,256]{2,1,0:T(8,128)(2,1)} %residue_pass.1), channel_id=1, source_target_pairs={{0,192},{32,224},{64,0},{96,32},{128,64},{160,96},{192,128},{224,1... | collective-permute-start | bytes 49160 | tf_op jit(solution)/shard_map/ppermute | solution.py:547
  71.8 8.2 %collective-permute-start.8 = (bf16[2,16,256]{2,1,0:T(8,128)(2,1)}, bf16[2,16,256]{2,1,0:T(8,128)(2,1)S(1)}, u32[]{:S(2)}, u32[]{:S(2)}) collective-permute-start(bf16[2,16,256]{2,1,0:T(8,128)(2,1)} %residue_pass.1), channel_id=1, source_target_pairs={{0,64},{32,96},{64,128},{96,160},{128,192},{160,224},{192,0},{224,... | collective-permute-start | bytes 49160 | tf_op jit(solution)/shard_map/ppermute | solution.py:547
  72.2 7.9 %collective-permute-start.7 = (bf16[2,16,256]{2,1,0:T(8,128)(2,1)}, bf16[2,16,256]{2,1,0:T(8,128)(2,1)S(1)}, u32[]{:S(2)}, u32[]{:S(2)}) collective-permute-start(bf16[2,16,256]{2,1,0:T(8,128)(2,1)} %residue_pass.1), channel_id=1, source_target_pairs={{0,128},{32,160},{64,192},{96,224},{128,0},{160,32},{192,64},{224,... | collective-permute-start | bytes 49160 | tf_op jit(solution)/shard_map/ppermute | solution.py:547
  75.4 1.0 %copy-start = (bf16[32,64,256]{2,1,0:T(8,128)(2,1)}, bf16[32,64,256]{2,1,0:T(8,128)(2,1)S(1)}, u32[]{:S(2)}) copy-start(bf16[32,64,256]{2,1,0:T(8,128)(2,1)S(1)} %all-to-all-done.grad_hbm) | copy-start | bytes 3145732

commit v3 on v2

--- a/solution.py
+++ b/solution.py
@@ -13,6 +13,7 @@
 LANES = 128
 UNROLL = 8
 PIECES = 4
+CHUNK = 256
 ROW_BLOCK = 16
 
 
@@ -27,10 +28,12 @@
     return copies
 
 
-def call(kernel, outs, scratch, sems, name, estimate, *operands):
+def call(kernel, outs, scratch, sems, name, estimate, near, *operands):
     return pl.pallas_call(
         kernel,
-        in_specs=[pl.BlockSpec(memory_space=pl.ANY)] * len(operands),
+        in_specs=[
+            pl.BlockSpec(memory_space=pltpu.VMEM if k in near else pl.ANY) for k in range(len(operands))
+        ],
         out_specs=[pl.BlockSpec(memory_space=pl.ANY)] * len(outs),
         out_shape=outs,
         scratch_shapes=scratch + [pltpu.SemaphoreType.DMA((sems,))],
@@ -85,19 +88,20 @@
         1 + 2 * blocks,
         "norm_rows",
         cost(8 * rows * width, 4 * rows * width),
+        (),
         u_rows,
         gain,
     )[0]
 
 
-def final_kernel(u_hbm, gain_hbm, grad_hbm, out_hbm, u_ref, gain_ref, grad_ref, out_ref, sems):
-    blocks, groups, rows, chans = grad_ref.shape
+def final_kernel(u_hbm, gain_hbm, grad_ref, out_hbm, u_ref, gain_ref, out_ref, sems):
+    blocks, rows, _ = u_ref.shape
+    groups, _, chans = grad_ref.shape
     width = groups * chans
     span = [pl.ds(b * rows, rows) for b in range(blocks)]
     gain_copy, *copies = load(
         [(gain_hbm, gain_ref)]
-        + [(u_hbm.at[span[b]], u_ref.at[b]) for b in range(blocks)]
-        + [(grad_hbm.at[:, span[b]], grad_ref.at[b]) for b in range(blocks)],
+        + [(u_hbm.at[span[b]], u_ref.at[b]) for b in range(blocks)],
         sems,
     )
     gain_copy.wait()
@@ -105,19 +109,18 @@
     for b in range(blocks):
         copies[b].wait()
         inv = inverse_rms(u_ref.at[b])
-        copies[blocks + b].wait()
         total = jnp.zeros((rows, chans), F32)
         for c in range(groups):
             cols = slice(c * chans, (c + 1) * chans)
             normal = u_ref[b, :, cols].astype(F32) * inv
-            total = total + normal * (gain_ref[:, cols] * grad_ref[b, c].astype(F32))
+            total = total + normal * (gain_ref[:, cols] * grad_ref[c, span[b], :].astype(F32))
         project = jnp.sum(total, axis=1, keepdims=True) / width
         for c in range(groups):
             cols = slice(c * chans, (c + 1) * chans)
             normal = u_ref[b, :, cols].astype(F32) * inv
-            scaled = gain_ref[:, cols] * grad_ref[b, c].astype(F32)
+            scaled = gain_ref[:, cols] * grad_ref[c, span[b], :].astype(F32)
             out_ref[b, :, cols] = (inv * (scaled - normal * project)).astype(BF16)
-        copy = pltpu.make_async_copy(out_ref.at[b], out_hbm.at[span[b]], sems.at[1 + 2 * blocks + b])
+        copy = pltpu.make_async_copy(out_ref.at[b], out_hbm.at[span[b]], sems.at[1 + blocks + b])
         copy.start()
         out_copies.append(copy)
     for copy in out_copies:
@@ -134,12 +137,12 @@
         [
             pltpu.VMEM((blocks, ROW_BLOCK, width), BF16),
             pltpu.VMEM((1, width), F32),
-            pltpu.VMEM((blocks, groups, ROW_BLOCK, chans), BF16),
             pltpu.VMEM((blocks, ROW_BLOCK, width), BF16),
         ],
-        1 + 3 * blocks,
+        1 + 2 * blocks,
         "final_rows",
         cost(16 * rows * width, 6 * rows * width),
+        (2,),
         u_rows,
         gain,
         grad_rows,
@@ -212,11 +215,13 @@
     return [(source_ref.at[rows], target_ref.at[rows]) for rows in spans]
 
 
-def widen(source_ref, target_ref, copies, chunk=32):
+def widen(source_ref, target_ref, copies):
     halves, tokens, _ = target_ref.shape
-    size = tokens // len(copies)
-    for k, copy in enumerate(copies):
-        copy.wait()
+    size = tokens // max(len(copies), 1)
+    chunk = min(CHUNK, size)
+    for k in range(tokens // size):
+        if copies:
+            copies[k].wait()
 
         def body(j, _):
             rows = pl.ds(k * size + j * chunk, chunk)
@@ -317,6 +322,7 @@
         2 + PIECES,
         "leave",
         cost(2 * tokens * chans * modes, 2 * tokens * chans),
+        (),
         doc_lengths,
         rates,
         grad_out,
@@ -327,8 +333,8 @@
     lens_hbm, rates_hbm, residues_hbm, skip_hbm, grad_hbm, seg_hbm, *refs,
 ):
     later = refs[: -14]
-    (out_hbm, arrive_hbm, lens_ref, rates_ref, weight_ref, skip_ref, grad_ref, seg_ref, later_ref,
-     arrive_ref, wide_ref, decay_ref, cuts_ref, sems) = refs[-14:]
+    (out_hbm, arrive_hbm, lens_ref, rates_ref, weight_ref, skip_ref, grad_ref, seg_ref,
+     arrive_ref, wide_ref, conv_ref, decay_ref, cuts_ref, sems) = refs[-14:]
     tokens, chans = grad_ref.shape
     modes = rates_ref.shape[0]
     seg_len = tokens // SEGS
@@ -337,11 +343,10 @@
             (lens_hbm, lens_ref), (rates_hbm, rates_ref), (residues_hbm, weight_ref),
             (skip_hbm, skip_ref), (seg_hbm, seg_ref),
         ]
-        + [(ref, later_ref.at[k]) for k, ref in enumerate(later)]
         + pieces(grad_hbm, grad_ref),
         sems,
     )
-    copies, grad_copies = copies[: 4 + len(later)], copies[4 + len(later) :]
+    copies, grad_copies = copies[:4], copies[4:]
     here = lax.axis_index("ctx")
     base = here * tokens
     lens_copy.wait()
@@ -357,7 +362,7 @@
     arriving = jnp.zeros((modes, chans), F32)
     for k in range(len(later), 0, -1):
         kept = jnp.where(any_start(starts, (here + k) * tokens, tokens), 0.0, 1.0)
-        arriving = later_ref[k - 1] + (through * kept) * arriving
+        arriving = later[k - 1][...] + (through * kept) * arriving
     through = jnp.exp(-rates * float(seg_len))
     put_segment(arrive_ref, SEGS - 1, modes, arriving)
     for s in range(SEGS - 1, 0, -1):
@@ -381,7 +386,7 @@
             terms = [weight[r] * back[r] for r in range(modes)] + [skip * grad]
             while len(terms) > 1:
                 terms = [a + b for a, b in zip(terms[::2], terms[1::2])] + terms[len(terms) // 2 * 2 :]
-            wide_ref[h, rows, :] = terms[0]
+            conv_ref[h, rows, :] = terms[0]
             return tuple(decay[r] * back[r] for r in range(modes))
 
         def cut(place, stream, state):
@@ -394,14 +399,15 @@
     out_copies = []
     for k, (source, target) in enumerate(pieces(grad_ref, out_hbm)):
         size = target.shape[0]
+        chunk = min(CHUNK, size)
 
         def narrow(j, _):
-            rows = pl.ds(k * size + j * 32, 32)
-            for h in range(wide_ref.shape[0]):
-                grad_ref[rows, h * LANES : (h + 1) * LANES] = wide_ref[h, rows, :].astype(BF16)
+            rows = pl.ds(k * size + j * chunk, chunk)
+            for h in range(conv_ref.shape[0]):
+                grad_ref[rows, h * LANES : (h + 1) * LANES] = conv_ref[h, rows, :].astype(BF16)
             return 0
 
-        lax.fori_loop(0, size // 32, narrow, 0)
+        lax.fori_loop(0, size // chunk, narrow, 0)
         copy = pltpu.make_async_copy(source, target, sems.at[1 + k])
         copy.start()
         out_copies.append(copy)
@@ -415,8 +421,7 @@
     tokens = grad_out.shape[0]
     kinds = state_scratch(doc_lengths.shape[0], modes, tokens, chans)
     kinds["skip"] = pltpu.VMEM((1, chans), F32)
-    kinds["later"] = pltpu.VMEM((len(later), modes, chans), F32)
-    names = ("lens", "mode", "mode", "skip", "narrow", "segs", "later", "segs", "wide", "mode", "cuts")
+    names = ("lens", "mode", "mode", "skip", "narrow", "segs", "segs", "wide", "wide", "mode", "cuts")
     return call(
         back_kernel,
         [
@@ -424,9 +429,10 @@
             jax.ShapeDtypeStruct((chans // LANES, SEGS * modes, LANES), F32),
         ],
         [kinds[k] for k in names],
-        5 + len(later) + PIECES,
+        5 + PIECES,
         "back_pass",
         cost(4 * tokens * chans * modes, 4 * tokens * chans),
+        range(6, 6 + len(later)),
         doc_lengths,
         rates,
         residues,
@@ -438,8 +444,8 @@
 
 
 def residue_kernel(
-    window, lens_hbm, streams_hbm, rates_hbm, grad_hbm, x_hbm, arrive_hbm, out_hbm,
-    lens_ref, streams_ref, rates_ref, grad_ref, x_ref, arrive_ref, out_ref,
+    window, lens_hbm, streams_hbm, rates_hbm, grad_hbm, x_ref, arrive_hbm, out_hbm,
+    lens_ref, streams_ref, rates_ref, grad_ref, arrive_ref, out_ref,
     wide_ref, x_wide_ref, decay_ref, total_ref, cuts_ref, sems,
 ):
     tokens, chans = grad_ref.shape
@@ -450,8 +456,7 @@
             (lens_hbm, lens_ref), (streams_hbm, streams_ref), (rates_hbm, rates_ref),
             (arrive_hbm, arrive_ref),
         ]
-        + pieces(grad_hbm, grad_ref)
-        + pieces(x_hbm, x_ref),
+        + pieces(grad_hbm, grad_ref),
         sems,
     )
     base = lax.axis_index("ctx") * tokens
@@ -463,8 +468,8 @@
     store_cuts(cuts_ref, cut_codes(starts, streams[1:], base, seg_len))
     decay_all = jnp.exp(-rates_ref[...])
     decay_ref[...] = decay_all
-    widen(grad_ref, wide_ref, copies[: len(copies) // 2])
-    widen(x_ref, x_wide_ref, copies[len(copies) // 2 :])
+    widen(x_ref, x_wide_ref, ())
+    widen(grad_ref, wide_ref, copies)
     total_ref[...] = jnp.zeros_like(total_ref)
     row = lax.broadcasted_iota(jnp.int32, (SEGS, LANES), 0)
     first = base + row * seg_len
@@ -513,7 +518,7 @@
     kinds = state_scratch(doc_lengths.shape[0], modes, tokens, chans)
     kinds["out"] = pltpu.VMEM((2, modes, chans), BF16)
     kinds["total"] = pltpu.VMEM((2, modes, SEGS, chans), F32)
-    names = ("lens", "lens", "mode", "narrow", "narrow", "segs", "out", "wide", "wide", "mode", "total", "cuts")
+    names = ("lens", "lens", "mode", "narrow", "segs", "out", "wide", "wide", "mode", "total", "cuts")
 
     def kernel(*refs):
         residue_kernel(window, *refs)
@@ -522,9 +527,10 @@
         kernel,
         [jax.ShapeDtypeStruct((2, modes, chans), BF16)],
         [kinds[k] for k in names],
-        4 + 2 * (PIECES),
+        4 + PIECES,
         "residue_pass",
         cost(4 * tokens * chans * modes, 4 * tokens * chans),
+        (4,),
         doc_lengths,
         doc_streams,
         rates,
@@ -537,20 +543,24 @@
 def from_later(value, axis):
     count = lax.axis_size(axis)
     return [
-        lax.ppermute(value, axis, [(i + k, i) for i in range(count - k)]) for k in range(1, count)
+        lax.ppermute(value, axis, [(i + k, i) for i in range(count - k)])
+        for k in range(1, max(2, count // 2 + 1))
     ]
 
 
 def sum_over(value, axis):
     count = lax.axis_size(axis)
+    half = count // 2
     parts = [value] + [
-        lax.ppermute(value, axis, [(i, (i + k) % count) for i in range(count)]) for k in range(1, count)
+        lax.ppermute(value, axis, [(i, i // half * half + (i + k) % half) for i in range(count)])
+        for k in range(1, half)
     ]
     parts = [part.astype(F32) for part in parts]
     while len(parts) > 1:
-        half = len(parts) // 2
-        parts = [a + b for a, b in zip(parts[:half], parts[half:])]
-    return parts[0]
+        middle = len(parts) // 2
+        parts = [a + b for a, b in zip(parts[:middle], parts[middle:])]
+    other = lax.ppermute(parts[0], axis, [(i, (i + half) % count) for i in range(count)])
+    return parts[0] + other
 
 
 def local(u_rows, gain, skip, residues, rates, grad_out, doc_lengths, doc_streams):

time: 81.3 us -> 78.5 us (0.966)
  the two profiles are of different devices: /device:TPU:2 before, /device:TPU:1 now
where the time goes in v3:
time: 78.5 us; the launch traced here: 77.3 us
  Pallas kernels  32.3 us (41%)
  starting transfers between devices  31.5 us (40%)
  waiting for transfers between devices  8.75 us (11%)
  local copies, waits for them, and re-layouts  2.55 us (3%)
  other arithmetic  1.35 us (2%)
    pallas_call x5, Pallas kernels, call(): pl.pallas_call(kernel, in_specs=[pl.BlockSpec(memory_space=pltpu.VMEM if...  32.3 us
    all_to_all x1, starting transfers between devices, local(): lax.all_to_all(x_send, 'ch', split_axis=0, concat_axis=0, tiled=True)  8.6 us
    all_to_all x1, starting transfers between devices, local(): lax.all_to_all(normed_grad.reshape(groups, tokens // groups, chans), 'ch'...  7.96 us
    ppermute x3, starting transfers between devices, sum_over(): lax.ppermute(value, axis, [(i, i // half * half + (i + k) % half) for i i...  6.67 us
    ppermute x4, starting transfers between devices, from_later(): lax.ppermute(value, axis, [(i + k, i) for i in range(count - k)])  5.17 us
    ppermute x4, waiting for transfers between devices, from_later(): lax.ppermute(value, axis, [(i + k, i) for i in range(count - k)])  4.51 us
    ppermute x3, waiting for transfers between devices, sum_over(): lax.ppermute(value, axis, [(i, i // half * half + (i + k) % half) for i i...  4.23 us
    ppermute x1, starting transfers between devices, sum_over(): lax.ppermute(parts[0], axis, [(i, (i + half) % count) for i in range(coun...  3.12 us
  transfers between devices with their start and end apart: 10, of which 3 were waited for; matrix products, arithmetic and copies ran while one was open for 1% of the time, Pallas kernels for 38%

profile of v3, /device:TPU:1, one launch (start us, length us, event | category | flops | bytes accessed | tf_op | source)
XLA Modules:
  0.0 77.3 jit_solution(14268605497103384182)
XLA Ops:
  0.6 2.6 %norm_rows.1 = bf16[32,64,256]{2,1,0:T(8,128)(2,1)} custom-call(bf16[64,8192]{1,0:T(8,128)(2,1)} %u_hbm.3, f32[1,8192]{1,0:T(1,128)} %bitcast.13), custom_call_target="tpu_custom_call" | custom-call | flops 4194304 | bytes 2097152 | tf_op jit(solution)/shard_map/norm_rows/pallas_call | solution.py:32
  3.2 8.6 %all-to-all-start.1 = ((bf16[32,64,256]{2,1,0:T(8,128)(2,1)}), bf16[32,64,256]{2,1,0:T(8,128)(2,1)S(1)}, u32[]{:S(2)}, u32[]{:S(2)}) async-start(bf16[32,64,256]{2,1,0:T(8,128)(2,1)} %norm_rows.1), calls=%async_computation.1 | async-start | bytes 2097152 | tf_op jit(solution)/shard_map/all_to_all | solution.py:573
  11.8 5.6 %leave.1 = (f32[2,128,128]{2,1,0:T(8,128)}, f32[16,256]{1,0:T(8,128)}) custom-call(s32[4]{0:T(128)} %refs_0_.1, f32[16,256]{1,0:T(8,128)} %bitcast.10, bf16[2048,256]{1,0:T(8,128)(2,1)} %refs_3_.1), custom_call_target="tpu_custom_call" | custom-call | flops 16777216 | bytes 1048576 | tf_op jit(solution)/shard_map/leave/pallas_call | solution.py:32
  17.4 1.3 %collective-permute-start.3 = (f32[16,256]{1,0:T(8,128)}, f32[16,256]{1,0:T(8,128)S(1)}, u32[]{:S(2)}, u32[]{:S(2)}) collective-permute-start(f32[16,256]{1,0:T(8,128)} %get-tuple-element.10), channel_id=1, source_target_pairs={{128,0},{160,32},{192,64},{224,96},{129,1},{161,33},{193,65},{225,... | collective-permute-start | bytes 49160 | tf_op jit(solution)/shard_map/ppermute | solution.py:546
  18.7 1.3 %collective-permute-start.2 = (f32[16,256]{1,0:T(8,128)}, f32[16,256]{1,0:T(8,128)S(1)}, u32[]{:S(2)}, u32[]{:S(2)}) collective-permute-start(f32[16,256]{1,0:T(8,128)} %get-tuple-element.10), channel_id=1, source_target_pairs={{96,0},{128,32},{160,64},{192,96},{224,128},{97,1},{129,33},{161,6... | collective-permute-start | bytes 49160 | tf_op jit(solution)/shard_map/ppermute | solution.py:546
  20.0 1.3 %collective-permute-start.1 = (f32[16,256]{1,0:T(8,128)}, f32[16,256]{1,0:T(8,128)S(1)}, u32[]{:S(2)}, u32[]{:S(2)}) collective-permute-start(f32[16,256]{1,0:T(8,128)} %get-tuple-element.10), channel_id=1, source_target_pairs={{64,0},{96,32},{128,64},{160,96},{192,128},{224,160},{65,1},{97,33... | collective-permute-start | bytes 49160 | tf_op jit(solution)/shard_map/ppermute | solution.py:546
  21.3 1.3 %collective-permute-start = (f32[16,256]{1,0:T(8,128)}, f32[16,256]{1,0:T(8,128)S(1)}, u32[]{:S(2)}, u32[]{:S(2)}) collective-permute-start(f32[16,256]{1,0:T(8,128)} %get-tuple-element.10), channel_id=1, source_target_pairs={{32,0},{64,32},{96,64},{128,96},{160,128},{192,160},{224,192},{33,... | collective-permute-start | bytes 49160 | tf_op jit(solution)/shard_map/ppermute | solution.py:546
  22.6 4.5 %collective-permute-done.3.refs_3_ = f32[16,256]{1,0:T(8,128)S(1)} collective-permute-done((f32[16,256]{1,0:T(8,128)}, f32[16,256]{1,0:T(8,128)S(1)}, u32[]{:S(2)}, u32[]{:S(2)}) %collective-permute-start.3) | collective-permute-done | bytes 16416 | tf_op jit(solution)/shard_map/ppermute | solution.py:546
  27.1 0.0 copy-start.2
  27.1 0.0 collective-permute-done.2.refs_2_
  27.1 0.0 copy-start.3
  27.1 0.0 collective-permute-done.1.refs_1_
  27.1 0.0 copy-start.4
  27.1 0.0 collective-permute-done.refs_0_
  27.1 0.0 copy-start.5
  27.1 0.6 copy-done.2
  27.7 0.0 copy-done.3
  27.7 0.0 copy-done.4
  27.7 0.0 copy-done.5
  27.7 9.6 %back_pass.1 = (bf16[2048,256]{1,0:T(8,128)(2,1)}, f32[2,128,128]{2,1,0:T(8,128)}) custom-call(s32[4]{0:T(128)} %refs_0_.1, f32[16,256]{1,0:T(8,128)} %bitcast.11, f32[16,256]{1,0:T(8,128)} %bitcast.15, f32[1,256]{1,0:T(1,128)} %bitcast.16, bf16[2048,256]{1,0:T(8,128)(2,1)} %refs_3_.1, f32[2,128,128]{2,1,0:T(8,128)} %get-tuple-element.9.seg_hbm, ...), custom_call_target="tpu_custom_call" | custom-call | flops 33554432 | bytes 2097152 | tf_op jit(solution)/shard_map/back_pass/pallas_call | solution.py:32
  37.3 0.0 all-to-all-done.1
  37.3 0.0 copy-start.1
  37.3 1.0 %copy-done.1 = bf16[32,64,256]{2,1,0:T(8,128)(2,1)} copy-done((bf16[32,64,256]{2,1,0:T(8,128)(2,1)}, bf16[32,64,256]{2,1,0:T(8,128)(2,1)S(1)}, u32[]{:S(2)}) %copy-start.1) | copy-done | bytes 1048600
  38.3 8.0 %all-to-all-start = ((bf16[32,64,256]{2,1,0:T(8,128)(2,1)}), bf16[32,64,256]{2,1,0:T(8,128)(2,1)S(1)}, u32[]{:S(2)}, u32[]{:S(2)}) async-start(bf16[32,64,256]{2,1,0:T(8,128)(2,1)} %bitcast.9), calls=%async_computation | async-start | bytes 2097152 | tf_op jit(solution)/shard_map/all_to_all | solution.py:580
  46.3 10.3 %residue_pass.1 = bf16[2,16,256]{2,1,0:T(8,128)(2,1)} custom-call(s32[4]{0:T(128)} %refs_0_.1, s32[4]{0:T(128)} %refs_1_.1, f32[16,256]{1,0:T(8,128)} %bitcast.12, bf16[2048,256]{1,0:T(8,128)(2,1)} %refs_3_.1, bf16[2048,256]{1,0:T(8,128)(2,1)} %bitcast.8, f32[2,128,128]{2,1,0:T(8,128)} %get-tuple-element.13.refs_5_), custom_call_target="tpu_custom_call" | custom-call | flops 33554432 | bytes 2097152 | tf_op jit(solution)/shard_map/residue_pass/pallas_call | solution.py:32
  56.6 6.3 %collective-permute-start.6 = (bf16[2,16,256]{2,1,0:T(8,128)(2,1)}, bf16[2,16,256]{2,1,0:T(8,128)(2,1)S(1)}, u32[]{:S(2)}, u32[]{:S(2)}) collective-permute-start(bf16[2,16,256]{2,1,0:T(8,128)(2,1)} %residue_pass.1), channel_id=1, source_target_pairs={{0,96},{32,0},{64,32},{96,64},{128,224},{160,128},{192,160},{224,1... | collective-permute-start | bytes 49160 | tf_op jit(solution)/shard_map/ppermute | solution.py:555
  62.9 0.0 collective-permute-start.5
  62.9 0.4 collective-permute-start.4
  63.3 0.7 collective-permute-done.6
  64.0 3.5 %collective-permute-done.5 = bf16[2,16,256]{2,1,0:T(8,128)(2,1)S(1)} collective-permute-done((bf16[2,16,256]{2,1,0:T(8,128)(2,1)}, bf16[2,16,256]{2,1,0:T(8,128)(2,1)S(1)}, u32[]{:S(2)}, u32[]{:S(2)}) %collective-permute-start.5) | collective-permute-done | bytes 16416 | tf_op jit(solution)/shard_map/ppermute | solution.py:555
  67.5 0.0 collective-permute-done.4
  67.5 0.7 add_add_fusion
  68.2 3.1 %collective-permute-start.7 = (f32[2,16,256]{2,1,0:T(8,128)S(1)}, f32[2,16,256]{2,1,0:T(8,128)S(1)}, u32[]{:S(2)}, u32[]{:S(2)}) collective-permute-start(f32[2,16,256]{2,1,0:T(8,128)S(1)} %add_add_fusion), channel_id=1, source_target_pairs={{0,128},{32,160},{64,192},{96,224},{128,0},{160,32},{192,64},{224,... | collective-permute-start | bytes 98312 | tf_op jit(solution)/shard_map/ppermute | solution.py:562
  71.4 0.0 all-to-all-done.grad_ref
  71.4 0.0 copy-start
  71.4 1.0 %copy-done = bf16[32,64,256]{2,1,0:T(8,128)(2,1)} copy-done((bf16[32,64,256]{2,1,0:T(8,128)(2,1)}, bf16[32,64,256]{2,1,0:T(8,128)(2,1)S(1)}, u32[]{:S(2)}) %copy-start) | copy-done | bytes 1048600
  72.3 4.3 %final_rows.1 = bf16[64,8192]{1,0:T(8,128)(2,1)} custom-call(bf16[64,8192]{1,0:T(8,128)(2,1)} %u_hbm.3, f32[1,8192]{1,0:T(1,128)} %bitcast.14, bf16[32,64,256]{2,1,0:T(8,128)(2,1)} %copy-done), custom_call_target="tpu_custom_call" | custom-call | flops 8388608 | bytes 3145728 | tf_op jit(solution)/shard_map/final_rows/pallas_call | solution.py:32
  76.6 0.0 collective-permute-done.7
  76.7 0.6 add_bitcast_fusion
Async XLA Ops:
  3.2 34.1 %all-to-all-start.1 = ((bf16[32,64,256]{2,1,0:T(8,128)(2,1)}), bf16[32,64,256]{2,1,0:T(8,128)(2,1)S(1)}, u32[]{:S(2)}, u32[]{:S(2)}) async-start(bf16[32,64,256]{2,1,0:T(8,128)(2,1)} %norm_rows.1), calls=%async_computation.1 | async-start | bytes 2097152 | tf_op jit(solution)/shard_map/all_to_all | solution.py:573
  17.4 9.7 %collective-permute-start.3 = (f32[16,256]{1,0:T(8,128)}, f32[16,256]{1,0:T(8,128)S(1)}, u32[]{:S(2)}, u32[]{:S(2)}) collective-permute-start(f32[16,256]{1,0:T(8,128)} %get-tuple-element.10), channel_id=1, source_target_pairs={{128,0},{160,32},{192,64},{224,96},{129,1},{161,33},{193,65},{225,... | collective-permute-start | bytes 49160 | tf_op jit(solution)/shard_map/ppermute | solution.py:546
  18.7 8.4 %collective-permute-start.2 = (f32[16,256]{1,0:T(8,128)}, f32[16,256]{1,0:T(8,128)S(1)}, u32[]{:S(2)}, u32[]{:S(2)}) collective-permute-start(f32[16,256]{1,0:T(8,128)} %get-tuple-element.10), channel_id=1, source_target_pairs={{96,0},{128,32},{160,64},{192,96},{224,128},{97,1},{129,33},{161,6... | collective-permute-start | bytes 49160 | tf_op jit(solution)/shard_map/ppermute | solution.py:546
  20.0 7.1 %collective-permute-start.1 = (f32[16,256]{1,0:T(8,128)}, f32[16,256]{1,0:T(8,128)S(1)}, u32[]{:S(2)}, u32[]{:S(2)}) collective-permute-start(f32[16,256]{1,0:T(8,128)} %get-tuple-element.10), channel_id=1, source_target_pairs={{64,0},{96,32},{128,64},{160,96},{192,128},{224,160},{65,1},{97,33... | collective-permute-start | bytes 49160 | tf_op jit(solution)/shard_map/ppermute | solution.py:546
  21.3 5.8 %collective-permute-start = (f32[16,256]{1,0:T(8,128)}, f32[16,256]{1,0:T(8,128)S(1)}, u32[]{:S(2)}, u32[]{:S(2)}) collective-permute-start(f32[16,256]{1,0:T(8,128)} %get-tuple-element.10), channel_id=1, source_target_pairs={{32,0},{64,32},{96,64},{128,96},{160,128},{192,160},{224,192},{33,... | collective-permute-start | bytes 49160 | tf_op jit(solution)/shard_map/ppermute | solution.py:546
  27.1 0.6 copy-start.2
  27.1 0.6 copy-start.3
  27.1 0.6 copy-start.4
  27.1 0.6 copy-start.5
  37.3 1.0 %copy-start.1 = (bf16[32,64,256]{2,1,0:T(8,128)(2,1)}, bf16[32,64,256]{2,1,0:T(8,128)(2,1)S(1)}, u32[]{:S(2)}) copy-start(bf16[32,64,256]{2,1,0:T(8,128)(2,1)S(1)} %all-to-all-done.1) | copy-start | bytes 3145732
  38.3 33.1 %all-to-all-start = ((bf16[32,64,256]{2,1,0:T(8,128)(2,1)}), bf16[32,64,256]{2,1,0:T(8,128)(2,1)S(1)}, u32[]{:S(2)}, u32[]{:S(2)}) async-start(bf16[32,64,256]{2,1,0:T(8,128)(2,1)} %bitcast.9), calls=%async_computation | async-start | bytes 2097152 | tf_op jit(solution)/shard_map/all_to_all | solution.py:580
  56.6 7.4 %collective-permute-start.6 = (bf16[2,16,256]{2,1,0:T(8,128)(2,1)}, bf16[2,16,256]{2,1,0:T(8,128)(2,1)S(1)}, u32[]{:S(2)}, u32[]{:S(2)}) collective-permute-start(bf16[2,16,256]{2,1,0:T(8,128)(2,1)} %residue_pass.1), channel_id=1, source_target_pairs={{0,96},{32,0},{64,32},{96,64},{128,224},{160,128},{192,160},{224,1... | collective-permute-start | bytes 49160 | tf_op jit(solution)/shard_map/ppermute | solution.py:555
  62.9 4.6 %collective-permute-start.5 = (bf16[2,16,256]{2,1,0:T(8,128)(2,1)}, bf16[2,16,256]{2,1,0:T(8,128)(2,1)S(1)}, u32[]{:S(2)}, u32[]{:S(2)}) collective-permute-start(bf16[2,16,256]{2,1,0:T(8,128)(2,1)} %residue_pass.1), channel_id=1, source_target_pairs={{0,32},{32,64},{64,96},{96,0},{128,160},{160,192},{192,224},{224,1... | collective-permute-start | bytes 49160 | tf_op jit(solution)/shard_map/ppermute | solution.py:555
  62.9 4.6 %collective-permute-start.4 = (bf16[2,16,256]{2,1,0:T(8,128)(2,1)}, bf16[2,16,256]{2,1,0:T(8,128)(2,1)S(1)}, u32[]{:S(2)}, u32[]{:S(2)}) collective-permute-start(bf16[2,16,256]{2,1,0:T(8,128)(2,1)} %residue_pass.1), channel_id=1, source_target_pairs={{0,64},{32,96},{64,0},{96,32},{128,192},{160,224},{192,128},{224,1... | collective-permute-start | bytes 49160 | tf_op jit(solution)/shard_map/ppermute | solution.py:555
  68.2 8.4 %collective-permute-start.7 = (f32[2,16,256]{2,1,0:T(8,128)S(1)}, f32[2,16,256]{2,1,0:T(8,128)S(1)}, u32[]{:S(2)}, u32[]{:S(2)}) collective-permute-start(f32[2,16,256]{2,1,0:T(8,128)S(1)} %add_add_fusion), channel_id=1, source_target_pairs={{0,128},{32,160},{64,192},{96,224},{128,0},{160,32},{192,64},{224,... | collective-permute-start | bytes 98312 | tf_op jit(solution)/shard_map/ppermute | solution.py:562
  71.4 1.0 %copy-start = (bf16[32,64,256]{2,1,0:T(8,128)(2,1)}, bf16[32,64,256]{2,1,0:T(8,128)(2,1)S(1)}, u32[]{:S(2)}) copy-start(bf16[32,64,256]{2,1,0:T(8,128)(2,1)S(1)} %all-to-all-done.grad_ref) | copy-start | bytes 3145732

commit v4 on v3

--- a/solution.py
+++ b/solution.py
@@ -32,12 +32,12 @@
     return pl.pallas_call(
         kernel,
         in_specs=[
-            pl.BlockSpec(memory_space=pltpu.VMEM if k in near else pl.ANY) for k in range(len(operands))
+            pl.BlockSpec(memory_space=pltpu.VMEM if k in near else pltpu.HBM) for k in range(len(operands))
         ],
-        out_specs=[pl.BlockSpec(memory_space=pl.ANY)] * len(outs),
+        out_specs=[pl.BlockSpec(memory_space=pltpu.HBM)] * len(outs),
         out_shape=outs,
         scratch_shapes=scratch + [pltpu.SemaphoreType.DMA((sems,))],
-        compiler_params=pltpu.CompilerParams(vmem_limit_bytes=60 * 1024 * 1024),
+        compiler_params=pltpu.CompilerParams(vmem_limit_bytes=16 * 1024 * 1024),
         cost_estimate=estimate,
         name=name,
     )(*operands)
@@ -347,7 +347,7 @@
         sems,
     )
     copies, grad_copies = copies[:4], copies[4:]
-    here = lax.axis_index("ctx")
+    here, last = lax.axis_index("ctx"), lax.axis_size("ctx")
     base = here * tokens
     lens_copy.wait()
     starts = doc_starts(lens_ref)
@@ -363,6 +363,7 @@
     for k in range(len(later), 0, -1):
         kept = jnp.where(any_start(starts, (here + k) * tokens, tokens), 0.0, 1.0)
         arriving = later[k - 1][...] + (through * kept) * arriving
+        arriving = jnp.where(here + k < last, arriving, 0.0)
     through = jnp.exp(-rates * float(seg_len))
     put_segment(arrive_ref, SEGS - 1, modes, arriving)
     for s in range(SEGS - 1, 0, -1):
@@ -543,8 +544,8 @@
 def from_later(value, axis):
     count = lax.axis_size(axis)
     return [
-        lax.ppermute(value, axis, [(i + k, i) for i in range(count - k)])
-        for k in range(1, max(2, count // 2 + 1))
+        lax.ppermute(value, axis, [((i + k) % count, i) for i in range(count)])
+        for k in range(1, count // 2 + 1)
     ]
 
 

time: 78.5 us -> 76 us (0.968)
  the two profiles are of different devices: /device:TPU:1 before, /device:TPU:2 now
where the time goes in v4:
time: 76 us; the launch traced here: 75.6 us
  starting transfers between devices  34.3 us (45%)
  Pallas kernels  24.3 us (32%)
  waiting for transfers between devices  9 us (12%)
  local copies, waits for them, and re-layouts  6.55 us (9%)
  between operations  0.79 us (1%)
    pallas_call x5, Pallas kernels, call(): pl.pallas_call(kernel, in_specs=[pl.BlockSpec(memory_space=pltpu.VMEM if...  24.3 us
    ppermute x4, starting transfers between devices, from_later(): lax.ppermute(value, axis, [((i + k) % count, i) for i in range(count)])  12.8 us
    all_to_all x1, starting transfers between devices, local(): lax.all_to_all(x_send, 'ch', split_axis=0, concat_axis=0, tiled=True)  7.77 us
    all_to_all x1, starting transfers between devices, local(): lax.all_to_all(normed_grad.reshape(groups, tokens // groups, chans), 'ch'...  7.38 us
    unnamed x26, local copies, waits for them, and re-layouts  6.55 us
    ppermute x3, waiting for transfers between devices, sum_over(): lax.ppermute(value, axis, [(i, i // half * half + (i + k) % half) for i i...  4.72 us
    ppermute x1, starting transfers between devices, sum_over(): lax.ppermute(parts[0], axis, [(i, (i + half) % count) for i in range(coun...  4.23 us
    ppermute x4, waiting for transfers between devices, from_later(): lax.ppermute(value, axis, [((i + k) % count, i) for i in range(count)])  2.84 us
  transfers between devices with their start and end apart: 10, of which 6 were waited for; matrix products, arithmetic and copies ran while one was open for 0% of the time, Pallas kernels for 30%

profile of v4, /device:TPU:2, one launch (start us, length us, event | category | flops | bytes accessed | tf_op | source)
XLA Modules:
  0.0 75.6 jit_solution(5920246726546061901)
XLA Ops:
  0.6 0.0 copy-start.1
  0.6 1.2 %copy-done.1 = bf16[64,8192]{1,0:T(8,128)(2,1)S(1)} copy-done((bf16[64,8192]{1,0:T(8,128)(2,1)S(1)}, bf16[64,8192]{1,0:T(8,128)(2,1)}, u32[]{:S(2)}) %copy-start.1) | copy-done | bytes 1048600
  1.9 0.0 copy-start.7
  1.9 0.8 %copy-done.7 = f32[8192]{0:T(1024)S(1)} copy-done((f32[8192]{0:T(1024)S(1)}, f32[8192]{0:T(1024)}, u32[]{:S(2)}) %copy-start.7) | copy-done | bytes 32792
  2.6 1.7 %norm_rows.1 = bf16[32,64,256]{2,1,0:T(8,128)(2,1)} custom-call(bf16[64,8192]{1,0:T(8,128)(2,1)S(1)} %copy-done.1, f32[1,8192]{1,0:T(1,128)S(1)} %bitcast.13), custom_call_target="tpu_custom_call" | custom-call | flops 4194304 | bytes 2097152 | tf_op jit(solution)/shard_map/norm_rows/pallas_call | solution.py:32
  4.3 0.0 copy-start
  4.3 0.0 copy-start.6
  4.3 0.0 copy-start.10
  4.3 7.8 %all-to-all-start.1 = ((bf16[32,64,256]{2,1,0:T(8,128)(2,1)}), bf16[32,64,256]{2,1,0:T(8,128)(2,1)S(1)}, u32[]{:S(2)}, u32[]{:S(2)}) async-start(bf16[32,64,256]{2,1,0:T(8,128)(2,1)} %norm_rows.1), calls=%async_computation.1 | async-start | bytes 2097152 | tf_op jit(solution)/shard_map/all_to_all | solution.py:574
  12.1 0.0 copy-done
  12.1 0.0 copy-done.6
  12.1 0.0 copy-done.10
  12.1 0.0 copy-start.9
  12.2 4.6 %leave.1 = (f32[2,128,128]{2,1,0:T(8,128)S(1)}, f32[16,256]{1,0:T(8,128)S(1)}) custom-call(s32[4]{0:T(128)S(1)} %copy-done.10, f32[16,256]{1,0:T(8,128)S(1)} %bitcast.10, bf16[2048,256]{1,0:T(8,128)(2,1)S(1)} %copy-done), custom_call_target="tpu_custom_call" | custom-call | flops 16777216 | bytes 1048576 | tf_op jit(solution)/shard_map/leave/pallas_call | solution.py:32
  16.8 7.3 %collective-permute-start.3 = (f32[16,256]{1,0:T(8,128)S(1)}, f32[16,256]{1,0:T(8,128)S(1)}, u32[]{:S(2)}, u32[]{:S(2)}) collective-permute-start(f32[16,256]{1,0:T(8,128)S(1)} %get-tuple-element.10), channel_id=1, source_target_pairs={{128,0},{160,32},{192,64},{224,96},{0,128},{32,160},{64,192},{96,2... | collective-permute-start | bytes 49160 | tf_op jit(solution)/shard_map/ppermute | solution.py:547
  24.0 0.0 collective-permute-start.2
  24.0 4.6 %collective-permute-start.1 = (f32[16,256]{1,0:T(8,128)S(1)}, f32[16,256]{1,0:T(8,128)S(1)}, u32[]{:S(2)}, u32[]{:S(2)}) collective-permute-start(f32[16,256]{1,0:T(8,128)S(1)} %get-tuple-element.10), channel_id=1, source_target_pairs={{64,0},{96,32},{128,64},{160,96},{192,128},{224,160},{0,192},{32,2... | collective-permute-start | bytes 49160 | tf_op jit(solution)/shard_map/ppermute | solution.py:547
  28.6 0.9 %collective-permute-start = (f32[16,256]{1,0:T(8,128)S(1)}, f32[16,256]{1,0:T(8,128)S(1)}, u32[]{:S(2)}, u32[]{:S(2)}) collective-permute-start(f32[16,256]{1,0:T(8,128)S(1)} %get-tuple-element.10), channel_id=1, source_target_pairs={{32,0},{64,32},{96,64},{128,96},{160,128},{192,160},{224,192},{0,2... | collective-permute-start | bytes 49160 | tf_op jit(solution)/shard_map/ppermute | solution.py:547
  29.5 0.0 collective-permute-done.3.refs_3_
  29.5 0.0 collective-permute-done.2.refs_2_
  29.6 0.5 collective-permute-done.1.refs_1_
  30.1 2.3 %collective-permute-done.refs_0_ = f32[16,256]{1,0:T(8,128)S(1)} collective-permute-done((f32[16,256]{1,0:T(8,128)S(1)}, f32[16,256]{1,0:T(8,128)S(1)}, u32[]{:S(2)}, u32[]{:S(2)}) %collective-permute-start) | collective-permute-done | bytes 16416 | tf_op jit(solution)/shard_map/ppermute | solution.py:547
  32.4 0.0 copy-start.11
  32.4 0.0 copy-done.9
  32.4 0.7 copy-done.11
  33.1 7.7 %back_pass.1 = (bf16[2048,256]{1,0:T(8,128)(2,1)S(1)}, f32[2,128,128]{2,1,0:T(8,128)S(1)}) custom-call(s32[4]{0:T(128)S(1)} %copy-done.10, f32[16,256]{1,0:T(8,128)S(1)} %bitcast.11, f32[16,256]{1,0:T(8,128)S(1)} %bitcast.15, f32[1,256]{1,0:T(1,128)S(1)} %bitcast.16, bf16[2048,256]{1,0:T(8,128)(2,1)S(1)} %copy-done, ...), custom_call_target="tpu_custom_call" | custom-call | flops 33554432 | bytes 2097152 | tf_op jit(solution)/shard_map/back_pass/pallas_call | solution.py:32
  40.8 0.0 copy-start.5
  40.8 1.0 %copy-done.5 = bf16[2048,256]{1,0:T(8,128)(2,1)} copy-done((bf16[2048,256]{1,0:T(8,128)(2,1)}, bf16[2048,256]{1,0:T(8,128)(2,1)S(1)}, u32[]{:S(2)}) %copy-start.5) | copy-done | bytes 1048600
  41.7 0.0 all-to-all-done.1
  41.7 0.0 copy-start.3
  41.7 1.0 %copy-done.3 = bf16[32,64,256]{2,1,0:T(8,128)(2,1)} copy-done((bf16[32,64,256]{2,1,0:T(8,128)(2,1)}, bf16[32,64,256]{2,1,0:T(8,128)(2,1)S(1)}, u32[]{:S(2)}) %copy-start.3) | copy-done | bytes 1048600
  42.8 7.4 %all-to-all-start = ((bf16[32,64,256]{2,1,0:T(8,128)(2,1)}), bf16[32,64,256]{2,1,0:T(8,128)(2,1)S(1)}, u32[]{:S(2)}, u32[]{:S(2)}) async-start(bf16[32,64,256]{2,1,0:T(8,128)(2,1)} %bitcast.9), calls=%async_computation | async-start | bytes 2097152 | tf_op jit(solution)/shard_map/all_to_all | solution.py:581
  50.2 0.0 copy-start.12
  50.2 0.6 copy-done.12
  50.8 0.0 copy-start.4
  50.8 1.2 %copy-done.4 = bf16[32,64,256]{2,1,0:T(8,128)(2,1)S(1)} copy-done((bf16[32,64,256]{2,1,0:T(8,128)(2,1)S(1)}, bf16[32,64,256]{2,1,0:T(8,128)(2,1)}, u32[]{:S(2)}) %copy-start.4) | copy-done | bytes 1048600
  52.0 0.0 copy-start.2
  52.0 8.1 %residue_pass.1 = bf16[2,16,256]{2,1,0:T(8,128)(2,1)S(1)} custom-call(s32[4]{0:T(128)S(1)} %copy-done.10, s32[4]{0:T(128)S(1)} %copy-done.12, f32[16,256]{1,0:T(8,128)S(1)} %bitcast.12, bf16[2048,256]{1,0:T(8,128)(2,1)S(1)} %copy-done, bf16[2048,256]{1,0:T(8,128)(2,1)S(1)} %bitcast.8, f32[2,128,128]{2,1,0:T(8,128)S(1)} %get-tuple-element.13.refs_5_), custom_call_target="tpu_custom_call" | custom-call | flops 33554432 | bytes 2097152 | tf_op jit(solution)/shard_map/residue_pass/pallas_call | solution.py:32
  60.2 0.0 copy-start.8
  60.2 0.9 %collective-permute-start.6 = (bf16[2,16,256]{2,1,0:T(8,128)(2,1)S(1)}, bf16[2,16,256]{2,1,0:T(8,128)(2,1)S(1)}, u32[]{:S(2)}, u32[]{:S(2)}) collective-permute-start(bf16[2,16,256]{2,1,0:T(8,128)(2,1)S(1)} %residue_pass.1), channel_id=1, source_target_pairs={{0,96},{32,0},{64,32},{96,64},{128,224},{160,128},{192,160},{224,1... | collective-permute-start | bytes 49160 | tf_op jit(solution)/shard_map/ppermute | solution.py:556
  61.1 1.2 %collective-permute-start.5 = (bf16[2,16,256]{2,1,0:T(8,128)(2,1)S(1)}, bf16[2,16,256]{2,1,0:T(8,128)(2,1)S(1)}, u32[]{:S(2)}, u32[]{:S(2)}) collective-permute-start(bf16[2,16,256]{2,1,0:T(8,128)(2,1)S(1)} %residue_pass.1), channel_id=1, source_target_pairs={{0,32},{32,64},{64,96},{96,0},{128,160},{160,192},{192,224},{224,1... | collective-permute-start | bytes 49160 | tf_op jit(solution)/shard_map/ppermute | solution.py:556
  62.3 0.0 collective-permute-start.4
  62.3 1.7 %collective-permute-done.6 = bf16[2,16,256]{2,1,0:T(8,128)(2,1)S(1)} collective-permute-done((bf16[2,16,256]{2,1,0:T(8,128)(2,1)S(1)}, bf16[2,16,256]{2,1,0:T(8,128)(2,1)S(1)}, u32[]{:S(2)}, u32[]{:S(2)}) %collective-permute-start.6) | collective-permute-done | bytes 16416 | tf_op jit(solution)/shard_map/ppermute | solution.py:556
  64.0 2.7 %collective-permute-done.5 = bf16[2,16,256]{2,1,0:T(8,128)(2,1)S(1)} collective-permute-done((bf16[2,16,256]{2,1,0:T(8,128)(2,1)S(1)}, bf16[2,16,256]{2,1,0:T(8,128)(2,1)S(1)}, u32[]{:S(2)}, u32[]{:S(2)}) %collective-permute-start.5) | collective-permute-done | bytes 16416 | tf_op jit(solution)/shard_map/ppermute | solution.py:556
  66.7 0.4 collective-permute-done.4
  67.0 4.2 %collective-permute-start.7 = (f32[2,16,256]{2,1,0:T(8,128)S(1)}, f32[2,16,256]{2,1,0:T(8,128)S(1)}, u32[]{:S(2)}, u32[]{:S(2)}) collective-permute-start(f32[2,16,256]{2,1,0:T(8,128)S(1)} %add_add_fusion), channel_id=1, source_target_pairs={{0,128},{32,160},{64,192},{96,224},{128,0},{160,32},{192,64},{224,... | collective-permute-start | bytes 98312 | tf_op jit(solution)/shard_map/ppermute | solution.py:563
  71.3 0.0 all-to-all-done.grad_ref
  71.3 0.0 copy-done.2
  71.3 0.0 copy-done.8
  71.3 2.2 %final_rows.1 = bf16[64,8192]{1,0:T(8,128)(2,1)} custom-call(bf16[64,8192]{1,0:T(8,128)(2,1)S(1)} %copy-done.2, f32[1,8192]{1,0:T(1,128)S(1)} %bitcast.14, bf16[32,64,256]{2,1,0:T(8,128)(2,1)S(1)} %all-to-all-done.grad_ref), custom_call_target="tpu_custom_call" | custom-call | flops 8388608 | bytes 3145728 | tf_op jit(solution)/shard_map/final_rows/pallas_call | solution.py:32
  73.5 1.4 %collective-permute-done.7 = f32[2,16,256]{2,1,0:T(8,128)S(1)} collective-permute-done((f32[2,16,256]{2,1,0:T(8,128)S(1)}, f32[2,16,256]{2,1,0:T(8,128)S(1)}, u32[]{:S(2)}, u32[]{:S(2)}) %collective-permute-start.7) | collective-permute-done | bytes 32800 | tf_op jit(solution)/shard_map/ppermute | solution.py:563
  74.9 0.6 add_bitcast_fusion
  (1 shorter events, 0.0 us)
Async XLA Ops:
  0.6 1.2 %copy-start.1 = (bf16[64,8192]{1,0:T(8,128)(2,1)S(1)}, bf16[64,8192]{1,0:T(8,128)(2,1)}, u32[]{:S(2)}) copy-start(bf16[64,8192]{1,0:T(8,128)(2,1)} %u_hbm.3) | copy-start | bytes 3145732
  1.9 0.8 %copy-start.7 = (f32[8192]{0:T(1024)S(1)}, f32[8192]{0:T(1024)}, u32[]{:S(2)}) copy-start(f32[8192]{0:T(1024)} %param.9) | copy-start | bytes 98308
  4.3 7.8 %copy-start = (bf16[2048,256]{1,0:T(8,128)(2,1)S(1)}, bf16[2048,256]{1,0:T(8,128)(2,1)}, u32[]{:S(2)}) copy-start(bf16[2048,256]{1,0:T(8,128)(2,1)} %refs_3_.1) | copy-start | bytes 3145732
  4.3 7.8 %copy-start.6 = (f32[256,16]{0,1:T(8,128)S(1)}, f32[256,16]{0,1:T(8,128)}, u32[]{:S(2)}) copy-start(f32[256,16]{0,1:T(8,128)} %param.12) | copy-start | bytes 49156
  4.3 7.8 %copy-start.10 = (s32[4]{0:T(128)S(1)}, s32[4]{0:T(128)}, u32[]{:S(2)}) copy-start(s32[4]{0:T(128)} %refs_0_.1) | copy-start | bytes 52
  4.3 37.4 %all-to-all-start.1 = ((bf16[32,64,256]{2,1,0:T(8,128)(2,1)}), bf16[32,64,256]{2,1,0:T(8,128)(2,1)S(1)}, u32[]{:S(2)}, u32[]{:S(2)}) async-start(bf16[32,64,256]{2,1,0:T(8,128)(2,1)} %norm_rows.1), calls=%async_computation.1 | async-start | bytes 2097152 | tf_op jit(solution)/shard_map/all_to_all | solution.py:574
  12.1 20.2 %copy-start.9 = (f32[256,16]{0,1:T(8,128)S(1)}, f32[256,16]{0,1:T(8,128)}, u32[]{:S(2)}) copy-start(f32[256,16]{0,1:T(8,128)} %param.11) | copy-start | bytes 49156
  16.8 12.8 %collective-permute-start.3 = (f32[16,256]{1,0:T(8,128)S(1)}, f32[16,256]{1,0:T(8,128)S(1)}, u32[]{:S(2)}, u32[]{:S(2)}) collective-permute-start(f32[16,256]{1,0:T(8,128)S(1)} %get-tuple-element.10), channel_id=1, source_target_pairs={{128,0},{160,32},{192,64},{224,96},{0,128},{32,160},{64,192},{96,2... | collective-permute-start | bytes 49160 | tf_op jit(solution)/shard_map/ppermute | solution.py:547
  24.0 5.5 %collective-permute-start.2 = (f32[16,256]{1,0:T(8,128)S(1)}, f32[16,256]{1,0:T(8,128)S(1)}, u32[]{:S(2)}, u32[]{:S(2)}) collective-permute-start(f32[16,256]{1,0:T(8,128)S(1)} %get-tuple-element.10), channel_id=1, source_target_pairs={{96,0},{128,32},{160,64},{192,96},{224,128},{0,160},{32,192},{64,2... | collective-permute-start | bytes 49160 | tf_op jit(solution)/shard_map/ppermute | solution.py:547
  24.0 6.0 %collective-permute-start.1 = (f32[16,256]{1,0:T(8,128)S(1)}, f32[16,256]{1,0:T(8,128)S(1)}, u32[]{:S(2)}, u32[]{:S(2)}) collective-permute-start(f32[16,256]{1,0:T(8,128)S(1)} %get-tuple-element.10), channel_id=1, source_target_pairs={{64,0},{96,32},{128,64},{160,96},{192,128},{224,160},{0,192},{32,2... | collective-permute-start | bytes 49160 | tf_op jit(solution)/shard_map/ppermute | solution.py:547
  28.6 3.7 %collective-permute-start = (f32[16,256]{1,0:T(8,128)S(1)}, f32[16,256]{1,0:T(8,128)S(1)}, u32[]{:S(2)}, u32[]{:S(2)}) collective-permute-start(f32[16,256]{1,0:T(8,128)S(1)} %get-tuple-element.10), channel_id=1, source_target_pairs={{32,0},{64,32},{96,64},{128,96},{160,128},{192,160},{224,192},{0,2... | collective-permute-start | bytes 49160 | tf_op jit(solution)/shard_map/ppermute | solution.py:547
  32.4 0.7 copy-start.11
  40.8 1.0 %copy-start.5 = (bf16[2048,256]{1,0:T(8,128)(2,1)}, bf16[2048,256]{1,0:T(8,128)(2,1)S(1)}, u32[]{:S(2)}) copy-start(bf16[2048,256]{1,0:T(8,128)(2,1)S(1)} %get-tuple-element.11) | copy-start | bytes 3145732
  41.7 1.0 %copy-start.3 = (bf16[32,64,256]{2,1,0:T(8,128)(2,1)}, bf16[32,64,256]{2,1,0:T(8,128)(2,1)S(1)}, u32[]{:S(2)}) copy-start(bf16[32,64,256]{2,1,0:T(8,128)(2,1)S(1)} %all-to-all-done.1) | copy-start | bytes 3145732
  42.8 28.5 %all-to-all-start = ((bf16[32,64,256]{2,1,0:T(8,128)(2,1)}), bf16[32,64,256]{2,1,0:T(8,128)(2,1)S(1)}, u32[]{:S(2)}, u32[]{:S(2)}) async-start(bf16[32,64,256]{2,1,0:T(8,128)(2,1)} %bitcast.9), calls=%async_computation | async-start | bytes 2097152 | tf_op jit(solution)/shard_map/all_to_all | solution.py:581
  50.2 0.7 copy-start.12
  50.8 1.2 %copy-start.4 = (bf16[32,64,256]{2,1,0:T(8,128)(2,1)S(1)}, bf16[32,64,256]{2,1,0:T(8,128)(2,1)}, u32[]{:S(2)}) copy-start(bf16[32,64,256]{2,1,0:T(8,128)(2,1)} %copy-done.3) | copy-start | bytes 3145732
  52.0 19.2 %copy-start.2 = (bf16[64,8192]{1,0:T(8,128)(2,1)S(1)}, bf16[64,8192]{1,0:T(8,128)(2,1)}, u32[]{:S(2)}) copy-start(bf16[64,8192]{1,0:T(8,128)(2,1)} %u_hbm.3) | copy-start | bytes 3145732
  60.2 11.1 %copy-start.8 = (f32[8192]{0:T(1024)S(1)}, f32[8192]{0:T(1024)}, u32[]{:S(2)}) copy-start(f32[8192]{0:T(1024)} %param.9) | copy-start | bytes 98308
  60.2 3.8 %collective-permute-start.6 = (bf16[2,16,256]{2,1,0:T(8,128)(2,1)S(1)}, bf16[2,16,256]{2,1,0:T(8,128)(2,1)S(1)}, u32[]{:S(2)}, u32[]{:S(2)}) collective-permute-start(bf16[2,16,256]{2,1,0:T(8,128)(2,1)S(1)} %residue_pass.1), channel_id=1, source_target_pairs={{0,96},{32,0},{64,32},{96,64},{128,224},{160,128},{192,160},{224,1... | collective-permute-start | bytes 49160 | tf_op jit(solution)/shard_map/ppermute | solution.py:556
  61.1 5.5 %collective-permute-start.5 = (bf16[2,16,256]{2,1,0:T(8,128)(2,1)S(1)}, bf16[2,16,256]{2,1,0:T(8,128)(2,1)S(1)}, u32[]{:S(2)}, u32[]{:S(2)}) collective-permute-start(bf16[2,16,256]{2,1,0:T(8,128)(2,1)S(1)} %residue_pass.1), channel_id=1, source_target_pairs={{0,32},{32,64},{64,96},{96,0},{128,160},{160,192},{192,224},{224,1... | collective-permute-start | bytes 49160 | tf_op jit(solution)/shard_map/ppermute | solution.py:556
  62.3 4.7 %collective-permute-start.4 = (bf16[2,16,256]{2,1,0:T(8,128)(2,1)S(1)}, bf16[2,16,256]{2,1,0:T(8,128)(2,1)S(1)}, u32[]{:S(2)}, u32[]{:S(2)}) collective-permute-start(bf16[2,16,256]{2,1,0:T(8,128)(2,1)S(1)} %residue_pass.1), channel_id=1, source_target_pairs={{0,64},{32,96},{64,0},{96,32},{128,192},{160,224},{192,128},{224,1... | collective-permute-start | bytes 49160 | tf_op jit(solution)/shard_map/ppermute | solution.py:556
  67.0 7.9 %collective-permute-start.7 = (f32[2,16,256]{2,1,0:T(8,128)S(1)}, f32[2,16,256]{2,1,0:T(8,128)S(1)}, u32[]{:S(2)}, u32[]{:S(2)}) collective-permute-start(f32[2,16,256]{2,1,0:T(8,128)S(1)} %add_add_fusion), channel_id=1, source_target_pairs={{0,128},{32,160},{64,192},{96,224},{128,0},{160,32},{192,64},{224,... | collective-permute-start | bytes 98312 | tf_op jit(solution)/shard_map/ppermute | solution.py:563

commit v5 on v4

v5 whole, which is shorter than its diff:
```python
import math

import jax
import jax.numpy as jnp
from jax import lax
from jax.experimental import pallas as pl
from jax.experimental.pallas import tpu as pltpu
from jax.sharding import PartitionSpec as P

F32 = jnp.float32
BF16 = jnp.bfloat16
SEGS = 8
LANES = 128
UNROLL = 8
STEPS = 32
ROW_BLOCK = 16


def cost(flops, size):
    return pl.CostEstimate(flops=flops, bytes_accessed=size, transcendentals=0)


def load(pairs, sems):
    copies = [pltpu.make_async_copy(a, b, sems.at[k]) for k, (a, b) in enumerate(pairs)]
    for copy in copies:
        copy.start()
    return copies


def call(kernel, outs, scratch, name, estimate, spaces, out_spaces, operands, limit=16):
    return pl.pallas_call(
        kernel,
        in_specs=[pl.BlockSpec(memory_space=space) for space in spaces],
        out_specs=[pl.BlockSpec(memory_space=space) for space in out_spaces],
        out_shape=outs,
        scratch_shapes=scratch,
        compiler_params=pltpu.CompilerParams(vmem_limit_bytes=limit * 1024 * 1024),
        cost_estimate=estimate,
        name=name,
    )(*operands)


def inverse_rms(u_ref, eps=1e-05):
    rows, width = u_ref.shape
    total = jnp.zeros((rows, LANES), F32)
    for c in range(width // LANES):
        part = u_ref[:, c * LANES : (c + 1) * LANES].astype(F32)
        total = total + part * part
    return lax.rsqrt(jnp.sum(total, axis=1, keepdims=True) / width + eps)


def norm_kernel(u_hbm, gain_hbm, out_hbm, u_ref, gain_ref, out_ref, sems):
    blocks, groups, rows, chans = out_ref.shape
    span = [pl.ds(b * rows, rows) for b in range(blocks)]
    gain_copy, *u_copies = load(
        [(gain_hbm, gain_ref)] + [(u_hbm.at[span[b]], u_ref.at[b]) for b in range(blocks)], sems
    )
    gain_copy.wait()
    out_copies = []
    for b in range(blocks):
        u_copies[b].wait()
        inv = inverse_rms(u_ref.at[b])
        for c in range(groups):
            cols = slice(c * chans, (c + 1) * chans)
            normal = u_ref[b, :, cols].astype(F32) * inv
            out_ref[b, c] = (normal * gain_ref[:, cols]).astype(BF16)
        copy = pltpu.make_async_copy(out_ref.at[b], out_hbm.at[:, span[b]], sems.at[1 + blocks + b])
        copy.start()
        out_copies.append(copy)
    for copy in out_copies:
        copy.wait()


def norm_rows(u_rows, gain, groups):
    rows, width = u_rows.shape
    chans, blocks = width // groups, rows // ROW_BLOCK
    return call(
        norm_kernel,
        [jax.ShapeDtypeStruct((groups, rows, chans), BF16)],
        [
            pltpu.VMEM((blocks, ROW_BLOCK, width), BF16),
            pltpu.VMEM((1, width), F32),
            pltpu.VMEM((blocks, groups, ROW_BLOCK, chans), BF16),
            pltpu.SemaphoreType.DMA((1 + 2 * blocks,)),
        ],
        "norm_rows",
        cost(8 * rows * width, 4 * rows * width),
        [pl.ANY] * 2,
        [pl.ANY],
        (u_rows, gain),
        60,
    )[0]


def final_kernel(u_ref, gain_ref, grad_ref, out_hbm, out_ref, sems):
    blocks, rows, _ = out_ref.shape
    groups, _, chans = grad_ref.shape
    width = groups * chans
    out_copies = []
    for b in range(blocks):
        span = pl.ds(b * rows, rows)
        inv = inverse_rms(u_ref.at[span])
        total = jnp.zeros((rows, chans), F32)
        for c in range(groups):
            cols = slice(c * chans, (c + 1) * chans)
            normal = u_ref[span, cols].astype(F32) * inv
            total = total + normal * (gain_ref[:, cols] * grad_ref[c, span, :].astype(F32))
        project = jnp.sum(total, axis=1, keepdims=True) / width
        for c in range(groups):
            cols = slice(c * chans, (c + 1) * chans)
            normal = u_ref[span, cols].astype(F32) * inv
            scaled = gain_ref[:, cols] * grad_ref[c, span, :].astype(F32)
            out_ref[b, :, cols] = (inv * (scaled - normal * project)).astype(BF16)
        copy = pltpu.make_async_copy(out_ref.at[b], out_hbm.at[span], sems.at[b])
        copy.start()
        out_copies.append(copy)
    for copy in out_copies:
        copy.wait()


def final_rows(u_rows, gain, grad_rows):
    rows, width = u_rows.shape
    blocks = rows // ROW_BLOCK
    return call(
        final_kernel,
        [jax.ShapeDtypeStruct((rows, width), BF16)],
        [
            pltpu.VMEM((blocks, ROW_BLOCK, width), BF16),
            pltpu.SemaphoreType.DMA((blocks,)),
        ],
        "final_rows",
        cost(16 * rows * width, 6 * rows * width),
        [pltpu.VMEM] * 3,
        [pl.ANY],
        (u_rows, gain, grad_rows),
    )[0]


def doc_starts(lens_ref):
    starts, at = [], jnp.int32(0)
    for k in range(lens_ref.shape[0] - 1):
        at = at + lens_ref[k]
        starts.append(at)
    return starts


def sort_down(codes):
    codes = list(codes)
    for end in range(len(codes) - 1, 0, -1):
        for k in range(end):
            high = jnp.maximum(codes[k], codes[k + 1])
            low = jnp.minimum(codes[k], codes[k + 1])
            codes[k], codes[k + 1] = high, low
    return codes


def cut_codes(starts, streams, base, seg_len):
    codes = []
    for start, stream in zip(starts, streams):
        place = start - base
        inside = (place >= 0) & (place < SEGS * seg_len)
        code = (place % seg_len) * 16 + place // seg_len
        codes.append(jnp.where(inside, code, 15) * 2 + stream)
    return sort_down(codes)


def any_start(starts, first, count):
    found = jnp.bool_(False)
    for start in starts:
        found = found | ((start >= first) & (start < first + count))
    return found


def time_loop(cuts_ref, seg_len, step, cut, carry):
    def piece(p, state):
        top, inner = state
        code = cuts_ref[p]
        low = code // 32
        count = top - low
        full = count // UNROLL

        def many(k, value):
            first = top - (k + 1) * UNROLL
            for j in range(UNROLL - 1, -1, -1):
                value = step(first + j, value)
            return value

        def one(k, value):
            return step(top - full * UNROLL - 1 - k, value)

        inner = lax.fori_loop(0, full, many, inner)
        inner = lax.fori_loop(0, count - full * UNROLL, one, inner)
        inner = cut((code // 2) % 16, code % 2, inner)
        return (low, inner)

    return lax.fori_loop(0, cuts_ref.shape[0], piece, (jnp.int32(seg_len), carry))[1]


def order_matrix(steps, to_steps):
    size = SEGS * steps
    row = lax.broadcasted_iota(jnp.int32, (size, size), 0)
    col = lax.broadcasted_iota(jnp.int32, (size, size), 1)
    by_step, by_segment = (row, col) if to_steps else (col, row)
    return (by_segment == by_step % SEGS * steps + by_step // SEGS).astype(F32).astype(BF16)


def block_steps(tokens):
    return min(STEPS, tokens // SEGS)


def to_steps(source_ref, target_ref, order_ref):
    halves, tokens, _ = target_ref.shape
    steps, seg_len = block_steps(tokens), tokens // SEGS

    def body(b, _):
        rows = [
            source_ref[pl.ds(pl.multiple_of(s * seg_len + b * steps, steps), steps), :] for s in range(SEGS)
        ]
        block = jnp.dot(order_ref[...], jnp.concatenate(rows, axis=0), preferred_element_type=F32)
        size = SEGS * steps
        for h in range(halves):
            target_ref[h, pl.ds(pl.multiple_of(b * size, size), size), :] = block[
                :, h * LANES : (h + 1) * LANES
            ]
        return 0

    lax.fori_loop(0, seg_len // steps, body, 0)


def from_steps(source_ref, target_ref, order_ref):
    halves, tokens, _ = source_ref.shape
    steps, seg_len = block_steps(tokens), tokens // SEGS

    def body(b, _):
        size = SEGS * steps
        rows = pl.ds(pl.multiple_of(b * size, size), size)
        block = jnp.concatenate([source_ref[h, rows, :].astype(BF16) for h in range(halves)], axis=1)
        block = jnp.dot(order_ref[...], block, preferred_element_type=F32).astype(BF16)
        for s in range(SEGS):
            target_ref[pl.ds(pl.multiple_of(s * seg_len + b * steps, steps), steps), :] = block[
                s * steps : (s + 1) * steps
            ]
        return 0

    lax.fori_loop(0, seg_len // steps, body, 0)


def step_rows(i):
    return pl.ds(pl.multiple_of(i * SEGS, SEGS), SEGS)


def spread(ref, r, cols):
    return jnp.broadcast_to(ref[r : r + 1, cols], (SEGS, LANES))


def segment(ref, s, modes):
    rows = slice(s * modes, (s + 1) * modes)
    return jnp.concatenate([ref[h, rows, :] for h in range(ref.shape[0])], axis=1)


def put_segment(ref, s, modes, value):
    for h in range(ref.shape[0]):
        ref[h, s * modes : (s + 1) * modes, :] = value[:, h * LANES : (h + 1) * LANES]


def store_cuts(cuts_ref, codes):
    for k, code in enumerate(codes):
        cuts_ref[k] = code
    cuts_ref[len(codes)] = jnp.int32(30)


def leave_kernel(
    lens_ref, rates_ref, residues_ref, skip_ref, grad_ref, seg_ref, dev_ref, coef_ref,
    wide_ref, order_ref, cuts_ref,
):
    tokens, chans = grad_ref.shape
    modes = rates_ref.shape[0]
    seg_len = tokens // SEGS
    base = lax.axis_index("ctx") * tokens
    starts = doc_starts(lens_ref)
    store_cuts(cuts_ref, cut_codes(starts, [0] * len(starts), base, seg_len))
    order_ref[...] = order_matrix(block_steps(tokens), True)
    to_steps(grad_ref, wide_ref, order_ref)
    rates = rates_ref[...]
    decay_all = jnp.exp(-rates)
    mode_scale = jnp.sqrt(1.0 - decay_all * decay_all)
    coef_ref[:modes] = decay_all
    coef_ref[modes : 2 * modes] = mode_scale
    coef_ref[2 * modes : 3 * modes] = residues_ref[...] * mode_scale
    coef_ref[3 * modes :] = jnp.broadcast_to(skip_ref[...], (SEGS, chans))
    row = lax.broadcasted_iota(jnp.int32, (SEGS, LANES), 0)
    for h in range(chans // LANES):
        cols = slice(h * LANES, (h + 1) * LANES)
        decay = [spread(coef_ref, r, cols) for r in range(modes)]

        def step(i, state):
            grad = wide_ref[h, step_rows(i), :]
            return tuple(grad + decay[r] * state[r] for r in range(modes))

        def cut(place, stream, state):
            hold = row != place
            return tuple(jnp.where(hold, part, 0.0) for part in state)

        zero = jnp.zeros((SEGS, LANES), F32)
        state = time_loop(cuts_ref, seg_len, step, cut, (zero,) * modes)
        for r in range(modes):
            seg_ref[h, pl.ds(r, SEGS, stride=modes), :] = decay[r] * state[r]
    through = jnp.exp(-rates * float(seg_len))
    leaving = segment(seg_ref, SEGS - 1, modes)
    for s in range(SEGS - 2, -1, -1):
        kept = jnp.where(any_start(starts, base + s * seg_len, seg_len), 0.0, 1.0)
        leaving = segment(seg_ref, s, modes) + (through * kept) * leaving
    dev_ref[...] = leaving


def state_scratch(docs, modes, tokens, chans):
    halves, size = chans // LANES, SEGS * block_steps(tokens)
    return {
        "cuts": pltpu.SMEM((docs,), jnp.int32),
        "narrow": pltpu.VMEM((tokens, chans), BF16),
        "wide": pltpu.VMEM((halves, tokens, LANES), F32),
        "order": pltpu.VMEM((size, size), BF16),
        "segs": pltpu.VMEM((halves, SEGS * modes, LANES), F32),
        "weights": pltpu.VMEM((modes, SEGS, LANES), F32),
        "total": pltpu.VMEM((2, modes, SEGS, chans), F32),
        "sems": pltpu.SemaphoreType.DMA((1,)),
    }


def leave(doc_lengths, rates, residues, skip, grad_out):
    modes, chans = rates.shape
    tokens = grad_out.shape[0]
    kinds = state_scratch(doc_lengths.shape[0], modes, tokens, chans)
    return call(
        leave_kernel,
        [
            jax.ShapeDtypeStruct((chans // LANES, SEGS * modes, LANES), F32),
            jax.ShapeDtypeStruct((modes, chans), F32),
            jax.ShapeDtypeStruct((3 * modes + SEGS, chans), F32),
        ],
        [kinds[k] for k in ("wide", "order", "cuts")],
        "leave",
        cost(2 * tokens * chans * modes, 2 * tokens * chans),
        [pltpu.SMEM] + [pltpu.VMEM] * 4,
        [pltpu.VMEM] * 3,
        (doc_lengths, rates, residues, skip, grad_out),
    )


def back_kernel(window, lens_ref, streams_ref, rates_ref, coef_ref, grad_ref, x_ref, seg_ref, *refs):
    later = refs[:-12]
    (out_hbm, residue_ref, out_ref, arrive_ref, wide_ref, x_wide_ref, conv_ref, weight_ref, total_ref,
     order_ref, cuts_ref, sems) = refs[-12:]
    tokens, chans = grad_ref.shape
    modes = rates_ref.shape[0]
    seg_len = tokens // SEGS
    here, last = lax.axis_index("ctx"), lax.axis_size("ctx")
    base = here * tokens
    starts = doc_starts(lens_ref)
    streams = [streams_ref[k] for k in range(len(starts) + 1)]
    store_cuts(cuts_ref, cut_codes(starts, streams[1:], base, seg_len))
    rates = rates_ref[...]
    through = jnp.exp(-rates * float(tokens))
    arriving = jnp.zeros((modes, chans), F32)
    for k in range(len(later), 0, -1):
        kept = jnp.where(any_start(starts, (here + k) * tokens, tokens), 0.0, 1.0)
        arriving = later[k - 1][...] + (through * kept) * arriving
        arriving = jnp.where(here + k < last, arriving, 0.0)
    through = jnp.exp(-rates * float(seg_len))
    put_segment(arrive_ref, SEGS - 1, modes, arriving)
    for s in range(SEGS - 1, 0, -1):
        kept = jnp.where(any_start(starts, base + s * seg_len, seg_len), 0.0, 1.0)
        arriving = segment(seg_ref, s, modes) + (through * kept) * arriving
        put_segment(arrive_ref, s - 1, modes, arriving)
    order_ref[...] = order_matrix(block_steps(tokens), True)
    to_steps(grad_ref, wide_ref, order_ref)
    to_steps(x_ref, x_wide_ref, order_ref)
    total_ref[...] = jnp.zeros_like(total_ref)
    row = lax.broadcasted_iota(jnp.int32, (SEGS, LANES), 0)
    first = base + row * seg_len
    stream_at = jnp.full((SEGS, LANES), streams[0], jnp.int32)
    for start, stream in zip(starts, streams[1:]):
        stream_at = jnp.where(first >= start, stream, stream_at)
    for h in range(chans // LANES):
        cols = slice(h * LANES, (h + 1) * LANES)
        decay = [spread(coef_ref, r, cols) for r in range(modes)]
        for r in range(modes):
            weight_ref[r] = spread(coef_ref, 2 * modes + r, cols)
        skip = coef_ref[3 * modes :, cols]

        def step(i, carry):
            state, total = carry
            rows = step_rows(i)
            grad = wide_ref[h, rows, :]
            x = x_wide_ref[h, rows, :]
            sums = [skip * grad, None, None, None]
            new_state, new_total = [], []
            for r in range(modes):
                back = grad + state[r]
                term = weight_ref[r] * back
                sums[r % 4] = term if sums[r % 4] is None else sums[r % 4] + term
                new_total.append(total[r] + x * back)
                new_state.append(decay[r] * back)
            conv_ref[h, rows, :] = (sums[0] + sums[1]) + (sums[2] + sums[3])
            return (tuple(new_state), tuple(new_total))

        def cut(place, stream, carry):
            state, total = carry
            hold = row != place
            for r in range(modes):
                total_ref[stream, r, :, cols] += jnp.where(hold, 0.0, total[r])
            return (
                tuple(jnp.where(hold, part, 0.0) for part in state),
                tuple(jnp.where(hold, part, 0.0) for part in total),
            )

        zero = jnp.zeros((SEGS, LANES), F32)
        entry = tuple(arrive_ref[h, pl.ds(r, SEGS, stride=modes), :] for r in range(modes))
        _, total = time_loop(cuts_ref, seg_len, step, cut, (entry, (zero,) * modes))
        for s in range(2):
            for r in range(modes):
                total_ref[s, r, :, cols] += jnp.where(stream_at == s, total[r], 0.0)
    order_ref[...] = order_matrix(block_steps(tokens), False)
    from_steps(conv_ref, out_ref, order_ref)
    copy = pltpu.make_async_copy(out_ref, out_hbm, sems.at[0])
    copy.start()
    scale = coef_ref[modes : 2 * modes] / math.sqrt(window)
    for s in range(2):
        residue_ref[s] = (jnp.sum(total_ref[s], axis=1) * scale).astype(BF16)
    copy.wait()


def back_pass(doc_lengths, doc_streams, rates, coef, grad_out, x_cols, seg_leaving, later, window):
    modes, chans = rates.shape
    tokens = grad_out.shape[0]
    kinds = state_scratch(doc_lengths.shape[0], modes, tokens, chans)
    names = ("narrow", "segs", "wide", "wide", "wide", "weights", "total", "order", "cuts", "sems")

    def kernel(*refs):
        back_kernel(window, *refs)

    return call(
        kernel,
        [
            jax.ShapeDtypeStruct((tokens, chans), BF16),
            jax.ShapeDtypeStruct((2, modes, chans), BF16),
        ],
        [kinds[k] for k in names],
        "back_pass",
        cost(6 * tokens * chans * modes, 6 * tokens * chans),
        [pltpu.SMEM] * 2 + [pltpu.VMEM] * (5 + len(later)),
        [pl.ANY, pltpu.VMEM],
        (doc_lengths, doc_streams, rates, coef, grad_out, x_cols, seg_leaving, *later),
        24,
    )


def from_later(value, axis):
    count = lax.axis_size(axis)
    return [
        lax.ppermute(value, axis, [((i + k) % count, i) for i in range(count)])
        for k in range(1, count // 2 + 1)
    ]


def sum_over(value, axis):
    count = lax.axis_size(axis)
    half = count // 2
    parts = [value] + [
        lax.ppermute(value, axis, [(i, i // half * half + (i + k) % half) for i in range(count)])
        for k in range(1, half)
    ]
    parts = [part.astype(F32) for part in parts]
    while len(parts) > 1:
        middle = len(parts) // 2
        parts = [a + b for a, b in zip(parts[:middle], parts[middle:])]
    other = lax.ppermute(parts[0], axis, [(i, (i + half) % count) for i in range(count)])
    return parts[0] + other


def local(u_rows, gain, skip, residues, rates, grad_out, doc_lengths, doc_streams):
    ctx, groups = lax.axis_size("ctx"), lax.axis_size("ch")
    tokens, chans = grad_out.shape
    gain = gain[None, :]
    rates, residues = rates.T, residues.T
    x_send = norm_rows(u_rows, gain, groups)
    x_send, rates = lax.optimization_barrier((x_send, rates))
    x_cols = lax.all_to_all(x_send, "ch", split_axis=0, concat_axis=0, tiled=True)
    x_cols = x_cols.reshape(tokens, chans)
    seg_leaving, dev_leaving, coef = leave(doc_lengths, rates, residues, skip[None, :], grad_out)
    later = from_later(dev_leaving, "ctx")
    normed_grad, parts = back_pass(
        doc_lengths, doc_streams, rates, coef, grad_out, x_cols, seg_leaving, later, tokens * ctx
    )
    grad_rows = lax.all_to_all(
        normed_grad.reshape(groups, tokens // groups, chans), "ch", split_axis=0, concat_axis=0, tiled=True
    )
    residue_grad = sum_over(parts, "ctx").transpose(0, 2, 1)
    input_grad = final_rows(u_rows, gain, grad_rows)
    return (input_grad, residue_grad)


def solution(mesh):
    return jax.shard_map(
        local,
        mesh=mesh,
        in_specs=(
            P(("ctx", "ch"), None),
            P(),
            P("ch"),
            P("ch", None),
            P("ch", None),
            P("ctx", "ch"),
            P(),
            P(),
        ),
        out_specs=(P(("ctx", "ch"), None), P(None, "ch", None)),
        check_vma=False,
    )
```

time: 76 us -> 74.6 us (0.982)
  the two profiles are of different devices: /device:TPU:2 before, /device:TPU:1 now
where the time goes in v5:
time: 74.6 us; the launch traced here: 74.2 us
  starting transfers between devices  35.4 us (47%)
  Pallas kernels  23.4 us (31%)
  waiting for transfers between devices  12.7 us (17%)
  local copies, waits for them, and re-layouts  1.34 us (2%)
  between operations  0.76 us (1%)
    pallas_call x4, Pallas kernels, call(): pl.pallas_call(kernel, in_specs=[pl.BlockSpec(memory_space=space) for spa...  23.4 us
    ppermute x4, starting transfers between devices, from_later(): lax.ppermute(value, axis, [((i + k) % count, i) for i in range(count)])  11.7 us
    all_to_all x1, starting transfers between devices, local(): lax.all_to_all(normed_grad.reshape(groups, tokens // groups, chans), 'ch'...  9.51 us
    all_to_all x1, starting transfers between devices, local(): lax.all_to_all(x_send, 'ch', split_axis=0, concat_axis=0, tiled=True)  8.73 us
    ppermute x3, waiting for transfers between devices, sum_over(): lax.ppermute(value, axis, [(i, i // half * half + (i + k) % half) for i i...  4.12 us
    ppermute x1, starting transfers between devices, sum_over(): lax.ppermute(parts[0], axis, [(i, (i + half) % count) for i in range(coun...  3.92 us
    all_to_all x1, waiting for transfers between devices, local(): lax.all_to_all(normed_grad.reshape(groups, tokens // groups, chans), 'ch'...  3.55 us
    ppermute x1, waiting for transfers between devices, sum_over(): lax.ppermute(parts[0], axis, [(i, (i + half) % count) for i in range(coun...  3.12 us
  transfers between devices with their start and end apart: 10, of which 6 were waited for; matrix products, arithmetic and copies ran while one was open for 1% of the time, Pallas kernels for 7%

profile of v5, /device:TPU:1, one launch (start us, length us, event | category | flops | bytes accessed | tf_op | source)
XLA Modules:
  0.0 74.2 jit_solution(17487895783718271542)
XLA Ops:
  0.6 2.5 %norm_rows.1 = bf16[32,64,256]{2,1,0:T(8,128)(2,1)} custom-call(bf16[64,8192]{1,0:T(8,128)(2,1)} %u_ref.1, f32[1,8192]{1,0:T(1,128)} %bitcast.9), custom_call_target="tpu_custom_call" | custom-call | flops 4194304 | bytes 2097152 | tf_op jit(solution)/shard_map/norm_rows/pallas_call | solution.py:31
  3.2 0.0 copy-start.1
  3.2 0.0 copy-start.3
  3.2 0.0 copy-start.4
  3.2 8.7 %all-to-all-start = ((bf16[32,64,256]{2,1,0:T(8,128)(2,1)}), bf16[32,64,256]{2,1,0:T(8,128)(2,1)S(1)}, u32[]{:S(2)}, u32[]{:S(2)}) async-start(bf16[32,64,256]{2,1,0:T(8,128)(2,1)} %norm_rows.1), calls=%async_computation | async-start | bytes 2097152 | tf_op jit(solution)/shard_map/all_to_all | solution.py:488
  12.0 0.0 copy-start.5
  12.0 0.0 copy-start.6
  12.0 0.0 copy-done.1
  12.0 0.0 copy-done.3
  12.0 0.0 copy-done.4
  12.0 0.6 copy-done.5
  12.6 0.0 copy-done.6
  12.7 4.9 %leave.1 = (f32[2,128,128]{2,1,0:T(8,128)S(1)}, f32[16,256]{1,0:T(8,128)S(1)}, f32[56,256]{1,0:T(8,128)S(1)}) custom-call(s32[4]{0:T(128)S(1)} %copy-done.5, f32[16,256]{1,0:T(8,128)S(1)} %bitcast.11, f32[16,256]{1,0:T(8,128)S(1)} %bitcast.13, f32[1,256]{1,0:T(1,128)S(1)} %bitcast.14, bf16[2048,256]{1,0:T(8,128)(2,1)S(1)} %copy-done.1), custom_call_target="tpu_custom_call" | custom-call | flops 16777216 | bytes 1048576 | tf_op jit(solution)/shard_map/leave/pallas_call | solution.py:31
  17.5 7.0 %collective-permute-start.3 = (f32[16,256]{1,0:T(8,128)S(1)}, f32[16,256]{1,0:T(8,128)S(1)}, u32[]{:S(2)}, u32[]{:S(2)}) collective-permute-start(f32[16,256]{1,0:T(8,128)S(1)} %get-tuple-element.13), channel_id=1, source_target_pairs={{128,0},{160,32},{192,64},{224,96},{0,128},{32,160},{64,192},{96,2... | collective-permute-start | bytes 49160 | tf_op jit(solution)/shard_map/ppermute | solution.py:461
  24.5 0.0 collective-permute-start.2
  24.5 4.0 %collective-permute-start.1 = (f32[16,256]{1,0:T(8,128)S(1)}, f32[16,256]{1,0:T(8,128)S(1)}, u32[]{:S(2)}, u32[]{:S(2)}) collective-permute-start(f32[16,256]{1,0:T(8,128)S(1)} %get-tuple-element.13), channel_id=1, source_target_pairs={{64,0},{96,32},{128,64},{160,96},{192,128},{224,160},{0,192},{32,2... | collective-permute-start | bytes 49160 | tf_op jit(solution)/shard_map/ppermute | solution.py:461
  28.6 0.7 collective-permute-start
  29.3 0.0 collective-permute-done.3.refs_10_
  29.3 0.0 collective-permute-done.2.refs_9_
  29.3 0.1 collective-permute-done.1.refs_8_
  29.4 1.7 %collective-permute-done.refs_7_ = f32[16,256]{1,0:T(8,128)S(1)} collective-permute-done((f32[16,256]{1,0:T(8,128)S(1)}, f32[16,256]{1,0:T(8,128)S(1)}, u32[]{:S(2)}, u32[]{:S(2)}) %collective-permute-start) | collective-permute-done | bytes 16416 | tf_op jit(solution)/shard_map/ppermute | solution.py:461
  31.1 0.0 all-to-all-done
  31.1 0.0 copy-start.7
  31.1 0.7 copy-done.7
  31.8 14.1 %back_pass.1 = (bf16[2048,256]{1,0:T(8,128)(2,1)}, bf16[2,16,256]{2,1,0:T(8,128)(2,1)S(1)}) custom-call(s32[4]{0:T(128)S(1)} %copy-done.5, s32[4]{0:T(128)S(1)} %copy-done.7, f32[16,256]{1,0:T(8,128)S(1)} %bitcast.12, f32[56,256]{1,0:T(8,128)S(1)} %get-tuple-element.10.refs_3_, bf16[2048,256]{1,0:T(8,128)(2,1)S(1)} %copy-done.1, ...), custom_call_target="tpu_custom_call" | custom-call | flops 50331648 | bytes 3145728 | tf_op jit(solution)/shard_map/back_pass/pallas_call | solution.py:31
  45.9 0.0 copy-start
  45.9 9.5 %all-to-all-start.1 = ((bf16[32,64,256]{2,1,0:T(8,128)(2,1)}), bf16[32,64,256]{2,1,0:T(8,128)(2,1)S(1)}, u32[]{:S(2)}, u32[]{:S(2)}) async-start(bf16[32,64,256]{2,1,0:T(8,128)(2,1)} %bitcast.5), calls=%async_computation.1 | async-start | bytes 2097152 | tf_op jit(solution)/shard_map/all_to_all | solution.py:495
  55.4 1.0 %collective-permute-start.6 = (bf16[2,16,256]{2,1,0:T(8,128)(2,1)S(1)}, bf16[2,16,256]{2,1,0:T(8,128)(2,1)S(1)}, u32[]{:S(2)}, u32[]{:S(2)}) collective-permute-start(bf16[2,16,256]{2,1,0:T(8,128)(2,1)S(1)} %get-tuple-element.15), channel_id=1, source_target_pairs={{0,96},{32,0},{64,32},{96,64},{128,224},{160,128},{192,160},{224,1... | collective-permute-start | bytes 49160 | tf_op jit(solution)/shard_map/ppermute | solution.py:470
  56.4 0.6 collective-permute-start.5
  57.0 0.0 collective-permute-start.4
  57.0 1.4 %collective-permute-done.6 = bf16[2,16,256]{2,1,0:T(8,128)(2,1)S(1)} collective-permute-done((bf16[2,16,256]{2,1,0:T(8,128)(2,1)S(1)}, bf16[2,16,256]{2,1,0:T(8,128)(2,1)S(1)}, u32[]{:S(2)}, u32[]{:S(2)}) %collective-permute-start.6) | collective-permute-done | bytes 16416 | tf_op jit(solution)/shard_map/ppermute | solution.py:470
  58.4 2.7 %collective-permute-done.5 = bf16[2,16,256]{2,1,0:T(8,128)(2,1)S(1)} collective-permute-done((bf16[2,16,256]{2,1,0:T(8,128)(2,1)S(1)}, bf16[2,16,256]{2,1,0:T(8,128)(2,1)S(1)}, u32[]{:S(2)}, u32[]{:S(2)}) %collective-permute-start.5) | collective-permute-done | bytes 16416 | tf_op jit(solution)/shard_map/ppermute | solution.py:470
  61.1 0.0 collective-permute-done.4
  61.1 0.0 copy-start.2
  61.1 3.9 %collective-permute-start.7 = (f32[2,16,256]{2,1,0:T(8,128)S(1)}, f32[2,16,256]{2,1,0:T(8,128)S(1)}, u32[]{:S(2)}, u32[]{:S(2)}) collective-permute-start(f32[2,16,256]{2,1,0:T(8,128)S(1)} %add_add_fusion), channel_id=1, source_target_pairs={{0,128},{32,160},{64,192},{96,224},{128,0},{160,32},{192,64},{224,... | collective-permute-start | bytes 98312 | tf_op jit(solution)/shard_map/ppermute | solution.py:477
  65.0 3.1 %collective-permute-done.7 = f32[2,16,256]{2,1,0:T(8,128)S(1)} collective-permute-done((f32[2,16,256]{2,1,0:T(8,128)S(1)}, f32[2,16,256]{2,1,0:T(8,128)S(1)}, u32[]{:S(2)}, u32[]{:S(2)}) %collective-permute-start.7) | collective-permute-done | bytes 32800 | tf_op jit(solution)/shard_map/ppermute | solution.py:477
  68.2 0.6 add_bitcast_fusion
  68.8 3.6 %all-to-all-done.1.grad_ref = bf16[32,64,256]{2,1,0:T(8,128)(2,1)S(1)} async-done(((bf16[32,64,256]{2,1,0:T(8,128)(2,1)}), bf16[32,64,256]{2,1,0:T(8,128)(2,1)S(1)}, u32[]{:S(2)}, u32[]{:S(2)}) %all-to-all-start.1) | async-done | bytes 1048608 | tf_op jit(solution)/shard_map/all_to_all | solution.py:495
  72.3 0.0 copy-done
  72.3 0.0 copy-done.2
  72.3 1.9 %final_rows.1 = bf16[64,8192]{1,0:T(8,128)(2,1)} custom-call(bf16[64,8192]{1,0:T(8,128)(2,1)S(1)} %copy-done, f32[1,8192]{1,0:T(1,128)S(1)} %bitcast.10, bf16[32,64,256]{2,1,0:T(8,128)(2,1)S(1)} %all-to-all-done.1.grad_ref), custom_call_target="tpu_custom_call" | custom-call | flops 8388608 | bytes 3145728 | tf_op jit(solution)/shard_map/final_rows/pallas_call | solution.py:31
  (1 shorter events, 0.0 us)
Async XLA Ops:
  3.2 8.8 %copy-start.1 = (bf16[2048,256]{1,0:T(8,128)(2,1)S(1)}, bf16[2048,256]{1,0:T(8,128)(2,1)}, u32[]{:S(2)}) copy-start(bf16[2048,256]{1,0:T(8,128)(2,1)} %refs_4_.1) | copy-start | bytes 3145732
  3.2 8.8 %copy-start.3 = (f32[256,16]{0,1:T(8,128)S(1)}, f32[256,16]{0,1:T(8,128)}, u32[]{:S(2)}) copy-start(f32[256,16]{0,1:T(8,128)} %param.12) | copy-start | bytes 49156
  3.2 8.8 %copy-start.4 = (f32[256,16]{0,1:T(8,128)S(1)}, f32[256,16]{0,1:T(8,128)}, u32[]{:S(2)}) copy-start(f32[256,16]{0,1:T(8,128)} %param.11) | copy-start | bytes 49156
  3.2 27.9 %all-to-all-start = ((bf16[32,64,256]{2,1,0:T(8,128)(2,1)}), bf16[32,64,256]{2,1,0:T(8,128)(2,1)S(1)}, u32[]{:S(2)}, u32[]{:S(2)}) async-start(bf16[32,64,256]{2,1,0:T(8,128)(2,1)} %norm_rows.1), calls=%async_computation | async-start | bytes 2097152 | tf_op jit(solution)/shard_map/all_to_all | solution.py:488
  12.0 0.7 copy-start.5
  12.0 0.7 copy-start.6
  17.5 11.7 %collective-permute-start.3 = (f32[16,256]{1,0:T(8,128)S(1)}, f32[16,256]{1,0:T(8,128)S(1)}, u32[]{:S(2)}, u32[]{:S(2)}) collective-permute-start(f32[16,256]{1,0:T(8,128)S(1)} %get-tuple-element.13), channel_id=1, source_target_pairs={{128,0},{160,32},{192,64},{224,96},{0,128},{32,160},{64,192},{96,2... | collective-permute-start | bytes 49160 | tf_op jit(solution)/shard_map/ppermute | solution.py:461
  24.5 4.7 %collective-permute-start.2 = (f32[16,256]{1,0:T(8,128)S(1)}, f32[16,256]{1,0:T(8,128)S(1)}, u32[]{:S(2)}, u32[]{:S(2)}) collective-permute-start(f32[16,256]{1,0:T(8,128)S(1)} %get-tuple-element.13), channel_id=1, source_target_pairs={{96,0},{128,32},{160,64},{192,96},{224,128},{0,160},{32,192},{64,2... | collective-permute-start | bytes 49160 | tf_op jit(solution)/shard_map/ppermute | solution.py:461
  24.5 4.9 %collective-permute-start.1 = (f32[16,256]{1,0:T(8,128)S(1)}, f32[16,256]{1,0:T(8,128)S(1)}, u32[]{:S(2)}, u32[]{:S(2)}) collective-permute-start(f32[16,256]{1,0:T(8,128)S(1)} %get-tuple-element.13), channel_id=1, source_target_pairs={{64,0},{96,32},{128,64},{160,96},{192,128},{224,160},{0,192},{32,2... | collective-permute-start | bytes 49160 | tf_op jit(solution)/shard_map/ppermute | solution.py:461
  28.6 2.6 %collective-permute-start = (f32[16,256]{1,0:T(8,128)S(1)}, f32[16,256]{1,0:T(8,128)S(1)}, u32[]{:S(2)}, u32[]{:S(2)}) collective-permute-start(f32[16,256]{1,0:T(8,128)S(1)} %get-tuple-element.13), channel_id=1, source_target_pairs={{32,0},{64,32},{96,64},{128,96},{160,128},{192,160},{224,192},{0,2... | collective-permute-start | bytes 49160 | tf_op jit(solution)/shard_map/ppermute | solution.py:461
  31.1 0.7 copy-start.7
  45.9 26.4 %copy-start = (bf16[64,8192]{1,0:T(8,128)(2,1)S(1)}, bf16[64,8192]{1,0:T(8,128)(2,1)}, u32[]{:S(2)}) copy-start(bf16[64,8192]{1,0:T(8,128)(2,1)} %u_ref.1) | copy-start | bytes 3145732
  45.9 26.4 %all-to-all-start.1 = ((bf16[32,64,256]{2,1,0:T(8,128)(2,1)}), bf16[32,64,256]{2,1,0:T(8,128)(2,1)S(1)}, u32[]{:S(2)}, u32[]{:S(2)}) async-start(bf16[32,64,256]{2,1,0:T(8,128)(2,1)} %bitcast.5), calls=%async_computation.1 | async-start | bytes 2097152 | tf_op jit(solution)/shard_map/all_to_all | solution.py:495
  55.4 3.0 %collective-permute-start.6 = (bf16[2,16,256]{2,1,0:T(8,128)(2,1)S(1)}, bf16[2,16,256]{2,1,0:T(8,128)(2,1)S(1)}, u32[]{:S(2)}, u32[]{:S(2)}) collective-permute-start(bf16[2,16,256]{2,1,0:T(8,128)(2,1)S(1)} %get-tuple-element.15), channel_id=1, source_target_pairs={{0,96},{32,0},{64,32},{96,64},{128,224},{160,128},{192,160},{224,1... | collective-permute-start | bytes 49160 | tf_op jit(solution)/shard_map/ppermute | solution.py:470
  56.4 4.7 %collective-permute-start.5 = (bf16[2,16,256]{2,1,0:T(8,128)(2,1)S(1)}, bf16[2,16,256]{2,1,0:T(8,128)(2,1)S(1)}, u32[]{:S(2)}, u32[]{:S(2)}) collective-permute-start(bf16[2,16,256]{2,1,0:T(8,128)(2,1)S(1)} %get-tuple-element.15), channel_id=1, source_target_pairs={{0,32},{32,64},{64,96},{96,0},{128,160},{160,192},{192,224},{224,1... | collective-permute-start | bytes 49160 | tf_op jit(solution)/shard_map/ppermute | solution.py:470
  57.0 4.1 %collective-permute-start.4 = (bf16[2,16,256]{2,1,0:T(8,128)(2,1)S(1)}, bf16[2,16,256]{2,1,0:T(8,128)(2,1)S(1)}, u32[]{:S(2)}, u32[]{:S(2)}) collective-permute-start(bf16[2,16,256]{2,1,0:T(8,128)(2,1)S(1)} %get-tuple-element.15), channel_id=1, source_target_pairs={{0,64},{32,96},{64,0},{96,32},{128,192},{160,224},{192,128},{224,1... | collective-permute-start | bytes 49160 | tf_op jit(solution)/shard_map/ppermute | solution.py:470
  61.1 11.2 %copy-start.2 = (f32[8192]{0:T(1024)S(1)}, f32[8192]{0:T(1024)}, u32[]{:S(2)}) copy-start(f32[8192]{0:T(1024)} %param.9) | copy-start | bytes 98308
  61.1 7.0 %collective-permute-start.7 = (f32[2,16,256]{2,1,0:T(8,128)S(1)}, f32[2,16,256]{2,1,0:T(8,128)S(1)}, u32[]{:S(2)}, u32[]{:S(2)}) collective-permute-start(f32[2,16,256]{2,1,0:T(8,128)S(1)} %add_add_fusion), channel_id=1, source_target_pairs={{0,128},{32,160},{64,192},{96,224},{128,0},{160,32},{192,64},{224,... | collective-permute-start | bytes 98312 | tf_op jit(solution)/shard_map/ppermute | solution.py:477

commit v6 on v5

--- a/solution.py
+++ b/solution.py
@@ -11,7 +11,7 @@
 BF16 = jnp.bfloat16
 SEGS = 8
 LANES = 128
-UNROLL = 8
+UNROLL = 16
 STEPS = 32
 ROW_BLOCK = 16
 
@@ -270,7 +270,7 @@
 
 
 def leave_kernel(
-    lens_ref, rates_ref, residues_ref, skip_ref, grad_ref, seg_ref, dev_ref, coef_ref,
+    lens_ref, streams_ref, rates_ref, residues_ref, skip_ref, grad_ref, seg_ref, dev_ref, coef_ref,
     wide_ref, order_ref, cuts_ref,
 ):
     tokens, chans = grad_ref.shape
@@ -278,7 +278,8 @@
     seg_len = tokens // SEGS
     base = lax.axis_index("ctx") * tokens
     starts = doc_starts(lens_ref)
-    store_cuts(cuts_ref, cut_codes(starts, [0] * len(starts), base, seg_len))
+    streams = [streams_ref[k] for k in range(len(starts) + 1)]
+    store_cuts(cuts_ref, cut_codes(starts, streams[1:], base, seg_len))
     order_ref[...] = order_matrix(block_steps(tokens), True)
     to_steps(grad_ref, wide_ref, order_ref)
     rates = rates_ref[...]
@@ -320,14 +321,12 @@
         "narrow": pltpu.VMEM((tokens, chans), BF16),
         "wide": pltpu.VMEM((halves, tokens, LANES), F32),
         "order": pltpu.VMEM((size, size), BF16),
-        "segs": pltpu.VMEM((halves, SEGS * modes, LANES), F32),
-        "weights": pltpu.VMEM((modes, SEGS, LANES), F32),
         "total": pltpu.VMEM((2, modes, SEGS, chans), F32),
         "sems": pltpu.SemaphoreType.DMA((1,)),
     }
 
 
-def leave(doc_lengths, rates, residues, skip, grad_out):
+def leave(doc_lengths, doc_streams, rates, residues, skip, grad_out):
     modes, chans = rates.shape
     tokens = grad_out.shape[0]
     kinds = state_scratch(doc_lengths.shape[0], modes, tokens, chans)
@@ -341,16 +340,15 @@
         [kinds[k] for k in ("wide", "order", "cuts")],
         "leave",
         cost(2 * tokens * chans * modes, 2 * tokens * chans),
-        [pltpu.SMEM] + [pltpu.VMEM] * 4,
+        [pltpu.SMEM] * 2 + [pltpu.VMEM] * 4,
         [pltpu.VMEM] * 3,
-        (doc_lengths, rates, residues, skip, grad_out),
-    )
-
-
-def back_kernel(window, lens_ref, streams_ref, rates_ref, coef_ref, grad_ref, x_ref, seg_ref, *refs):
-    later = refs[:-12]
-    (out_hbm, residue_ref, out_ref, arrive_ref, wide_ref, x_wide_ref, conv_ref, weight_ref, total_ref,
-     order_ref, cuts_ref, sems) = refs[-12:]
+        (doc_lengths, doc_streams, rates, residues, skip, grad_out),
+    )
+
+
+def back_kernel(lens_ref, streams_ref, rates_ref, coef_ref, grad_ref, seg_ref, *refs):
+    later = refs[:-8]
+    out_hbm, arrive_ref, out_ref, wide_ref, conv_ref, order_ref, cuts_ref, sems = refs[-8:]
     tokens, chans = grad_ref.shape
     modes = rates_ref.shape[0]
     seg_len = tokens // SEGS
@@ -374,6 +372,71 @@
         put_segment(arrive_ref, s - 1, modes, arriving)
     order_ref[...] = order_matrix(block_steps(tokens), True)
     to_steps(grad_ref, wide_ref, order_ref)
+    row = lax.broadcasted_iota(jnp.int32, (SEGS, LANES), 0)
+    for h in range(chans // LANES):
+        cols = slice(h * LANES, (h + 1) * LANES)
+        decay = [spread(coef_ref, r, cols) for r in range(modes)]
+        weight = [spread(coef_ref, 2 * modes + r, cols) for r in range(modes)]
+        skip = coef_ref[3 * modes :, cols]
+
+        def step(i, state):
+            rows = step_rows(i)
+            grad = wide_ref[h, rows, :]
+            sums = [skip * grad, None, None, None]
+            new_state = []
+            for r in range(modes):
+                back = grad + state[r]
+                term = weight[r] * back
+                sums[r % 4] = term if sums[r % 4] is None else sums[r % 4] + term
+                new_state.append(decay[r] * back)
+            conv_ref[h, rows, :] = (sums[0] + sums[1]) + (sums[2] + sums[3])
+            return tuple(new_state)
+
+        def cut(place, stream, state):
+            hold = row != place
+            return tuple(jnp.where(hold, part, 0.0) for part in state)
+
+        entry = tuple(arrive_ref[h, pl.ds(r, SEGS, stride=modes), :] for r in range(modes))
+        time_loop(cuts_ref, seg_len, step, cut, entry)
+    order_ref[...] = order_matrix(block_steps(tokens), False)
+    from_steps(conv_ref, out_ref, order_ref)
+    copy = pltpu.make_async_copy(out_ref, out_hbm, sems.at[0])
+    copy.start()
+    copy.wait()
+
+
+def back_pass(doc_lengths, doc_streams, rates, coef, grad_out, seg_leaving, later):
+    modes, chans = rates.shape
+    tokens = grad_out.shape[0]
+    kinds = state_scratch(doc_lengths.shape[0], modes, tokens, chans)
+    return call(
+        back_kernel,
+        [
+            jax.ShapeDtypeStruct((tokens, chans), BF16),
+            jax.ShapeDtypeStruct((chans // LANES, SEGS * modes, LANES), F32),
+        ],
+        [kinds[k] for k in ("narrow", "wide", "wide", "order", "cuts", "sems")],
+        "back_pass",
+        cost(4 * tokens * chans * modes, 4 * tokens * chans),
+        [pltpu.SMEM] * 2 + [pltpu.VMEM] * (4 + len(later)),
+        [pl.ANY, pltpu.VMEM],
+        (doc_lengths, doc_streams, rates, coef, grad_out, seg_leaving, *later),
+    )
+
+
+def residue_kernel(
+    window, lens_ref, streams_ref, coef_ref, grad_ref, x_ref, arrive_ref, residue_ref,
+    wide_ref, x_wide_ref, total_ref, order_ref, cuts_ref,
+):
+    tokens, chans = grad_ref.shape
+    modes = residue_ref.shape[1]
+    seg_len = tokens // SEGS
+    base = lax.axis_index("ctx") * tokens
+    starts = doc_starts(lens_ref)
+    streams = [streams_ref[k] for k in range(len(starts) + 1)]
+    store_cuts(cuts_ref, cut_codes(starts, streams[1:], base, seg_len))
+    order_ref[...] = order_matrix(block_steps(tokens), True)
+    to_steps(grad_ref, wide_ref, order_ref)
     to_steps(x_ref, x_wide_ref, order_ref)
     total_ref[...] = jnp.zeros_like(total_ref)
     row = lax.broadcasted_iota(jnp.int32, (SEGS, LANES), 0)
@@ -384,25 +447,15 @@
     for h in range(chans // LANES):
         cols = slice(h * LANES, (h + 1) * LANES)
         decay = [spread(coef_ref, r, cols) for r in range(modes)]
-        for r in range(modes):
-            weight_ref[r] = spread(coef_ref, 2 * modes + r, cols)
-        skip = coef_ref[3 * modes :, cols]
 
         def step(i, carry):
             state, total = carry
             rows = step_rows(i)
             grad = wide_ref[h, rows, :]
             x = x_wide_ref[h, rows, :]
-            sums = [skip * grad, None, None, None]
-            new_state, new_total = [], []
-            for r in range(modes):
-                back = grad + state[r]
-                term = weight_ref[r] * back
-                sums[r % 4] = term if sums[r % 4] is None else sums[r % 4] + term
-                new_total.append(total[r] + x * back)
-                new_state.append(decay[r] * back)
-            conv_ref[h, rows, :] = (sums[0] + sums[1]) + (sums[2] + sums[3])
-            return (tuple(new_state), tuple(new_total))
+            back = [grad + part for part in state]
+            total = tuple(total[r] + x * back[r] for r in range(modes))
+            return (tuple(decay[r] * back[r] for r in range(modes)), total)
 
         def cut(place, stream, carry):
             state, total = carry
@@ -420,39 +473,29 @@
         for s in range(2):
             for r in range(modes):
                 total_ref[s, r, :, cols] += jnp.where(stream_at == s, total[r], 0.0)
-    order_ref[...] = order_matrix(block_steps(tokens), False)
-    from_steps(conv_ref, out_ref, order_ref)
-    copy = pltpu.make_async_copy(out_ref, out_hbm, sems.at[0])
-    copy.start()
     scale = coef_ref[modes : 2 * modes] / math.sqrt(window)
     for s in range(2):
         residue_ref[s] = (jnp.sum(total_ref[s], axis=1) * scale).astype(BF16)
-    copy.wait()
-
-
-def back_pass(doc_lengths, doc_streams, rates, coef, grad_out, x_cols, seg_leaving, later, window):
-    modes, chans = rates.shape
-    tokens = grad_out.shape[0]
+
+
+def residue_pass(doc_lengths, doc_streams, coef, grad_out, x_cols, arriving, window):
+    tokens, chans = grad_out.shape
+    modes = arriving.shape[1] // SEGS
     kinds = state_scratch(doc_lengths.shape[0], modes, tokens, chans)
-    names = ("narrow", "segs", "wide", "wide", "wide", "weights", "total", "order", "cuts", "sems")
 
     def kernel(*refs):
-        back_kernel(window, *refs)
+        residue_kernel(window, *refs)
 
     return call(
         kernel,
-        [
-            jax.ShapeDtypeStruct((tokens, chans), BF16),
-            jax.ShapeDtypeStruct((2, modes, chans), BF16),
-        ],
-        [kinds[k] for k in names],
-        "back_pass",
-        cost(6 * tokens * chans * modes, 6 * tokens * chans),
-        [pltpu.SMEM] * 2 + [pltpu.VMEM] * (5 + len(later)),
-        [pl.ANY, pltpu.VMEM],
-        (doc_lengths, doc_streams, rates, coef, grad_out, x_cols, seg_leaving, *later),
-        24,
-    )
+        [jax.ShapeDtypeStruct((2, modes, chans), BF16)],
+        [kinds[k] for k in ("wide", "wide", "total", "order", "cuts")],
+        "residue_pass",
+        cost(4 * tokens * chans * modes, 4 * tokens * chans),
+        [pltpu.SMEM] * 2 + [pltpu.VMEM] * 4,
+        [pltpu.VMEM],
+        (doc_lengths, doc_streams, coef, grad_out, x_cols, arriving),
+    )[0]
 
 
 def from_later(value, axis):
@@ -487,14 +530,18 @@
     x_send, rates = lax.optimization_barrier((x_send, rates))
     x_cols = lax.all_to_all(x_send, "ch", split_axis=0, concat_axis=0, tiled=True)
     x_cols = x_cols.reshape(tokens, chans)
-    seg_leaving, dev_leaving, coef = leave(doc_lengths, rates, residues, skip[None, :], grad_out)
+    seg_leaving, dev_leaving, coef = leave(
+        doc_lengths, doc_streams, rates, residues, skip[None, :], grad_out
+    )
     later = from_later(dev_leaving, "ctx")
-    normed_grad, parts = back_pass(
-        doc_lengths, doc_streams, rates, coef, grad_out, x_cols, seg_leaving, later, tokens * ctx
+    x_cols, *later = lax.optimization_barrier((x_cols, *later))
+    normed_grad, arriving = back_pass(
+        doc_lengths, doc_streams, rates, coef, grad_out, seg_leaving, later
     )
     grad_rows = lax.all_to_all(
         normed_grad.reshape(groups, tokens // groups, chans), "ch", split_axis=0, concat_axis=0, tiled=True
     )
+    parts = residue_pass(doc_lengths, doc_streams, coef, grad_out, x_cols, arriving, tokens * ctx)
     residue_grad = sum_over(parts, "ctx").transpose(0, 2, 1)
     input_grad = final_rows(u_rows, gain, grad_rows)
     return (input_grad, residue_grad)

time: 74.6 us -> 77.7 us (1.042)
  the two profiles are of different devices: /device:TPU:1 before, /device:TPU:2 now
where the time goes in v6:
time: 77.7 us; the launch traced here: 77.3 us
  starting transfers between devices  34.9 us (45%)
  Pallas kernels  26.8 us (34%)
  waiting for transfers between devices  11.4 us (15%)
  local copies, waits for them, and re-layouts  2.84 us (4%)
  between operations  0.8 us (1%)
    pallas_call x5, Pallas kernels, call(): pl.pallas_call(kernel, in_specs=[pl.BlockSpec(memory_space=space) for spa...  26.8 us
    ppermute x4, starting transfers between devices, from_later(): lax.ppermute(value, axis, [((i + k) % count, i) for i in range(count)])  12.9 us
    all_to_all x1, starting transfers between devices, local(): lax.all_to_all(x_send, 'ch', split_axis=0, concat_axis=0, tiled=True)  7.77 us
    all_to_all x1, starting transfers between devices, local(): lax.all_to_all(normed_grad.reshape(groups, tokens // groups, chans), 'ch'...  7.37 us
    ppermute x3, waiting for transfers between devices, sum_over(): lax.ppermute(value, axis, [(i, i // half * half + (i + k) % half) for i i...  4.88 us
    ppermute x1, starting transfers between devices, sum_over(): lax.ppermute(parts[0], axis, [(i, (i + half) % count) for i in range(coun...  4.23 us
    ppermute x1, waiting for transfers between devices, sum_over(): lax.ppermute(parts[0], axis, [(i, (i + half) % count) for i in range(coun...  3.68 us
    unnamed x22, local copies, waits for them, and re-layouts  2.84 us
  transfers between devices with their start and end apart: 10, of which 5 were waited for; matrix products, arithmetic and copies ran while one was open for 1% of the time, Pallas kernels for 18%

profile of v6, /device:TPU:2, one launch (start us, length us, event | category | flops | bytes accessed | tf_op | source)
XLA Modules:
  0.0 77.3 jit_solution(5435870035865231331)
XLA Ops:
  0.6 2.5 %norm_rows.1 = bf16[32,64,256]{2,1,0:T(8,128)(2,1)} custom-call(bf16[64,8192]{1,0:T(8,128)(2,1)} %u_ref.1, f32[1,8192]{1,0:T(1,128)} %bitcast.10), custom_call_target="tpu_custom_call" | custom-call | flops 4194304 | bytes 2097152 | tf_op jit(solution)/shard_map/norm_rows/pallas_call | solution.py:31
  3.2 0.0 copy-start
  3.2 0.0 copy-start.6
  3.2 0.0 copy-start.7
  3.2 0.0 copy-start.10
  3.2 7.8 %all-to-all-start = ((bf16[32,64,256]{2,1,0:T(8,128)(2,1)}), bf16[32,64,256]{2,1,0:T(8,128)(2,1)S(1)}, u32[]{:S(2)}, u32[]{:S(2)}) async-start(bf16[32,64,256]{2,1,0:T(8,128)(2,1)} %norm_rows.1), calls=%async_computation | async-start | bytes 2097152 | tf_op jit(solution)/shard_map/all_to_all | solution.py:531
  11.0 0.0 copy-start.8
  11.0 0.0 copy-start.9
  11.0 0.0 copy-done
  11.0 0.0 copy-done.6
  11.0 0.0 copy-done.7
  11.1 0.0 copy-done.10
  11.1 0.6 copy-done.8
  11.7 0.0 copy-done.9
  11.7 4.8 %leave.1 = (f32[2,128,128]{2,1,0:T(8,128)S(1)}, f32[16,256]{1,0:T(8,128)S(1)}, f32[56,256]{1,0:T(8,128)S(1)}) custom-call(s32[4]{0:T(128)S(1)} %copy-done.8, s32[4]{0:T(128)S(1)} %copy-done.9, f32[16,256]{1,0:T(8,128)S(1)} %bitcast.12, f32[16,256]{1,0:T(8,128)S(1)} %bitcast.14, f32[1,256]{1,0:T(1,128)S(1)} %bitcast.15, bf16[2048,256]{1,0:T(8,128)(2,1)S(1)} %copy-done), custom_call_target="tpu_custom_call" | custom-call | flops 16777216 | bytes 1048576 | tf_op jit(solution)/shard_map/leave/pallas_call | solution.py:31
  16.4 7.3 %collective-permute-start.3 = (f32[16,256]{1,0:T(8,128)S(1)}, f32[16,256]{1,0:T(8,128)S(1)}, u32[]{:S(2)}, u32[]{:S(2)}) collective-permute-start(f32[16,256]{1,0:T(8,128)S(1)} %get-tuple-element.18), channel_id=1, source_target_pairs={{128,0},{160,32},{192,64},{224,96},{0,128},{32,160},{64,192},{96,2... | collective-permute-start | bytes 49160 | tf_op jit(solution)/shard_map/ppermute | solution.py:504
  23.7 0.0 collective-permute-start.2
  23.7 4.7 %collective-permute-start.1 = (f32[16,256]{1,0:T(8,128)S(1)}, f32[16,256]{1,0:T(8,128)S(1)}, u32[]{:S(2)}, u32[]{:S(2)}) collective-permute-start(f32[16,256]{1,0:T(8,128)S(1)} %get-tuple-element.18), channel_id=1, source_target_pairs={{64,0},{96,32},{128,64},{160,96},{192,128},{224,160},{0,192},{32,2... | collective-permute-start | bytes 49160 | tf_op jit(solution)/shard_map/ppermute | solution.py:504
  28.4 0.9 %collective-permute-start = (f32[16,256]{1,0:T(8,128)S(1)}, f32[16,256]{1,0:T(8,128)S(1)}, u32[]{:S(2)}, u32[]{:S(2)}) collective-permute-start(f32[16,256]{1,0:T(8,128)S(1)} %get-tuple-element.18), channel_id=1, source_target_pairs={{32,0},{64,32},{96,64},{128,96},{160,128},{192,160},{224,192},{0,2... | collective-permute-start | bytes 49160 | tf_op jit(solution)/shard_map/ppermute | solution.py:504
  29.3 0.0 collective-permute-done.3.refs_3_
  29.3 0.0 collective-permute-done.2.refs_2_
  29.3 0.5 collective-permute-done.1.refs_1_
  29.8 2.3 %collective-permute-done.refs_0_ = f32[16,256]{1,0:T(8,128)S(1)} collective-permute-done((f32[16,256]{1,0:T(8,128)S(1)}, f32[16,256]{1,0:T(8,128)S(1)}, u32[]{:S(2)}, u32[]{:S(2)}) %collective-permute-start) | collective-permute-done | bytes 16416 | tf_op jit(solution)/shard_map/ppermute | solution.py:504
  32.1 0.0 all-to-all-done
  32.1 0.0 copy-start.2
  32.1 8.8 %back_pass.1 = (bf16[2048,256]{1,0:T(8,128)(2,1)S(1)}, f32[2,128,128]{2,1,0:T(8,128)S(1)}) custom-call(s32[4]{0:T(128)S(1)} %copy-done.8, s32[4]{0:T(128)S(1)} %copy-done.9, f32[16,256]{1,0:T(8,128)S(1)} %bitcast.13, f32[56,256]{1,0:T(8,128)S(1)} %get-tuple-element.15.coef_ref.refs_2_, bf16[2048,256]{1,0:T(8,128)(2,1)S(1)} %copy-done, ...), custom_call_target="tpu_custom_call" | custom-call | flops 33554432 | bytes 2097152 | tf_op jit(solution)/shard_map/back_pass/pallas_call | solution.py:31
  41.0 0.0 copy-start.4
  41.0 1.0 %copy-done.4 = bf16[2048,256]{1,0:T(8,128)(2,1)} copy-done((bf16[2048,256]{1,0:T(8,128)(2,1)}, bf16[2048,256]{1,0:T(8,128)(2,1)S(1)}, u32[]{:S(2)}) %copy-start.4) | copy-done | bytes 1048600
  41.9 0.0 copy-done.2
  41.9 7.4 %all-to-all-start.1 = ((bf16[32,64,256]{2,1,0:T(8,128)(2,1)}), bf16[32,64,256]{2,1,0:T(8,128)(2,1)S(1)}, u32[]{:S(2)}, u32[]{:S(2)}) async-start(bf16[32,64,256]{2,1,0:T(8,128)(2,1)} %bitcast.9), calls=%async_computation.1 | async-start | bytes 2097152 | tf_op jit(solution)/shard_map/all_to_all | solution.py:541
  49.3 0.0 copy-start.3
  49.3 1.2 %copy-done.3 = bf16[32,64,256]{2,1,0:T(8,128)(2,1)S(1)} copy-done((bf16[32,64,256]{2,1,0:T(8,128)(2,1)S(1)}, bf16[32,64,256]{2,1,0:T(8,128)(2,1)}, u32[]{:S(2)}) %copy-start.3) | copy-done | bytes 1048600
  50.5 0.0 copy-start.1
  50.5 8.9 %residue_pass.1 = bf16[2,16,256]{2,1,0:T(8,128)(2,1)S(1)} custom-call(s32[4]{0:T(128)S(1)} %copy-done.8, s32[4]{0:T(128)S(1)} %copy-done.9, f32[56,256]{1,0:T(8,128)S(1)} %get-tuple-element.15.coef_ref.refs_2_, bf16[2048,256]{1,0:T(8,128)(2,1)S(1)} %copy-done, bf16[2048,256]{1,0:T(8,128)(2,1)S(1)} %bitcast.8, f32[2,128,128]{2,1,0:T(8,128)S(1)} %get-tuple-element.25.refs_5_), custom_call_target="tpu_custom_call" | custom-call | flops 33554432 | bytes 2097152 | tf_op jit(solution)/shard_map/residue_pass/pallas_call | solution.py:31
  59.4 2.0 %collective-permute-start.6 = (bf16[2,16,256]{2,1,0:T(8,128)(2,1)S(1)}, bf16[2,16,256]{2,1,0:T(8,128)(2,1)S(1)}, u32[]{:S(2)}, u32[]{:S(2)}) collective-permute-start(bf16[2,16,256]{2,1,0:T(8,128)(2,1)S(1)} %residue_pass.1), channel_id=1, source_target_pairs={{0,96},{32,0},{64,32},{96,64},{128,224},{160,128},{192,160},{224,1... | collective-permute-start | bytes 49160 | tf_op jit(solution)/shard_map/ppermute | solution.py:513
  61.4 0.1 collective-permute-start.5
  61.5 0.5 collective-permute-start.4
  62.0 1.2 %collective-permute-done.6 = bf16[2,16,256]{2,1,0:T(8,128)(2,1)S(1)} collective-permute-done((bf16[2,16,256]{2,1,0:T(8,128)(2,1)S(1)}, bf16[2,16,256]{2,1,0:T(8,128)(2,1)S(1)}, u32[]{:S(2)}, u32[]{:S(2)}) %collective-permute-start.6) | collective-permute-done | bytes 16416 | tf_op jit(solution)/shard_map/ppermute | solution.py:513
  63.2 3.7 %collective-permute-done.5 = bf16[2,16,256]{2,1,0:T(8,128)(2,1)S(1)} collective-permute-done((bf16[2,16,256]{2,1,0:T(8,128)(2,1)S(1)}, bf16[2,16,256]{2,1,0:T(8,128)(2,1)S(1)}, u32[]{:S(2)}, u32[]{:S(2)}) %collective-permute-start.5) | collective-permute-done | bytes 16416 | tf_op jit(solution)/shard_map/ppermute | solution.py:513
  66.9 0.0 collective-permute-done.4
  66.9 0.0 copy-start.5
  66.9 4.2 %collective-permute-start.7 = (f32[2,16,256]{2,1,0:T(8,128)S(1)}, f32[2,16,256]{2,1,0:T(8,128)S(1)}, u32[]{:S(2)}, u32[]{:S(2)}) collective-permute-start(f32[2,16,256]{2,1,0:T(8,128)S(1)} %add_add_fusion), channel_id=1, source_target_pairs={{0,128},{32,160},{64,192},{96,224},{128,0},{160,32},{192,64},{224,... | collective-permute-start | bytes 98312 | tf_op jit(solution)/shard_map/ppermute | solution.py:520
  71.2 3.7 %collective-permute-done.7 = f32[2,16,256]{2,1,0:T(8,128)S(1)} collective-permute-done((f32[2,16,256]{2,1,0:T(8,128)S(1)}, f32[2,16,256]{2,1,0:T(8,128)S(1)}, u32[]{:S(2)}, u32[]{:S(2)}) %collective-permute-start.7) | collective-permute-done | bytes 32800 | tf_op jit(solution)/shard_map/ppermute | solution.py:520
  74.8 0.6 add_bitcast_fusion
  75.5 0.0 all-to-all-done.1.grad_ref
  75.5 0.0 copy-done.1
  75.5 0.0 copy-done.5
  75.5 1.9 %final_rows.1 = bf16[64,8192]{1,0:T(8,128)(2,1)} custom-call(bf16[64,8192]{1,0:T(8,128)(2,1)S(1)} %copy-done.1, f32[1,8192]{1,0:T(1,128)S(1)} %bitcast.11, bf16[32,64,256]{2,1,0:T(8,128)(2,1)S(1)} %all-to-all-done.1.grad_ref), custom_call_target="tpu_custom_call" | custom-call | flops 8388608 | bytes 3145728 | tf_op jit(solution)/shard_map/final_rows/pallas_call | solution.py:31
  (1 shorter events, 0.0 us)
Async XLA Ops:
  3.2 7.8 %copy-start = (bf16[2048,256]{1,0:T(8,128)(2,1)S(1)}, bf16[2048,256]{1,0:T(8,128)(2,1)}, u32[]{:S(2)}) copy-start(bf16[2048,256]{1,0:T(8,128)(2,1)} %refs_3_.1) | copy-start | bytes 3145732
  3.2 7.8 %copy-start.6 = (f32[256,16]{0,1:T(8,128)S(1)}, f32[256,16]{0,1:T(8,128)}, u32[]{:S(2)}) copy-start(f32[256,16]{0,1:T(8,128)} %param.12) | copy-start | bytes 49156
  3.2 7.8 %copy-start.7 = (f32[256,16]{0,1:T(8,128)S(1)}, f32[256,16]{0,1:T(8,128)}, u32[]{:S(2)}) copy-start(f32[256,16]{0,1:T(8,128)} %param.11) | copy-start | bytes 49156
  3.2 7.8 %copy-start.10 = (f32[256]{0:T(256)S(1)}, f32[256]{0:T(256)}, u32[]{:S(2)}) copy-start(f32[256]{0:T(256)} %param.10) | copy-start | bytes 3076
  3.2 28.9 %all-to-all-start = ((bf16[32,64,256]{2,1,0:T(8,128)(2,1)}), bf16[32,64,256]{2,1,0:T(8,128)(2,1)S(1)}, u32[]{:S(2)}, u32[]{:S(2)}) async-start(bf16[32,64,256]{2,1,0:T(8,128)(2,1)} %norm_rows.1), calls=%async_computation | async-start | bytes 2097152 | tf_op jit(solution)/shard_map/all_to_all | solution.py:531
  11.0 0.7 copy-start.8
  11.0 0.7 copy-start.9
  16.4 12.9 %collective-permute-start.3 = (f32[16,256]{1,0:T(8,128)S(1)}, f32[16,256]{1,0:T(8,128)S(1)}, u32[]{:S(2)}, u32[]{:S(2)}) collective-permute-start(f32[16,256]{1,0:T(8,128)S(1)} %get-tuple-element.18), channel_id=1, source_target_pairs={{128,0},{160,32},{192,64},{224,96},{0,128},{32,160},{64,192},{96,2... | collective-permute-start | bytes 49160 | tf_op jit(solution)/shard_map/ppermute | solution.py:504
  23.7 5.6 %collective-permute-start.2 = (f32[16,256]{1,0:T(8,128)S(1)}, f32[16,256]{1,0:T(8,128)S(1)}, u32[]{:S(2)}, u32[]{:S(2)}) collective-permute-start(f32[16,256]{1,0:T(8,128)S(1)} %get-tuple-element.18), channel_id=1, source_target_pairs={{96,0},{128,32},{160,64},{192,96},{224,128},{0,160},{32,192},{64,2... | collective-permute-start | bytes 49160 | tf_op jit(solution)/shard_map/ppermute | solution.py:504
  23.7 6.1 %collective-permute-start.1 = (f32[16,256]{1,0:T(8,128)S(1)}, f32[16,256]{1,0:T(8,128)S(1)}, u32[]{:S(2)}, u32[]{:S(2)}) collective-permute-start(f32[16,256]{1,0:T(8,128)S(1)} %get-tuple-element.18), channel_id=1, source_target_pairs={{64,0},{96,32},{128,64},{160,96},{192,128},{224,160},{0,192},{32,2... | collective-permute-start | bytes 49160 | tf_op jit(solution)/shard_map/ppermute | solution.py:504
  28.4 3.7 %collective-permute-start = (f32[16,256]{1,0:T(8,128)S(1)}, f32[16,256]{1,0:T(8,128)S(1)}, u32[]{:S(2)}, u32[]{:S(2)}) collective-permute-start(f32[16,256]{1,0:T(8,128)S(1)} %get-tuple-element.18), channel_id=1, source_target_pairs={{32,0},{64,32},{96,64},{128,96},{160,128},{192,160},{224,192},{0,2... | collective-permute-start | bytes 49160 | tf_op jit(solution)/shard_map/ppermute | solution.py:504
  32.1 9.8 %copy-start.2 = (bf16[32,64,256]{2,1,0:T(8,128)(2,1)}, bf16[32,64,256]{2,1,0:T(8,128)(2,1)S(1)}, u32[]{:S(2)}) copy-start(bf16[32,64,256]{2,1,0:T(8,128)(2,1)S(1)} %all-to-all-done) | copy-start | bytes 3145732
  41.0 1.0 %copy-start.4 = (bf16[2048,256]{1,0:T(8,128)(2,1)}, bf16[2048,256]{1,0:T(8,128)(2,1)S(1)}, u32[]{:S(2)}) copy-start(bf16[2048,256]{1,0:T(8,128)(2,1)S(1)} %get-tuple-element.23) | copy-start | bytes 3145732
  41.9 33.5 %all-to-all-start.1 = ((bf16[32,64,256]{2,1,0:T(8,128)(2,1)}), bf16[32,64,256]{2,1,0:T(8,128)(2,1)S(1)}, u32[]{:S(2)}, u32[]{:S(2)}) async-start(bf16[32,64,256]{2,1,0:T(8,128)(2,1)} %bitcast.9), calls=%async_computation.1 | async-start | bytes 2097152 | tf_op jit(solution)/shard_map/all_to_all | solution.py:541
  49.3 1.2 %copy-start.3 = (bf16[32,64,256]{2,1,0:T(8,128)(2,1)S(1)}, bf16[32,64,256]{2,1,0:T(8,128)(2,1)}, u32[]{:S(2)}) copy-start(bf16[32,64,256]{2,1,0:T(8,128)(2,1)} %copy-done.2) | copy-start | bytes 3145732
  50.5 24.9 %copy-start.1 = (bf16[64,8192]{1,0:T(8,128)(2,1)S(1)}, bf16[64,8192]{1,0:T(8,128)(2,1)}, u32[]{:S(2)}) copy-start(bf16[64,8192]{1,0:T(8,128)(2,1)} %u_ref.1) | copy-start | bytes 3145732
  59.4 3.8 %collective-permute-start.6 = (bf16[2,16,256]{2,1,0:T(8,128)(2,1)S(1)}, bf16[2,16,256]{2,1,0:T(8,128)(2,1)S(1)}, u32[]{:S(2)}, u32[]{:S(2)}) collective-permute-start(bf16[2,16,256]{2,1,0:T(8,128)(2,1)S(1)} %residue_pass.1), channel_id=1, source_target_pairs={{0,96},{32,0},{64,32},{96,64},{128,224},{160,128},{192,160},{224,1... | collective-permute-start | bytes 49160 | tf_op jit(solution)/shard_map/ppermute | solution.py:513
  61.4 5.5 %collective-permute-start.5 = (bf16[2,16,256]{2,1,0:T(8,128)(2,1)S(1)}, bf16[2,16,256]{2,1,0:T(8,128)(2,1)S(1)}, u32[]{:S(2)}, u32[]{:S(2)}) collective-permute-start(bf16[2,16,256]{2,1,0:T(8,128)(2,1)S(1)} %residue_pass.1), channel_id=1, source_target_pairs={{0,32},{32,64},{64,96},{96,0},{128,160},{160,192},{192,224},{224,1... | collective-permute-start | bytes 49160 | tf_op jit(solution)/shard_map/ppermute | solution.py:513
  61.5 5.4 %collective-permute-start.4 = (bf16[2,16,256]{2,1,0:T(8,128)(2,1)S(1)}, bf16[2,16,256]{2,1,0:T(8,128)(2,1)S(1)}, u32[]{:S(2)}, u32[]{:S(2)}) collective-permute-start(bf16[2,16,256]{2,1,0:T(8,128)(2,1)S(1)} %residue_pass.1), channel_id=1, source_target_pairs={{0,64},{32,96},{64,0},{96,32},{128,192},{160,224},{192,128},{224,1... | collective-permute-start | bytes 49160 | tf_op jit(solution)/shard_map/ppermute | solution.py:513
  66.9 8.6 %copy-start.5 = (f32[8192]{0:T(1024)S(1)}, f32[8192]{0:T(1024)}, u32[]{:S(2)}) copy-start(f32[8192]{0:T(1024)} %param.9) | copy-start | bytes 98308
  66.9 7.9 %collective-permute-start.7 = (f32[2,16,256]{2,1,0:T(8,128)S(1)}, f32[2,16,256]{2,1,0:T(8,128)S(1)}, u32[]{:S(2)}, u32[]{:S(2)}) collective-permute-start(f32[2,16,256]{2,1,0:T(8,128)S(1)} %add_add_fusion), channel_id=1, source_target_pairs={{0,128},{32,160},{64,192},{96,224},{128,0},{160,32},{192,64},{224,... | collective-permute-start | bytes 98312 | tf_op jit(solution)/shard_map/ppermute | solution.py:520

commit v7 on v5

--- a/solution.py
+++ b/solution.py
@@ -12,7 +12,8 @@
 SEGS = 8
 LANES = 128
 UNROLL = 8
-STEPS = 32
+PIECES = 4
+CHUNK = 256
 ROW_BLOCK = 16
 
 
@@ -196,57 +197,34 @@
     return lax.fori_loop(0, cuts_ref.shape[0], piece, (jnp.int32(seg_len), carry))[1]
 
 
-def order_matrix(steps, to_steps):
-    size = SEGS * steps
-    row = lax.broadcasted_iota(jnp.int32, (size, size), 0)
-    col = lax.broadcasted_iota(jnp.int32, (size, size), 1)
-    by_step, by_segment = (row, col) if to_steps else (col, row)
-    return (by_segment == by_step % SEGS * steps + by_step // SEGS).astype(F32).astype(BF16)
-
-
-def block_steps(tokens):
-    return min(STEPS, tokens // SEGS)
-
-
-def to_steps(source_ref, target_ref, order_ref):
+def widen(source_ref, target_ref):
     halves, tokens, _ = target_ref.shape
-    steps, seg_len = block_steps(tokens), tokens // SEGS
-
-    def body(b, _):
-        rows = [
-            source_ref[pl.ds(pl.multiple_of(s * seg_len + b * steps, steps), steps), :] for s in range(SEGS)
-        ]
-        block = jnp.dot(order_ref[...], jnp.concatenate(rows, axis=0), preferred_element_type=F32)
-        size = SEGS * steps
+    chunk = min(CHUNK, tokens)
+
+    def body(j, _):
+        rows = pl.ds(pl.multiple_of(j * chunk, chunk), chunk)
         for h in range(halves):
-            target_ref[h, pl.ds(pl.multiple_of(b * size, size), size), :] = block[
-                :, h * LANES : (h + 1) * LANES
-            ]
+            target_ref[h, rows, :] = source_ref[rows, h * LANES : (h + 1) * LANES].astype(F32)
         return 0
 
-    lax.fori_loop(0, seg_len // steps, body, 0)
-
-
-def from_steps(source_ref, target_ref, order_ref):
+    lax.fori_loop(0, tokens // chunk, body, 0)
+
+
+def narrow_out(source_ref, target_ref, out_hbm, sems):
     halves, tokens, _ = source_ref.shape
-    steps, seg_len = block_steps(tokens), tokens // SEGS
-
-    def body(b, _):
-        size = SEGS * steps
-        rows = pl.ds(pl.multiple_of(b * size, size), size)
-        block = jnp.concatenate([source_ref[h, rows, :].astype(BF16) for h in range(halves)], axis=1)
-        block = jnp.dot(order_ref[...], block, preferred_element_type=F32).astype(BF16)
-        for s in range(SEGS):
-            target_ref[pl.ds(pl.multiple_of(s * seg_len + b * steps, steps), steps), :] = block[
-                s * steps : (s + 1) * steps
-            ]
-        return 0
-
-    lax.fori_loop(0, seg_len // steps, body, 0)
-
-
-def step_rows(i):
-    return pl.ds(pl.multiple_of(i * SEGS, SEGS), SEGS)
+    chunk = tokens // PIECES
+    copies = []
+    for k in range(PIECES):
+        rows = pl.ds(k * chunk, chunk)
+        for h in range(halves):
+            target_ref[rows, h * LANES : (h + 1) * LANES] = source_ref[h, rows, :].astype(BF16)
+        copies.append(pltpu.make_async_copy(target_ref.at[rows], out_hbm.at[rows], sems.at[k]))
+        copies[-1].start()
+    return copies
+
+
+def step_rows(i, seg_len):
+    return pl.ds(i, SEGS, stride=seg_len)
 
 
 def spread(ref, r, cols):
@@ -270,17 +248,17 @@
 
 
 def leave_kernel(
-    lens_ref, rates_ref, residues_ref, skip_ref, grad_ref, seg_ref, dev_ref, coef_ref,
-    wide_ref, order_ref, cuts_ref,
+    lens_ref, streams_ref, rates_ref, residues_ref, skip_ref, grad_ref, seg_ref, dev_ref, coef_ref,
+    wide_ref, cuts_ref,
 ):
     tokens, chans = grad_ref.shape
     modes = rates_ref.shape[0]
     seg_len = tokens // SEGS
     base = lax.axis_index("ctx") * tokens
     starts = doc_starts(lens_ref)
-    store_cuts(cuts_ref, cut_codes(starts, [0] * len(starts), base, seg_len))
-    order_ref[...] = order_matrix(block_steps(tokens), True)
-    to_steps(grad_ref, wide_ref, order_ref)
+    streams = [streams_ref[k] for k in range(len(starts) + 1)]
+    store_cuts(cuts_ref, cut_codes(starts, streams[1:], base, seg_len))
+    widen(grad_ref, wide_ref)
     rates = rates_ref[...]
     decay_all = jnp.exp(-rates)
     mode_scale = jnp.sqrt(1.0 - decay_all * decay_all)
@@ -294,7 +272,7 @@
         decay = [spread(coef_ref, r, cols) for r in range(modes)]
 
         def step(i, state):
-            grad = wide_ref[h, step_rows(i), :]
+            grad = wide_ref[h, step_rows(i, seg_len), :]
             return tuple(grad + decay[r] * state[r] for r in range(modes))
 
         def cut(place, stream, state):
@@ -314,20 +292,19 @@
 
 
 def state_scratch(docs, modes, tokens, chans):
-    halves, size = chans // LANES, SEGS * block_steps(tokens)
+    halves = chans // LANES
     return {
         "cuts": pltpu.SMEM((docs,), jnp.int32),
         "narrow": pltpu.VMEM((tokens, chans), BF16),
         "wide": pltpu.VMEM((halves, tokens, LANES), F32),
-        "order": pltpu.VMEM((size, size), BF16),
         "segs": pltpu.VMEM((halves, SEGS * modes, LANES), F32),
         "weights": pltpu.VMEM((modes, SEGS, LANES), F32),
         "total": pltpu.VMEM((2, modes, SEGS, chans), F32),
-        "sems": pltpu.SemaphoreType.DMA((1,)),
+        "sems": pltpu.SemaphoreType.DMA((PIECES,)),
     }
 
 
-def leave(doc_lengths, rates, residues, skip, grad_out):
+def leave(doc_lengths, doc_streams, rates, residues, skip, grad_out):
     modes, chans = rates.shape
     tokens = grad_out.shape[0]
     kinds = state_scratch(doc_lengths.shape[0], modes, tokens, chans)
@@ -338,19 +315,19 @@
             jax.ShapeDtypeStruct((modes, chans), F32),
             jax.ShapeDtypeStruct((3 * modes + SEGS, chans), F32),
         ],
-        [kinds[k] for k in ("wide", "order", "cuts")],
+        [kinds[k] for k in ("wide", "cuts")],
         "leave",
         cost(2 * tokens * chans * modes, 2 * tokens * chans),
-        [pltpu.SMEM] + [pltpu.VMEM] * 4,
+        [pltpu.SMEM] * 2 + [pltpu.VMEM] * 4,
         [pltpu.VMEM] * 3,
-        (doc_lengths, rates, residues, skip, grad_out),
+        (doc_lengths, doc_streams, rates, residues, skip, grad_out),
     )
 
 
 def back_kernel(window, lens_ref, streams_ref, rates_ref, coef_ref, grad_ref, x_ref, seg_ref, *refs):
-    later = refs[:-12]
+    later = refs[:-11]
     (out_hbm, residue_ref, out_ref, arrive_ref, wide_ref, x_wide_ref, conv_ref, weight_ref, total_ref,
-     order_ref, cuts_ref, sems) = refs[-12:]
+     cuts_ref, sems) = refs[-11:]
     tokens, chans = grad_ref.shape
     modes = rates_ref.shape[0]
     seg_len = tokens // SEGS
@@ -372,9 +349,8 @@
         kept = jnp.where(any_start(starts, base + s * seg_len, seg_len), 0.0, 1.0)
         arriving = segment(seg_ref, s, modes) + (through * kept) * arriving
         put_segment(arrive_ref, s - 1, modes, arriving)
-    order_ref[...] = order_matrix(block_steps(tokens), True)
-    to_steps(grad_ref, wide_ref, order_ref)
-    to_steps(x_ref, x_wide_ref, order_ref)
+    widen(grad_ref, wide_ref)
+    widen(x_ref, x_wide_ref)
     total_ref[...] = jnp.zeros_like(total_ref)
     row = lax.broadcasted_iota(jnp.int32, (SEGS, LANES), 0)
     first = base + row * seg_len
@@ -390,7 +366,7 @@
 
         def step(i, carry):
             state, total = carry
-            rows = step_rows(i)
+            rows = step_rows(i, seg_len)
             grad = wide_ref[h, rows, :]
             x = x_wide_ref[h, rows, :]
             sums = [skip * grad, None, None, None]
@@ -420,21 +396,19 @@
         for s in range(2):
             for r in range(modes):
                 total_ref[s, r, :, cols] += jnp.where(stream_at == s, total[r], 0.0)
-    order_ref[...] = order_matrix(block_steps(tokens), False)
-    from_steps(conv_ref, out_ref, order_ref)
-    copy = pltpu.make_async_copy(out_ref, out_hbm, sems.at[0])
-    copy.start()
+    copies = narrow_out(conv_ref, out_ref, out_hbm, sems)
     scale = coef_ref[modes : 2 * modes] / math.sqrt(window)
     for s in range(2):
         residue_ref[s] = (jnp.sum(total_ref[s], axis=1) * scale).astype(BF16)
-    copy.wait()
+    for copy in copies:
+        copy.wait()
 
 
 def back_pass(doc_lengths, doc_streams, rates, coef, grad_out, x_cols, seg_leaving, later, window):
     modes, chans = rates.shape
     tokens = grad_out.shape[0]
     kinds = state_scratch(doc_lengths.shape[0], modes, tokens, chans)
-    names = ("narrow", "segs", "wide", "wide", "wide", "weights", "total", "order", "cuts", "sems")
+    names = ("narrow", "segs", "wide", "wide", "wide", "weights", "total", "cuts", "sems")
 
     def kernel(*refs):
         back_kernel(window, *refs)
@@ -475,7 +449,7 @@
         middle = len(parts) // 2
         parts = [a + b for a, b in zip(parts[:middle], parts[middle:])]
     other = lax.ppermute(parts[0], axis, [(i, (i + half) % count) for i in range(count)])
-    return parts[0] + other
+    return (parts[0], other)
 
 
 def local(u_rows, gain, skip, residues, rates, grad_out, doc_lengths, doc_streams):
@@ -487,7 +461,9 @@
     x_send, rates = lax.optimization_barrier((x_send, rates))
     x_cols = lax.all_to_all(x_send, "ch", split_axis=0, concat_axis=0, tiled=True)
     x_cols = x_cols.reshape(tokens, chans)
-    seg_leaving, dev_leaving, coef = leave(doc_lengths, rates, residues, skip[None, :], grad_out)
+    seg_leaving, dev_leaving, coef = leave(
+        doc_lengths, doc_streams, rates, residues, skip[None, :], grad_out
+    )
     later = from_later(dev_leaving, "ctx")
     normed_grad, parts = back_pass(
         doc_lengths, doc_streams, rates, coef, grad_out, x_cols, seg_leaving, later, tokens * ctx
@@ -495,8 +471,10 @@
     grad_rows = lax.all_to_all(
         normed_grad.reshape(groups, tokens // groups, chans), "ch", split_axis=0, concat_axis=0, tiled=True
     )
-    residue_grad = sum_over(parts, "ctx").transpose(0, 2, 1)
+    mine, other = sum_over(parts, "ctx")
     input_grad = final_rows(u_rows, gain, grad_rows)
+    other, input_grad = lax.optimization_barrier((other, input_grad))
+    residue_grad = (mine + other).transpose(0, 2, 1)
     return (input_grad, residue_grad)
 
 

time: 74.6 us -> 72 us (0.965)
  Pallas kernels: 23.4 us -> 20.8 us
    all_to_all x1, waiting for transfers between devices: 3.55 us -> 7.12 us  [local(): lax.all_to_all(normed_grad.reshape(groups, tokens // groups, chans), 'ch'...]
    ppermute x1, waiting for transfers between devices: 3.12 us -> 0.01 us  [sum_over(): lax.ppermute(parts[0], axis, [(i, (i + half) % count) for i in range(coun...]
    pallas_call x4, Pallas kernels: 23.4 us -> 20.8 us  [call(): pl.pallas_call(kernel, in_specs=[pl.BlockSpec(memory_space=space) for spa...]
  transfers between devices with their start and end apart: 10 -> 10, of which waited for: 6 -> 5; matrix products, arithmetic and copies ran while one was open for 1% -> 0% of each run, Pallas kernels for 7% -> 9%
where the time goes in v7:
time: 72 us; the launch traced here: 71.6 us
  starting transfers between devices  35.5 us (49%)
  Pallas kernels  20.8 us (29%)
  waiting for transfers between devices  13.3 us (18%)
  between operations  0.79 us (1%)
    pallas_call x4, Pallas kernels, call(): pl.pallas_call(kernel, in_specs=[pl.BlockSpec(memory_space=space) for spa...  20.8 us
    ppermute x4, starting transfers between devices, from_later(): lax.ppermute(value, axis, [((i + k) % count, i) for i in range(count)])  11.8 us
    all_to_all x1, starting transfers between devices, local(): lax.all_to_all(normed_grad.reshape(groups, tokens // groups, chans), 'ch'...  9.51 us
    all_to_all x1, starting transfers between devices, local(): lax.all_to_all(x_send, 'ch', split_axis=0, concat_axis=0, tiled=True)  8.73 us
    all_to_all x1, waiting for transfers between devices, local(): lax.all_to_all(normed_grad.reshape(groups, tokens // groups, chans), 'ch'...  7.12 us
    ppermute x3, waiting for transfers between devices, sum_over(): lax.ppermute(value, axis, [(i, i // half * half + (i + k) % half) for i i...  4.31 us
    ppermute x1, starting transfers between devices, sum_over(): lax.ppermute(parts[0], axis, [(i, (i + half) % count) for i in range(coun...  3.84 us
    ppermute x4, waiting for transfers between devices, from_later(): lax.ppermute(value, axis, [((i + k) % count, i) for i in range(count)])  1.86 us
  transfers between devices with their start and end apart: 10, of which 5 were waited for; matrix products, arithmetic and copies ran while one was open for 0% of the time, Pallas kernels for 9%

profile of v7, /device:TPU:1, one launch (start us, length us, event | category | flops | bytes accessed | tf_op | source)
XLA Modules:
  0.0 71.6 jit_solution(4393746765542760357)
XLA Ops:
  0.6 2.5 %norm_rows.1 = bf16[32,64,256]{2,1,0:T(8,128)(2,1)} custom-call(bf16[64,8192]{1,0:T(8,128)(2,1)} %u_ref.1, f32[1,8192]{1,0:T(1,128)} %bitcast.9), custom_call_target="tpu_custom_call" | custom-call | flops 4194304 | bytes 2097152 | tf_op jit(solution)/shard_map/norm_rows/pallas_call | solution.py:32
  3.2 0.0 copy-start.1
  3.2 0.0 copy-start.3
  3.2 0.0 copy-start.4
  3.2 0.0 copy-start.7
  3.2 8.7 %all-to-all-start = ((bf16[32,64,256]{2,1,0:T(8,128)(2,1)}), bf16[32,64,256]{2,1,0:T(8,128)(2,1)S(1)}, u32[]{:S(2)}, u32[]{:S(2)}) async-start(bf16[32,64,256]{2,1,0:T(8,128)(2,1)} %norm_rows.1), calls=%async_computation | async-start | bytes 2097152 | tf_op jit(solution)/shard_map/all_to_all | solution.py:462
  12.0 0.0 copy-start.5
  12.0 0.0 copy-start.6
  12.0 0.0 copy-done.1
  12.0 0.0 copy-done.3
  12.0 0.0 copy-done.4
  12.0 0.0 copy-done.7
  12.0 0.6 copy-done.5
  12.6 0.0 copy-done.6
  12.6 4.3 %leave.1 = (f32[2,128,128]{2,1,0:T(8,128)S(1)}, f32[16,256]{1,0:T(8,128)S(1)}, f32[56,256]{1,0:T(8,128)S(1)}) custom-call(s32[4]{0:T(128)S(1)} %copy-done.5, s32[4]{0:T(128)S(1)} %copy-done.6, f32[16,256]{1,0:T(8,128)S(1)} %bitcast.11, f32[16,256]{1,0:T(8,128)S(1)} %bitcast.13, f32[1,256]{1,0:T(1,128)S(1)} %bitcast.14, bf16[2048,256]{1,0:T(8,128)(2,1)S(1)} %copy-done.1), custom_call_target="tpu_custom_call" | custom-call | flops 16777216 | bytes 1048576 | tf_op jit(solution)/shard_map/leave/pallas_call | solution.py:32
  16.9 7.1 %collective-permute-start.3 = (f32[16,256]{1,0:T(8,128)S(1)}, f32[16,256]{1,0:T(8,128)S(1)}, u32[]{:S(2)}, u32[]{:S(2)}) collective-permute-start(f32[16,256]{1,0:T(8,128)S(1)} %get-tuple-element.15), channel_id=1, source_target_pairs={{128,0},{160,32},{192,64},{224,96},{0,128},{32,160},{64,192},{96,2... | collective-permute-start | bytes 49160 | tf_op jit(solution)/shard_map/ppermute | solution.py:435
  24.1 0.0 collective-permute-start.2
  24.1 3.9 %collective-permute-start.1 = (f32[16,256]{1,0:T(8,128)S(1)}, f32[16,256]{1,0:T(8,128)S(1)}, u32[]{:S(2)}, u32[]{:S(2)}) collective-permute-start(f32[16,256]{1,0:T(8,128)S(1)} %get-tuple-element.15), channel_id=1, source_target_pairs={{64,0},{96,32},{128,64},{160,96},{192,128},{224,160},{0,192},{32,2... | collective-permute-start | bytes 49160 | tf_op jit(solution)/shard_map/ppermute | solution.py:435
  28.0 0.7 %collective-permute-start = (f32[16,256]{1,0:T(8,128)S(1)}, f32[16,256]{1,0:T(8,128)S(1)}, u32[]{:S(2)}, u32[]{:S(2)}) collective-permute-start(f32[16,256]{1,0:T(8,128)S(1)} %get-tuple-element.15), channel_id=1, source_target_pairs={{32,0},{64,32},{96,64},{128,96},{160,128},{192,160},{224,192},{0,2... | collective-permute-start | bytes 49160 | tf_op jit(solution)/shard_map/ppermute | solution.py:435
  28.7 0.0 collective-permute-done.3.refs_10_
  28.7 0.0 collective-permute-done.2.refs_9_
  28.7 0.1 collective-permute-done.1.refs_8_
  28.9 1.7 %collective-permute-done.refs_7_ = f32[16,256]{1,0:T(8,128)S(1)} collective-permute-done((f32[16,256]{1,0:T(8,128)S(1)}, f32[16,256]{1,0:T(8,128)S(1)}, u32[]{:S(2)}, u32[]{:S(2)}) %collective-permute-start) | collective-permute-done | bytes 16416 | tf_op jit(solution)/shard_map/ppermute | solution.py:435
  30.6 0.0 all-to-all-done
  30.6 12.1 %back_pass.1 = (bf16[2048,256]{1,0:T(8,128)(2,1)}, bf16[2,16,256]{2,1,0:T(8,128)(2,1)S(1)}) custom-call(s32[4]{0:T(128)S(1)} %copy-done.5, s32[4]{0:T(128)S(1)} %copy-done.6, f32[16,256]{1,0:T(8,128)S(1)} %bitcast.12, f32[56,256]{1,0:T(8,128)S(1)} %get-tuple-element.12.refs_3_, bf16[2048,256]{1,0:T(8,128)(2,1)S(1)} %copy-done.1, ...), custom_call_target="tpu_custom_call" | custom-call | flops 50331648 | bytes 3145728 | tf_op jit(solution)/shard_map/back_pass/pallas_call | solution.py:32
  42.6 0.0 copy-start
  42.7 9.5 %all-to-all-start.1 = ((bf16[32,64,256]{2,1,0:T(8,128)(2,1)}), bf16[32,64,256]{2,1,0:T(8,128)(2,1)S(1)}, u32[]{:S(2)}, u32[]{:S(2)}) async-start(bf16[32,64,256]{2,1,0:T(8,128)(2,1)} %bitcast.5), calls=%async_computation.1 | async-start | bytes 2097152 | tf_op jit(solution)/shard_map/all_to_all | solution.py:471
  52.2 0.0 copy-start.2
  52.2 1.2 %collective-permute-start.6 = (bf16[2,16,256]{2,1,0:T(8,128)(2,1)S(1)}, bf16[2,16,256]{2,1,0:T(8,128)(2,1)S(1)}, u32[]{:S(2)}, u32[]{:S(2)}) collective-permute-start(bf16[2,16,256]{2,1,0:T(8,128)(2,1)S(1)} %get-tuple-element.16), channel_id=1, source_target_pairs={{0,96},{32,0},{64,32},{96,64},{128,224},{160,128},{192,160},{224,1... | collective-permute-start | bytes 49160 | tf_op jit(solution)/shard_map/ppermute | solution.py:444
  53.4 0.3 collective-permute-start.5
  53.7 0.1 collective-permute-start.4
  53.8 1.3 %collective-permute-done.6 = bf16[2,16,256]{2,1,0:T(8,128)(2,1)S(1)} collective-permute-done((bf16[2,16,256]{2,1,0:T(8,128)(2,1)S(1)}, bf16[2,16,256]{2,1,0:T(8,128)(2,1)S(1)}, u32[]{:S(2)}, u32[]{:S(2)}) %collective-permute-start.6) | collective-permute-done | bytes 16416 | tf_op jit(solution)/shard_map/ppermute | solution.py:444
  55.2 3.0 %collective-permute-done.5 = bf16[2,16,256]{2,1,0:T(8,128)(2,1)S(1)} collective-permute-done((bf16[2,16,256]{2,1,0:T(8,128)(2,1)S(1)}, bf16[2,16,256]{2,1,0:T(8,128)(2,1)S(1)}, u32[]{:S(2)}, u32[]{:S(2)}) %collective-permute-start.5) | collective-permute-done | bytes 16416 | tf_op jit(solution)/shard_map/ppermute | solution.py:444
  58.1 0.0 collective-permute-done.4
  58.1 3.8 %collective-permute-start.7 = (f32[2,16,256]{2,1,0:T(8,128)S(1)}, f32[2,16,256]{2,1,0:T(8,128)S(1)}, u32[]{:S(2)}, u32[]{:S(2)}) collective-permute-start(f32[2,16,256]{2,1,0:T(8,128)S(1)} %add_add_fusion), channel_id=1, source_target_pairs={{0,128},{32,160},{64,192},{96,224},{128,0},{160,32},{192,64},{224,... | collective-permute-start | bytes 98312 | tf_op jit(solution)/shard_map/ppermute | solution.py:451
  62.0 7.1 %all-to-all-done.1.grad_ref = bf16[32,64,256]{2,1,0:T(8,128)(2,1)S(1)} async-done(((bf16[32,64,256]{2,1,0:T(8,128)(2,1)}), bf16[32,64,256]{2,1,0:T(8,128)(2,1)S(1)}, u32[]{:S(2)}, u32[]{:S(2)}) %all-to-all-start.1) | async-done | bytes 1048608 | tf_op jit(solution)/shard_map/all_to_all | solution.py:471
  69.1 0.0 copy-done
  69.1 0.0 copy-done.2
  69.1 1.9 %final_rows.1 = bf16[64,8192]{1,0:T(8,128)(2,1)} custom-call(bf16[64,8192]{1,0:T(8,128)(2,1)S(1)} %copy-done, f32[1,8192]{1,0:T(1,128)S(1)} %bitcast.10, bf16[32,64,256]{2,1,0:T(8,128)(2,1)S(1)} %all-to-all-done.1.grad_ref), custom_call_target="tpu_custom_call" | custom-call | flops 8388608 | bytes 3145728 | tf_op jit(solution)/shard_map/final_rows/pallas_call | solution.py:32
  71.0 0.0 collective-permute-done.7
  71.0 0.6 add_bitcast_fusion
  (1 shorter events, 0.0 us)
Async XLA Ops:
  3.2 8.8 %copy-start.1 = (bf16[2048,256]{1,0:T(8,128)(2,1)S(1)}, bf16[2048,256]{1,0:T(8,128)(2,1)}, u32[]{:S(2)}) copy-start(bf16[2048,256]{1,0:T(8,128)(2,1)} %refs_4_.1) | copy-start | bytes 3145732
  3.2 8.8 %copy-start.3 = (f32[256,16]{0,1:T(8,128)S(1)}, f32[256,16]{0,1:T(8,128)}, u32[]{:S(2)}) copy-start(f32[256,16]{0,1:T(8,128)} %param.12) | copy-start | bytes 49156
  3.2 8.8 %copy-start.4 = (f32[256,16]{0,1:T(8,128)S(1)}, f32[256,16]{0,1:T(8,128)}, u32[]{:S(2)}) copy-start(f32[256,16]{0,1:T(8,128)} %param.11) | copy-start | bytes 49156
  3.2 8.8 %copy-start.7 = (f32[256]{0:T(256)S(1)}, f32[256]{0:T(256)}, u32[]{:S(2)}) copy-start(f32[256]{0:T(256)} %param.10) | copy-start | bytes 3076
  3.2 27.3 %all-to-all-start = ((bf16[32,64,256]{2,1,0:T(8,128)(2,1)}), bf16[32,64,256]{2,1,0:T(8,128)(2,1)S(1)}, u32[]{:S(2)}, u32[]{:S(2)}) async-start(bf16[32,64,256]{2,1,0:T(8,128)(2,1)} %norm_rows.1), calls=%async_computation | async-start | bytes 2097152 | tf_op jit(solution)/shard_map/all_to_all | solution.py:462
  12.0 0.7 copy-start.5
  12.0 0.7 copy-start.6
  16.9 11.8 %collective-permute-start.3 = (f32[16,256]{1,0:T(8,128)S(1)}, f32[16,256]{1,0:T(8,128)S(1)}, u32[]{:S(2)}, u32[]{:S(2)}) collective-permute-start(f32[16,256]{1,0:T(8,128)S(1)} %get-tuple-element.15), channel_id=1, source_target_pairs={{128,0},{160,32},{192,64},{224,96},{0,128},{32,160},{64,192},{96,2... | collective-permute-start | bytes 49160 | tf_op jit(solution)/shard_map/ppermute | solution.py:435
  24.1 4.7 %collective-permute-start.2 = (f32[16,256]{1,0:T(8,128)S(1)}, f32[16,256]{1,0:T(8,128)S(1)}, u32[]{:S(2)}, u32[]{:S(2)}) collective-permute-start(f32[16,256]{1,0:T(8,128)S(1)} %get-tuple-element.15), channel_id=1, source_target_pairs={{96,0},{128,32},{160,64},{192,96},{224,128},{0,160},{32,192},{64,2... | collective-permute-start | bytes 49160 | tf_op jit(solution)/shard_map/ppermute | solution.py:435
  24.1 4.8 %collective-permute-start.1 = (f32[16,256]{1,0:T(8,128)S(1)}, f32[16,256]{1,0:T(8,128)S(1)}, u32[]{:S(2)}, u32[]{:S(2)}) collective-permute-start(f32[16,256]{1,0:T(8,128)S(1)} %get-tuple-element.15), channel_id=1, source_target_pairs={{64,0},{96,32},{128,64},{160,96},{192,128},{224,160},{0,192},{32,2... | collective-permute-start | bytes 49160 | tf_op jit(solution)/shard_map/ppermute | solution.py:435
  28.0 2.6 %collective-permute-start = (f32[16,256]{1,0:T(8,128)S(1)}, f32[16,256]{1,0:T(8,128)S(1)}, u32[]{:S(2)}, u32[]{:S(2)}) collective-permute-start(f32[16,256]{1,0:T(8,128)S(1)} %get-tuple-element.15), channel_id=1, source_target_pairs={{32,0},{64,32},{96,64},{128,96},{160,128},{192,160},{224,192},{0,2... | collective-permute-start | bytes 49160 | tf_op jit(solution)/shard_map/ppermute | solution.py:435
  42.6 26.4 %copy-start = (bf16[64,8192]{1,0:T(8,128)(2,1)S(1)}, bf16[64,8192]{1,0:T(8,128)(2,1)}, u32[]{:S(2)}) copy-start(bf16[64,8192]{1,0:T(8,128)(2,1)} %u_ref.1) | copy-start | bytes 3145732
  42.7 26.4 %all-to-all-start.1 = ((bf16[32,64,256]{2,1,0:T(8,128)(2,1)}), bf16[32,64,256]{2,1,0:T(8,128)(2,1)S(1)}, u32[]{:S(2)}, u32[]{:S(2)}) async-start(bf16[32,64,256]{2,1,0:T(8,128)(2,1)} %bitcast.5), calls=%async_computation.1 | async-start | bytes 2097152 | tf_op jit(solution)/shard_map/all_to_all | solution.py:471
  52.2 16.9 %copy-start.2 = (f32[8192]{0:T(1024)S(1)}, f32[8192]{0:T(1024)}, u32[]{:S(2)}) copy-start(f32[8192]{0:T(1024)} %param.9) | copy-start | bytes 98308
  52.2 3.0 %collective-permute-start.6 = (bf16[2,16,256]{2,1,0:T(8,128)(2,1)S(1)}, bf16[2,16,256]{2,1,0:T(8,128)(2,1)S(1)}, u32[]{:S(2)}, u32[]{:S(2)}) collective-permute-start(bf16[2,16,256]{2,1,0:T(8,128)(2,1)S(1)} %get-tuple-element.16), channel_id=1, source_target_pairs={{0,96},{32,0},{64,32},{96,64},{128,224},{160,128},{192,160},{224,1... | collective-permute-start | bytes 49160 | tf_op jit(solution)/shard_map/ppermute | solution.py:444
  53.4 4.7 %collective-permute-start.5 = (bf16[2,16,256]{2,1,0:T(8,128)(2,1)S(1)}, bf16[2,16,256]{2,1,0:T(8,128)(2,1)S(1)}, u32[]{:S(2)}, u32[]{:S(2)}) collective-permute-start(bf16[2,16,256]{2,1,0:T(8,128)(2,1)S(1)} %get-tuple-element.16), channel_id=1, source_target_pairs={{0,32},{32,64},{64,96},{96,0},{128,160},{160,192},{192,224},{224,1... | collective-permute-start | bytes 49160 | tf_op jit(solution)/shard_map/ppermute | solution.py:444
  53.7 4.4 %collective-permute-start.4 = (bf16[2,16,256]{2,1,0:T(8,128)(2,1)S(1)}, bf16[2,16,256]{2,1,0:T(8,128)(2,1)S(1)}, u32[]{:S(2)}, u32[]{:S(2)}) collective-permute-start(bf16[2,16,256]{2,1,0:T(8,128)(2,1)S(1)} %get-tuple-element.16), channel_id=1, source_target_pairs={{0,64},{32,96},{64,0},{96,32},{128,192},{160,224},{192,128},{224,1... | collective-permute-start | bytes 49160 | tf_op jit(solution)/shard_map/ppermute | solution.py:444
  58.1 12.8 %collective-permute-start.7 = (f32[2,16,256]{2,1,0:T(8,128)S(1)}, f32[2,16,256]{2,1,0:T(8,128)S(1)}, u32[]{:S(2)}, u32[]{:S(2)}) collective-permute-start(f32[2,16,256]{2,1,0:T(8,128)S(1)} %add_add_fusion), channel_id=1, source_target_pairs={{0,128},{32,160},{64,192},{96,224},{128,0},{160,32},{192,64},{224,... | collective-permute-start | bytes 98312 | tf_op jit(solution)/shard_map/ppermute | solution.py:451

commit v8 on v7

--- a/solution.py
+++ b/solution.py
@@ -11,7 +11,7 @@
 BF16 = jnp.bfloat16
 SEGS = 8
 LANES = 128
-UNROLL = 8
+UNROLL = 16
 PIECES = 4
 CHUNK = 256
 ROW_BLOCK = 16

time: 72 us -> 71.6 us (level)
  Pallas kernels: 20.8 us -> 20 us
    pallas_call x4, Pallas kernels: 20.8 us -> 20 us  [call(): pl.pallas_call(kernel, in_specs=[pl.BlockSpec(memory_space=space) for spa...]
  transfers between devices with their start and end apart: 10 -> 10, of which waited for: 5 -> 5; matrix products, arithmetic and copies ran while one was open for 0% -> 0% of each run, Pallas kernels for 9% -> 8%
where the time goes in v8:
time: 71.6 us; the launch traced here: 70.9 us
  starting transfers between devices  35.5 us (50%)
  Pallas kernels  20 us (28%)
  waiting for transfers between devices  13.3 us (19%)
  between operations  0.79 us (1%)
    pallas_call x4, Pallas kernels, call(): pl.pallas_call(kernel, in_specs=[pl.BlockSpec(memory_space=space) for spa...  20 us
    ppermute x4, starting transfers between devices, from_later(): lax.ppermute(value, axis, [((i + k) % count, i) for i in range(count)])  11.8 us
    all_to_all x1, starting transfers between devices, local(): lax.all_to_all(normed_grad.reshape(groups, tokens // groups, chans), 'ch'...  9.51 us
    all_to_all x1, starting transfers between devices, local(): lax.all_to_all(x_send, 'ch', split_axis=0, concat_axis=0, tiled=True)  8.73 us
    all_to_all x1, waiting for transfers between devices, local(): lax.all_to_all(normed_grad.reshape(groups, tokens // groups, chans), 'ch'...  7.12 us
    ppermute x3, waiting for transfers between devices, sum_over(): lax.ppermute(value, axis, [(i, i // half * half + (i + k) % half) for i i...  4.31 us
    ppermute x1, starting transfers between devices, sum_over(): lax.ppermute(parts[0], axis, [(i, (i + half) % count) for i in range(coun...  3.69 us
    ppermute x4, waiting for transfers between devices, from_later(): lax.ppermute(value, axis, [((i + k) % count, i) for i in range(count)])  1.86 us
  transfers between devices with their start and end apart: 10, of which 5 were waited for; matrix products, arithmetic and copies ran while one was open for 0% of the time, Pallas kernels for 8%

profile of v8, /device:TPU:1, one launch (start us, length us, event | category | flops | bytes accessed | tf_op | source)
XLA Modules:
  0.0 70.9 jit_solution(14625832653163610045)
XLA Ops:
  0.6 2.5 %norm_rows.1 = bf16[32,64,256]{2,1,0:T(8,128)(2,1)} custom-call(bf16[64,8192]{1,0:T(8,128)(2,1)} %u_ref.1, f32[1,8192]{1,0:T(1,128)} %bitcast.9), custom_call_target="tpu_custom_call" | custom-call | flops 4194304 | bytes 2097152 | tf_op jit(solution)/shard_map/norm_rows/pallas_call | solution.py:32
  3.2 0.0 copy-start.1
  3.2 0.0 copy-start.3
  3.2 0.0 copy-start.4
  3.2 0.0 copy-start.7
  3.2 8.7 %all-to-all-start = ((bf16[32,64,256]{2,1,0:T(8,128)(2,1)}), bf16[32,64,256]{2,1,0:T(8,128)(2,1)S(1)}, u32[]{:S(2)}, u32[]{:S(2)}) async-start(bf16[32,64,256]{2,1,0:T(8,128)(2,1)} %norm_rows.1), calls=%async_computation | async-start | bytes 2097152 | tf_op jit(solution)/shard_map/all_to_all | solution.py:462
  12.0 0.0 copy-start.5
  12.0 0.0 copy-start.6
  12.0 0.0 copy-done.1
  12.0 0.0 copy-done.3
  12.0 0.0 copy-done.4
  12.0 0.0 copy-done.7
  12.0 0.6 copy-done.5
  12.6 0.0 copy-done.6
  12.6 4.0 %leave.1 = (f32[2,128,128]{2,1,0:T(8,128)S(1)}, f32[16,256]{1,0:T(8,128)S(1)}, f32[56,256]{1,0:T(8,128)S(1)}) custom-call(s32[4]{0:T(128)S(1)} %copy-done.5, s32[4]{0:T(128)S(1)} %copy-done.6, f32[16,256]{1,0:T(8,128)S(1)} %bitcast.11, f32[16,256]{1,0:T(8,128)S(1)} %bitcast.13, f32[1,256]{1,0:T(1,128)S(1)} %bitcast.14, bf16[2048,256]{1,0:T(8,128)(2,1)S(1)} %copy-done.1), custom_call_target="tpu_custom_call" | custom-call | flops 16777216 | bytes 1048576 | tf_op jit(solution)/shard_map/leave/pallas_call | solution.py:32
  16.7 7.3 %collective-permute-start.3 = (f32[16,256]{1,0:T(8,128)S(1)}, f32[16,256]{1,0:T(8,128)S(1)}, u32[]{:S(2)}, u32[]{:S(2)}) collective-permute-start(f32[16,256]{1,0:T(8,128)S(1)} %get-tuple-element.15), channel_id=1, source_target_pairs={{128,0},{160,32},{192,64},{224,96},{0,128},{32,160},{64,192},{96,2... | collective-permute-start | bytes 49160 | tf_op jit(solution)/shard_map/ppermute | solution.py:435
  23.9 0.0 collective-permute-start.2
  23.9 3.8 %collective-permute-start.1 = (f32[16,256]{1,0:T(8,128)S(1)}, f32[16,256]{1,0:T(8,128)S(1)}, u32[]{:S(2)}, u32[]{:S(2)}) collective-permute-start(f32[16,256]{1,0:T(8,128)S(1)} %get-tuple-element.15), channel_id=1, source_target_pairs={{64,0},{96,32},{128,64},{160,96},{192,128},{224,160},{0,192},{32,2... | collective-permute-start | bytes 49160 | tf_op jit(solution)/shard_map/ppermute | solution.py:435
  27.7 0.7 %collective-permute-start = (f32[16,256]{1,0:T(8,128)S(1)}, f32[16,256]{1,0:T(8,128)S(1)}, u32[]{:S(2)}, u32[]{:S(2)}) collective-permute-start(f32[16,256]{1,0:T(8,128)S(1)} %get-tuple-element.15), channel_id=1, source_target_pairs={{32,0},{64,32},{96,64},{128,96},{160,128},{192,160},{224,192},{0,2... | collective-permute-start | bytes 49160 | tf_op jit(solution)/shard_map/ppermute | solution.py:435
  28.4 0.0 collective-permute-done.3.refs_10_
  28.5 0.0 collective-permute-done.2.refs_9_
  28.5 0.1 collective-permute-done.1.refs_8_
  28.6 1.7 %collective-permute-done.refs_7_ = f32[16,256]{1,0:T(8,128)S(1)} collective-permute-done((f32[16,256]{1,0:T(8,128)S(1)}, f32[16,256]{1,0:T(8,128)S(1)}, u32[]{:S(2)}, u32[]{:S(2)}) %collective-permute-start) | collective-permute-done | bytes 16416 | tf_op jit(solution)/shard_map/ppermute | solution.py:435
  30.3 0.0 all-to-all-done
  30.3 11.6 %back_pass.1 = (bf16[2048,256]{1,0:T(8,128)(2,1)}, bf16[2,16,256]{2,1,0:T(8,128)(2,1)S(1)}) custom-call(s32[4]{0:T(128)S(1)} %copy-done.5, s32[4]{0:T(128)S(1)} %copy-done.6, f32[16,256]{1,0:T(8,128)S(1)} %bitcast.12, f32[56,256]{1,0:T(8,128)S(1)} %get-tuple-element.12.refs_3_, bf16[2048,256]{1,0:T(8,128)(2,1)S(1)} %copy-done.1, ...), custom_call_target="tpu_custom_call" | custom-call | flops 50331648 | bytes 3145728 | tf_op jit(solution)/shard_map/back_pass/pallas_call | solution.py:32
  41.9 0.0 copy-start
  41.9 9.5 %all-to-all-start.1 = ((bf16[32,64,256]{2,1,0:T(8,128)(2,1)}), bf16[32,64,256]{2,1,0:T(8,128)(2,1)S(1)}, u32[]{:S(2)}, u32[]{:S(2)}) async-start(bf16[32,64,256]{2,1,0:T(8,128)(2,1)} %bitcast.5), calls=%async_computation.1 | async-start | bytes 2097152 | tf_op jit(solution)/shard_map/all_to_all | solution.py:471
  51.4 0.0 copy-start.2
  51.5 1.4 %collective-permute-start.6 = (bf16[2,16,256]{2,1,0:T(8,128)(2,1)S(1)}, bf16[2,16,256]{2,1,0:T(8,128)(2,1)S(1)}, u32[]{:S(2)}, u32[]{:S(2)}) collective-permute-start(bf16[2,16,256]{2,1,0:T(8,128)(2,1)S(1)} %get-tuple-element.16), channel_id=1, source_target_pairs={{0,96},{32,0},{64,32},{96,64},{128,224},{160,128},{192,160},{224,1... | collective-permute-start | bytes 49160 | tf_op jit(solution)/shard_map/ppermute | solution.py:444
  52.9 0.1 collective-permute-start.5
  53.0 0.2 collective-permute-start.4
  53.2 1.2 %collective-permute-done.6 = bf16[2,16,256]{2,1,0:T(8,128)(2,1)S(1)} collective-permute-done((bf16[2,16,256]{2,1,0:T(8,128)(2,1)S(1)}, bf16[2,16,256]{2,1,0:T(8,128)(2,1)S(1)}, u32[]{:S(2)}, u32[]{:S(2)}) %collective-permute-start.6) | collective-permute-done | bytes 16416 | tf_op jit(solution)/shard_map/ppermute | solution.py:444
  54.4 3.1 %collective-permute-done.5 = bf16[2,16,256]{2,1,0:T(8,128)(2,1)S(1)} collective-permute-done((bf16[2,16,256]{2,1,0:T(8,128)(2,1)S(1)}, bf16[2,16,256]{2,1,0:T(8,128)(2,1)S(1)}, u32[]{:S(2)}, u32[]{:S(2)}) %collective-permute-start.5) | collective-permute-done | bytes 16416 | tf_op jit(solution)/shard_map/ppermute | solution.py:444
  57.5 0.0 collective-permute-done.4
  57.6 3.7 %collective-permute-start.7 = (f32[2,16,256]{2,1,0:T(8,128)S(1)}, f32[2,16,256]{2,1,0:T(8,128)S(1)}, u32[]{:S(2)}, u32[]{:S(2)}) collective-permute-start(f32[2,16,256]{2,1,0:T(8,128)S(1)} %add_add_fusion), channel_id=1, source_target_pairs={{0,128},{32,160},{64,192},{96,224},{128,0},{160,32},{192,64},{224,... | collective-permute-start | bytes 98312 | tf_op jit(solution)/shard_map/ppermute | solution.py:451
  61.2 7.1 %all-to-all-done.1.grad_ref = bf16[32,64,256]{2,1,0:T(8,128)(2,1)S(1)} async-done(((bf16[32,64,256]{2,1,0:T(8,128)(2,1)}), bf16[32,64,256]{2,1,0:T(8,128)(2,1)S(1)}, u32[]{:S(2)}, u32[]{:S(2)}) %all-to-all-start.1) | async-done | bytes 1048608 | tf_op jit(solution)/shard_map/all_to_all | solution.py:471
  68.4 0.0 copy-done
  68.4 0.0 copy-done.2
  68.4 1.9 %final_rows.1 = bf16[64,8192]{1,0:T(8,128)(2,1)} custom-call(bf16[64,8192]{1,0:T(8,128)(2,1)S(1)} %copy-done, f32[1,8192]{1,0:T(1,128)S(1)} %bitcast.10, bf16[32,64,256]{2,1,0:T(8,128)(2,1)S(1)} %all-to-all-done.1.grad_ref), custom_call_target="tpu_custom_call" | custom-call | flops 8388608 | bytes 3145728 | tf_op jit(solution)/shard_map/final_rows/pallas_call | solution.py:32
  70.2 0.0 collective-permute-done.7
  70.3 0.6 add_bitcast_fusion
  (1 shorter events, 0.0 us)
Async XLA Ops:
  3.2 8.8 %copy-start.1 = (bf16[2048,256]{1,0:T(8,128)(2,1)S(1)}, bf16[2048,256]{1,0:T(8,128)(2,1)}, u32[]{:S(2)}) copy-start(bf16[2048,256]{1,0:T(8,128)(2,1)} %refs_4_.1) | copy-start | bytes 3145732
  3.2 8.8 %copy-start.3 = (f32[256,16]{0,1:T(8,128)S(1)}, f32[256,16]{0,1:T(8,128)}, u32[]{:S(2)}) copy-start(f32[256,16]{0,1:T(8,128)} %param.12) | copy-start | bytes 49156
  3.2 8.8 %copy-start.4 = (f32[256,16]{0,1:T(8,128)S(1)}, f32[256,16]{0,1:T(8,128)}, u32[]{:S(2)}) copy-start(f32[256,16]{0,1:T(8,128)} %param.11) | copy-start | bytes 49156
  3.2 8.8 %copy-start.7 = (f32[256]{0:T(256)S(1)}, f32[256]{0:T(256)}, u32[]{:S(2)}) copy-start(f32[256]{0:T(256)} %param.10) | copy-start | bytes 3076
  3.2 27.1 %all-to-all-start = ((bf16[32,64,256]{2,1,0:T(8,128)(2,1)}), bf16[32,64,256]{2,1,0:T(8,128)(2,1)S(1)}, u32[]{:S(2)}, u32[]{:S(2)}) async-start(bf16[32,64,256]{2,1,0:T(8,128)(2,1)} %norm_rows.1), calls=%async_computation | async-start | bytes 2097152 | tf_op jit(solution)/shard_map/all_to_all | solution.py:462
  12.0 0.7 copy-start.5
  12.0 0.7 copy-start.6
  16.7 11.8 %collective-permute-start.3 = (f32[16,256]{1,0:T(8,128)S(1)}, f32[16,256]{1,0:T(8,128)S(1)}, u32[]{:S(2)}, u32[]{:S(2)}) collective-permute-start(f32[16,256]{1,0:T(8,128)S(1)} %get-tuple-element.15), channel_id=1, source_target_pairs={{128,0},{160,32},{192,64},{224,96},{0,128},{32,160},{64,192},{96,2... | collective-permute-start | bytes 49160 | tf_op jit(solution)/shard_map/ppermute | solution.py:435
  23.9 4.5 %collective-permute-start.2 = (f32[16,256]{1,0:T(8,128)S(1)}, f32[16,256]{1,0:T(8,128)S(1)}, u32[]{:S(2)}, u32[]{:S(2)}) collective-permute-start(f32[16,256]{1,0:T(8,128)S(1)} %get-tuple-element.15), channel_id=1, source_target_pairs={{96,0},{128,32},{160,64},{192,96},{224,128},{0,160},{32,192},{64,2... | collective-permute-start | bytes 49160 | tf_op jit(solution)/shard_map/ppermute | solution.py:435
  23.9 4.6 %collective-permute-start.1 = (f32[16,256]{1,0:T(8,128)S(1)}, f32[16,256]{1,0:T(8,128)S(1)}, u32[]{:S(2)}, u32[]{:S(2)}) collective-permute-start(f32[16,256]{1,0:T(8,128)S(1)} %get-tuple-element.15), channel_id=1, source_target_pairs={{64,0},{96,32},{128,64},{160,96},{192,128},{224,160},{0,192},{32,2... | collective-permute-start | bytes 49160 | tf_op jit(solution)/shard_map/ppermute | solution.py:435
  27.7 2.6 %collective-permute-start = (f32[16,256]{1,0:T(8,128)S(1)}, f32[16,256]{1,0:T(8,128)S(1)}, u32[]{:S(2)}, u32[]{:S(2)}) collective-permute-start(f32[16,256]{1,0:T(8,128)S(1)} %get-tuple-element.15), channel_id=1, source_target_pairs={{32,0},{64,32},{96,64},{128,96},{160,128},{192,160},{224,192},{0,2... | collective-permute-start | bytes 49160 | tf_op jit(solution)/shard_map/ppermute | solution.py:435
  41.9 26.4 %copy-start = (bf16[64,8192]{1,0:T(8,128)(2,1)S(1)}, bf16[64,8192]{1,0:T(8,128)(2,1)}, u32[]{:S(2)}) copy-start(bf16[64,8192]{1,0:T(8,128)(2,1)} %u_ref.1) | copy-start | bytes 3145732
  41.9 26.4 %all-to-all-start.1 = ((bf16[32,64,256]{2,1,0:T(8,128)(2,1)}), bf16[32,64,256]{2,1,0:T(8,128)(2,1)S(1)}, u32[]{:S(2)}, u32[]{:S(2)}) async-start(bf16[32,64,256]{2,1,0:T(8,128)(2,1)} %bitcast.5), calls=%async_computation.1 | async-start | bytes 2097152 | tf_op jit(solution)/shard_map/all_to_all | solution.py:471
  51.4 16.9 %copy-start.2 = (f32[8192]{0:T(1024)S(1)}, f32[8192]{0:T(1024)}, u32[]{:S(2)}) copy-start(f32[8192]{0:T(1024)} %param.9) | copy-start | bytes 98308
  51.5 3.0 %collective-permute-start.6 = (bf16[2,16,256]{2,1,0:T(8,128)(2,1)S(1)}, bf16[2,16,256]{2,1,0:T(8,128)(2,1)S(1)}, u32[]{:S(2)}, u32[]{:S(2)}) collective-permute-start(bf16[2,16,256]{2,1,0:T(8,128)(2,1)S(1)} %get-tuple-element.16), channel_id=1, source_target_pairs={{0,96},{32,0},{64,32},{96,64},{128,224},{160,128},{192,160},{224,1... | collective-permute-start | bytes 49160 | tf_op jit(solution)/shard_map/ppermute | solution.py:444
  52.9 4.7 %collective-permute-start.5 = (bf16[2,16,256]{2,1,0:T(8,128)(2,1)S(1)}, bf16[2,16,256]{2,1,0:T(8,128)(2,1)S(1)}, u32[]{:S(2)}, u32[]{:S(2)}) collective-permute-start(bf16[2,16,256]{2,1,0:T(8,128)(2,1)S(1)} %get-tuple-element.16), channel_id=1, source_target_pairs={{0,32},{32,64},{64,96},{96,0},{128,160},{160,192},{192,224},{224,1... | collective-permute-start | bytes 49160 | tf_op jit(solution)/shard_map/ppermute | solution.py:444
  53.0 4.5 %collective-permute-start.4 = (bf16[2,16,256]{2,1,0:T(8,128)(2,1)S(1)}, bf16[2,16,256]{2,1,0:T(8,128)(2,1)S(1)}, u32[]{:S(2)}, u32[]{:S(2)}) collective-permute-start(bf16[2,16,256]{2,1,0:T(8,128)(2,1)S(1)} %get-tuple-element.16), channel_id=1, source_target_pairs={{0,64},{32,96},{64,0},{96,32},{128,192},{160,224},{192,128},{224,1... | collective-permute-start | bytes 49160 | tf_op jit(solution)/shard_map/ppermute | solution.py:444
  57.6 12.7 %collective-permute-start.7 = (f32[2,16,256]{2,1,0:T(8,128)S(1)}, f32[2,16,256]{2,1,0:T(8,128)S(1)}, u32[]{:S(2)}, u32[]{:S(2)}) collective-permute-start(f32[2,16,256]{2,1,0:T(8,128)S(1)} %add_add_fusion), channel_id=1, source_target_pairs={{0,128},{32,160},{64,192},{96,224},{128,0},{160,32},{192,64},{224,... | collective-permute-start | bytes 98312 | tf_op jit(solution)/shard_map/ppermute | solution.py:451
